TPU v7x, 32 devices: a whole 2x2x4 slice. The times are simulated.
32 devices in a mesh: rows: 8 (over z, x), band: 4 (over y, core).
Axes of the slice: x: 2, y: 2, z: 4, core: 2. Of those that a mesh axis runs over, the one named last changes fastest.
Arguments:
- latents: float32 [32, 1024, 16], P('rows', 'band'), may hold values from -6 to 6
- gauss_noise: float32 [32, 1024, 16], P('rows', 'band'), may hold values from -6 to 6
- image_counts: int32 [32], P('rows'), may hold values from 1 to 4, as said below
- timesteps: int32 [32, 4], P('rows'), may hold values from 1 to 999
- labels: int32 [32, 4], P('rows'), may hold values from 0 to 1000
- wide_weights: float32 [1152, 17280], P(('rows', 'band')), may hold values from -0.1875 to 0.1875
- square_weights: float32 [1152, 2304], P(('rows', 'band')), may hold values from -0.25 to 0.25
- down_weights: float32 [4608, 1152], P(('rows', 'band')), may hold values from -0.09375 to 0.09375
- embed_tables: float32 [1273, 1152], P(None, ('rows', 'band')), may hold values from -2 to 2
- all_biases: float32 [19, 1152], P(None, ('rows', 'band')), may hold values from -1.75 to 1.75
- head_weights: float32 [1153, 32], replicated, may hold values from -0.1875 to 0.1875
- first_wide: float32 [1152, 17280], P(('rows', 'band')), may hold values from -1.335144e-05 to 1.335144e-05
- first_square: float32 [1152, 2304], P(('rows', 'band')), may hold values from -1.335144e-05 to 1.335144e-05
- first_down: float32 [4608, 1152], P(('rows', 'band')), may hold values from -1.335144e-05 to 1.335144e-05
- first_tables: float32 [1273, 1152], P(None, ('rows', 'band')), may hold values from -1.335144e-05 to 1.335144e-05
- first_biases: float32 [19, 1152], P(None, ('rows', 'band')), may hold values from -6.1035156e-05 to 6.1035156e-05
- first_head: float32 [1153, 32], replicated, may hold values from -6.1035156e-05 to 6.1035156e-05
- second_wide: float32 [1152, 17280], P(('rows', 'band')), may hold values from 3.7676023e-13 to 1.5070409e-12
- second_square: float32 [1152, 2304], P(('rows', 'band')), may hold values from 3.7676023e-13 to 1.5070409e-12
- second_down: float32 [4608, 1152], P(('rows', 'band')), may hold values from 3.7676023e-13 to 1.5070409e-12
- second_tables: float32 [1273, 1152], P(None, ('rows', 'band')), may hold values from 3.7676023e-13 to 1.5070409e-12
- second_biases: float32 [19, 1152], P(None, ('rows', 'band')), may hold values from 9.4190055e-12 to 3.7676022e-11
- second_head: float32 [1153, 32], replicated, may hold values from 9.4190055e-12 to 3.7676022e-11
Outputs:
- new_wide: float32 [1152, 17280], P(('rows', 'band'))
- new_square: float32 [1152, 2304], P(('rows', 'band'))
- new_down: float32 [4608, 1152], P(('rows', 'band'))
- new_tables: float32 [1273, 1152], P(None, ('rows', 'band'))
- new_biases: float32 [19, 1152], P(None, ('rows', 'band'))
- new_head: float32 [1153, 32], replicated
- next_first_wide: float32 [1152, 17280], P(('rows', 'band'))
- next_first_square: float32 [1152, 2304], P(('rows', 'band'))
- next_first_down: float32 [4608, 1152], P(('rows', 'band'))
- next_first_tables: float32 [1273, 1152], P(None, ('rows', 'band'))
- next_first_biases: float32 [19, 1152], P(None, ('rows', 'band'))
- next_first_head: float32 [1153, 32], replicated
- next_second_wide: float32 [1152, 17280], P(('rows', 'band'))
- next_second_square: float32 [1152, 2304], P(('rows', 'band'))
- next_second_down: float32 [4608, 1152], P(('rows', 'band'))
- next_second_tables: float32 [1273, 1152], P(None, ('rows', 'band'))
- next_second_biases: float32 [19, 1152], P(None, ('rows', 'band'))
- next_second_head: float32 [1153, 32], replicated
- half_wide: bfloat16 [1152, 17280], P(('rows', 'band'))
- half_square: bfloat16 [1152, 2304], P(('rows', 'band'))
- half_down: bfloat16 [4608, 1152], P(('rows', 'band'))
- half_tables: bfloat16 [1273, 1152], P(None, ('rows', 'band'))
- half_biases: bfloat16 [19, 1152], P(None, ('rows', 'band'))
- half_head: bfloat16 [1153, 32], replicated
- grad_norm: float32 [], replicated
- loss_sum: float32 [], replicated
- image_total: float32 [], replicated
Inputs may be any that keep to these rules, and one draw needn't show every extreme that they name: `image_counts`: each row holds 1 or 4 images; among the 4 rows of one index of rows at least one holds 1.
All inputs are finite; a program needn't handle non-finite values.
Results may differ from a plain program's by a relative error of at most 0.0074.
Values may be sent and summed in bfloat16 or wider, within the bound.
A program may use at most 448 MiB of HBM per device.

v0:
```python
import math

import jax
import jax.numpy as jnp
from jax import lax
from jax.sharding import PartitionSpec as P

D = 1152
FF = 4608
HEADS = 16
CLASSES = 1001
FREQ = 256
PATCH_IN = 16
GRID = 32
SLOTS = 4
TIMESTEPS = 1000
STEP = 10


HIGHEST = lax.Precision.HIGHEST
BETA_LOW = 0.0001
BETA_HIGH = 0.02
NORM_EPS = 1e-06
CLIP_NORM = 0.1
DECAY_FIRST = 0.9
DECAY_SECOND = 0.999
ADAM_EPS = 1e-08
LEARN_RATES = (0.1, 0.1, 0.05, 0.2, 0.3, 0.1)


def for_sending(x):

    def short(part):
        return part.astype(jnp.bfloat16) if part.dtype == jnp.float32 else part

    return jax.tree.map(short, x)


def matmul(operand, weights):
    return jnp.einsum("...i,ij->...j", operand, weights, preferred_element_type=jnp.float32)


def matmul_back(gradient, weights):
    return jnp.einsum("...j,ij->...i", gradient, weights, preferred_element_type=jnp.float32)


def outer_sum(operand, gradient):
    return jnp.einsum(
        "ni,nj->ij",
        operand.reshape(-1, operand.shape[-1]),
        gradient.reshape(-1, gradient.shape[-1]),
        preferred_element_type=jnp.float32,
    )


def column_sum(gradient):
    return jnp.sum(gradient.reshape(-1, gradient.shape[-1]), axis=0, dtype=jnp.float32)


def spread(slot_hot, per_slot):
    return jnp.einsum("rns,rsk->rnk", slot_hot, per_slot, precision=HIGHEST)


def silu_back(values, gradient):
    return jax.vjp(jax.nn.silu, values)[1](gradient)[0]


def plan(time_steps):
    steps_all = jnp.arange(TIMESTEPS, dtype=jnp.int32)
    betas = BETA_LOW + (BETA_HIGH - BETA_LOW) * steps_all.astype(jnp.float32) / (TIMESTEPS - 1)
    cumulate = jnp.cumsum(jnp.log1p(-betas))
    pick_now = (time_steps[..., None] == steps_all).astype(jnp.float32)
    pick_prev = (time_steps[..., None] - 1 == steps_all).astype(jnp.float32)
    return jnp.stack(
        [
            jnp.sum(pick_now * betas, axis=-1),
            jnp.sum(pick_now * cumulate, axis=-1),
            jnp.sum(pick_prev * cumulate, axis=-1),
        ],
        axis=-1,
    )


def time_features(time_steps):
    half_width = FREQ // 2
    frequency = jnp.exp(
        -math.log(10000.0) * jnp.arange(half_width).astype(jnp.float32) / half_width
    )
    angles = time_steps.astype(jnp.float32)[..., None] * frequency
    return jnp.concatenate([jnp.cos(angles), jnp.sin(angles)], axis=-1)


def segments(place_at, counts):
    four_way = counts == SLOTS
    segment = jnp.where(four_way, place_at // (GRID * GRID // SLOTS), 0)
    return (segment, place_at - segment * (GRID * GRID // SLOTS), four_way)


def positions(place_at, counts):
    segment, local_index, four_way = segments(place_at, counts)
    grid_side = jnp.where(four_way, GRID // 2, GRID)
    row_coord = (local_index // grid_side).astype(jnp.float32)
    col_coord = (local_index % grid_side).astype(jnp.float32)
    quarter = D // 4
    omegas = jnp.exp(-math.log(10000.0) * jnp.arange(quarter).astype(jnp.float32) / quarter)
    along_row = row_coord[..., None] * omegas
    along_col = col_coord[..., None] * omegas
    return (
        jnp.concatenate(
            [jnp.sin(along_row), jnp.cos(along_row), jnp.sin(along_col), jnp.cos(along_col)],
            axis=-1,
        ),
        segment,
    )


def layer_norm(values):
    centered = values - jnp.mean(values, axis=-1, keepdims=True)
    return centered * lax.rsqrt(jnp.mean(centered * centered, axis=-1, keepdims=True) + NORM_EPS)


def modulate(values, shift, scaling):
    return layer_norm(values) * (1.0 + scaling) + shift


def patch_loss(output, target_noise, patch_sched):
    beta = patch_sched[..., 0:1]
    log_now = patch_sched[..., 1:2]
    log_prev = patch_sched[..., 2:3]
    error = output[..., :PATCH_IN] - target_noise
    log_beta = jnp.log(beta)
    keep_now = -jnp.expm1(log_now)
    log_post = log_beta + jnp.log(-jnp.expm1(log_prev)) - jnp.log(keep_now)
    coefficient = beta * lax.rsqrt(keep_now * (1.0 - beta))
    fraction = 0.5 * (output[..., PATCH_IN:] + 1.0)
    log_model = fraction * log_beta + (1.0 - fraction) * log_post
    diverge = 0.5 * (
        -1.0
        + log_model
        - log_post
        + jnp.exp(log_post - log_model)
        + (coefficient * error) ** 2 * jnp.exp(-log_model)
    )
    return jnp.mean(error * error, axis=-1) + jnp.mean(diverge, axis=-1) / math.log(2.0)


def unpack(wide_part, square_part, down_part, table_part, bias_part):
    triple, upward, adaptive, final_adaptive = jnp.split(
        wide_part, [3 * D, 3 * D + FF, 9 * D + FF], axis=1
    )
    output_proj, time_out = jnp.split(square_part, 2, axis=1)
    return dict(
        triple=triple,
        upward=upward,
        adaptive=adaptive,
        final_adaptive=final_adaptive,
        output_proj=output_proj,
        time_out=time_out,
        downward=down_part,
        time_in=table_part[:FREQ],
        patch_in=table_part[FREQ : FREQ + PATCH_IN],
        class_rows=table_part[FREQ + PATCH_IN :],
        bias_patch=bias_part[0],
        bias_time_in=bias_part[1],
        bias_time_out=bias_part[2],
        bias_adaptive=bias_part[3:9].reshape(-1),
        bias_query=bias_part[9],
        bias_value=bias_part[10],
        bias_output=bias_part[11],
        bias_upward=bias_part[12:16].reshape(-1),
        bias_downward=bias_part[16],
        bias_final=bias_part[17:19].reshape(-1),
    )


def split_heads(rows_in):
    return rows_in.reshape(rows_in.shape[0], HEADS, D // HEADS)


def head_scores(query_heads, key_heads, query_segment, key_segment):
    scores = jnp.einsum(
        "qhd,khd->hqk", query_heads, key_heads, preferred_element_type=jnp.float32
    ) * (D // HEADS) ** (-0.5)
    same_image = (query_segment[:, None] == key_segment[None, :])[None]
    return jnp.where(same_image, scores, -1e30)


def attend(pieces):
    query_row, key_row, value_row, query_segment, key_segment = pieces
    scores = head_scores(split_heads(query_row), split_heads(key_row), query_segment, key_segment)
    row_max = jnp.max(scores, axis=-1, keepdims=True)
    exponent = jnp.exp(scores - row_max)
    denominator = jnp.sum(exponent, axis=-1, keepdims=True)
    attention_weights = (exponent / denominator).astype(jnp.bfloat16)
    mixture = jnp.einsum(
        "hqk,khd->qhd",
        attention_weights,
        split_heads(value_row),
        preferred_element_type=jnp.float32,
    )
    return (mixture.reshape(query_row.shape[0], D), (row_max + jnp.log(denominator))[..., 0])


def back_common(
    query_heads, key_heads, value_row, grad_heads, log_total, query_segment, key_segment
):
    probabilities = jnp.exp(
        head_scores(query_heads, key_heads, query_segment, key_segment) - log_total[..., None]
    )
    grad_probs = jnp.einsum(
        "qhd,khd->hqk", grad_heads, split_heads(value_row), preferred_element_type=jnp.float32
    )
    return (probabilities, grad_probs)


def key_side(grad_scores, probabilities, query_heads, grad_heads, key_count):
    scaling = (D // HEADS) ** (-0.5)
    grad_key = (
        jnp.einsum("hqk,qhd->khd", grad_scores, query_heads, preferred_element_type=jnp.float32)
        * scaling
    )
    grad_value = jnp.einsum(
        "hqk,qhd->khd",
        probabilities.astype(jnp.bfloat16),
        grad_heads,
        preferred_element_type=jnp.float32,
    )
    return (grad_key.reshape(key_count, D), grad_value.reshape(key_count, D))


def query_back(pieces):
    query_row, key_row, value_row, grad_row, log_total, query_segment, key_segment = pieces
    key_heads = split_heads(key_row)
    probabilities, grad_probs = back_common(
        split_heads(query_row),
        key_heads,
        value_row,
        split_heads(grad_row),
        log_total,
        query_segment,
        key_segment,
    )
    inner = jnp.sum(probabilities * grad_probs, axis=-1, keepdims=True)
    grad_scores = (probabilities * (grad_probs - inner)).astype(jnp.bfloat16)
    grad_query = jnp.einsum(
        "hqk,khd->qhd", grad_scores, key_heads, preferred_element_type=jnp.float32
    ) * (D // HEADS) ** (-0.5)
    return (grad_query.reshape(query_row.shape[0], D), inner[..., 0], grad_scores, probabilities)


def attend_back(pieces):
    query_row, key_row, value_row, grad_row = (pieces[0], pieces[1], pieces[2], pieces[3])
    grad_query, inner, grad_scores, probabilities = query_back(pieces)
    grad_key, grad_value = key_side(
        grad_scores, probabilities, split_heads(query_row), split_heads(grad_row), key_row.shape[0]
    )
    return (grad_query, grad_key, grad_value)


def adamw_step(weight, first_old, second_old, gradient, step_rate):
    first_new = DECAY_FIRST * first_old + (1.0 - DECAY_FIRST) * gradient
    second_new = DECAY_SECOND * second_old + (1.0 - DECAY_SECOND) * gradient * gradient
    first_hat = first_new / (1.0 - DECAY_FIRST**STEP)
    second_hat = second_new / (1.0 - DECAY_SECOND**STEP)
    return (
        weight - step_rate * first_hat / (jnp.sqrt(second_hat) + ADAM_EPS),
        first_new,
        second_new,
    )


def body(
    latents,
    gauss_noise,
    image_counts,
    timesteps,
    labels,
    wide_weights,
    square_weights,
    down_weights,
    embed_tables,
    all_biases,
    head_weights,
    first_wide,
    first_square,
    first_down,
    first_tables,
    first_biases,
    first_head,
    second_wide,
    second_square,
    second_down,
    second_tables,
    second_biases,
    second_head,
):
    rows_here, band_len, _ = latents.shape
    patch_total = GRID * GRID
    gathered = (
        lax.all_gather(wide_weights.astype(jnp.bfloat16), ("rows", "band"), axis=0, tiled=True),
        lax.all_gather(square_weights.astype(jnp.bfloat16), ("rows", "band"), axis=0, tiled=True),
        lax.all_gather(down_weights.astype(jnp.bfloat16), ("rows", "band"), axis=0, tiled=True),
        lax.all_gather(embed_tables.astype(jnp.bfloat16), ("rows", "band"), axis=1, tiled=True),
        lax.all_gather(all_biases.astype(jnp.bfloat16), ("rows", "band"), axis=1, tiled=True),
    )
    images = lax.psum(jnp.sum(image_counts).astype(jnp.float32), "rows")
    pieces_map = unpack(
        gathered[0], gathered[1], gathered[2], gathered[3], gathered[4].astype(jnp.float32)
    )
    head_low = head_weights.astype(jnp.bfloat16)
    head_matrix = head_low[:D]
    sched_slots = plan(timesteps)
    frequency = time_features(timesteps).astype(jnp.bfloat16)
    time_pre = matmul(frequency, pieces_map["time_in"]) + pieces_map["bias_time_in"]
    time_act = jax.nn.silu(time_pre).astype(jnp.bfloat16)
    label_hot = (labels[..., None] == jnp.arange(CLASSES, dtype=jnp.int32)).astype(jnp.bfloat16)
    condition = (
        matmul(time_act, pieces_map["time_out"])
        + pieces_map["bias_time_out"]
        + matmul(label_hot, pieces_map["class_rows"])
    )
    cond_act = jax.nn.silu(condition).astype(jnp.bfloat16)
    modulation = matmul(cond_act, pieces_map["adaptive"]) + pieces_map["bias_adaptive"]
    final_mods = matmul(cond_act, pieces_map["final_adaptive"]) + pieces_map["bias_final"]
    band_start = lax.axis_index("band") * band_len
    counts = image_counts[:, None]
    position, segment = positions(
        (band_start + jnp.arange(band_len, dtype=jnp.int32))[None, :], counts
    )
    key_segment = segments(jnp.arange(patch_total, dtype=jnp.int32)[None, :], counts)[0]
    slot_hot = (segment[..., None] == jnp.arange(SLOTS, dtype=jnp.int32)).astype(jnp.float32)
    patch_mods = spread(slot_hot, modulation)
    patch_final = spread(slot_hot, final_mods)
    patch_sched = spread(slot_hot, sched_slots)
    shift_one, scale_one, gate_one, shift_two, scale_two, gate_two = jnp.split(
        patch_mods, 6, axis=-1
    )
    final_shift, final_scale = jnp.split(patch_final, 2, axis=-1)
    log_now = patch_sched[..., 1:2]
    noisy = (jnp.exp(0.5 * log_now) * latents + jnp.sqrt(-jnp.expm1(log_now)) * gauss_noise).astype(
        jnp.bfloat16
    )
    hidden_zero = matmul(noisy, pieces_map["patch_in"]) + pieces_map["bias_patch"] + position
    normed_one = modulate(hidden_zero, shift_one, scale_one).astype(jnp.bfloat16)
    query_bias = pieces_map["bias_query"]
    triple_bias = jnp.concatenate(
        [query_bias, jnp.zeros_like(query_bias), pieces_map["bias_value"]]
    )
    projected = (matmul(normed_one, pieces_map["triple"]) + triple_bias).astype(jnp.bfloat16)
    queries, key_rows, value_rows = jnp.split(projected, 3, axis=-1)
    key_all, value_all = (
        lax.all_gather(for_sending(key_rows), "band", axis=1, tiled=True).astype(key_rows.dtype),
        lax.all_gather(for_sending(value_rows), "band", axis=1, tiled=True).astype(
            value_rows.dtype
        ),
    )
    attended, log_total = lax.map(attend, (queries, key_all, value_all, segment, key_segment))
    attended_low = attended.astype(jnp.bfloat16)
    branch_one = matmul(attended_low, pieces_map["output_proj"]) + pieces_map["bias_output"]
    hidden_one = hidden_zero + gate_one * branch_one
    normed_two = modulate(hidden_one, shift_two, scale_two).astype(jnp.bfloat16)
    upward = matmul(normed_two, pieces_map["upward"]) + pieces_map["bias_upward"]
    active = jax.nn.gelu(upward, approximate=True).astype(jnp.bfloat16)
    branch_two = matmul(active, pieces_map["downward"]) + pieces_map["bias_downward"]
    hidden_two = hidden_one + gate_two * branch_two
    normed_out = modulate(hidden_two, final_shift, final_scale).astype(jnp.bfloat16)
    output = matmul(normed_out, head_matrix) + head_low[D].astype(jnp.float32)
    patch_share = jnp.where(counts == SLOTS, 1.0 / (patch_total // SLOTS), 1.0 / patch_total)
    losses, loss_back = jax.vjp(
        lambda argument: patch_loss(argument, gauss_noise, patch_sched), output
    )
    loss_local = jnp.sum(patch_share * losses)
    grad_out = loss_back(jnp.broadcast_to(patch_share / images, losses.shape))[0].astype(
        jnp.bfloat16
    )
    head_grad = jnp.concatenate(
        [outer_sum(normed_out, grad_out), column_sum(grad_out)[None]], axis=0
    )
    grad_two, grad_fshift, grad_fscale = jax.vjp(modulate, hidden_two, final_shift, final_scale)[1](
        matmul_back(grad_out, head_matrix)
    )
    grad_gate_two = grad_two * branch_two
    grad_branch_two = (gate_two * grad_two).astype(jnp.bfloat16)
    downward_grad = outer_sum(active, grad_branch_two)
    downward_bias = column_sum(grad_branch_two)
    grad_active = matmul_back(grad_branch_two, pieces_map["downward"])
    grad_upward = jax.vjp(lambda argument: jax.nn.gelu(argument, approximate=True), upward)[1](
        grad_active
    )[0].astype(jnp.bfloat16)
    upward_grad = outer_sum(normed_two, grad_upward)
    upward_bias = column_sum(grad_upward)
    grad_one_part, grad_shift_two, grad_scale_two = jax.vjp(
        modulate, hidden_one, shift_two, scale_two
    )[1](matmul_back(grad_upward, pieces_map["upward"]))
    grad_one = grad_two + grad_one_part
    grad_gate_one = grad_one * branch_one
    grad_branch_one = (gate_one * grad_one).astype(jnp.bfloat16)
    output_grad = outer_sum(attended_low, grad_branch_one)
    output_bias = column_sum(grad_branch_one)
    grad_attended = matmul_back(grad_branch_one, pieces_map["output_proj"]).astype(jnp.bfloat16)
    grad_query, grad_key_all, grad_value_all = lax.map(
        attend_back, (queries, key_all, value_all, grad_attended, log_total, segment, key_segment)
    )
    grad_key, grad_value = (
        lax.psum_scatter(
            grad_key_all.astype(jnp.bfloat16), "band", scatter_dimension=1, tiled=True
        ).astype(jnp.float32),
        lax.psum_scatter(
            grad_value_all.astype(jnp.bfloat16), "band", scatter_dimension=1, tiled=True
        ).astype(jnp.float32),
    )
    grad_projected = jnp.concatenate(
        [
            grad_query.astype(jnp.bfloat16),
            grad_key.astype(jnp.bfloat16),
            grad_value.astype(jnp.bfloat16),
        ],
        axis=-1,
    )
    triple_grad = outer_sum(normed_one, grad_projected)
    triple_bias_grad = column_sum(grad_projected)
    grad_zero_part, grad_shift_one, grad_scale_one = jax.vjp(
        modulate, hidden_zero, shift_one, scale_one
    )[1](matmul_back(grad_projected, pieces_map["triple"]))
    grad_zero = (grad_one + grad_zero_part).astype(jnp.bfloat16)
    patch_grad = outer_sum(noisy, grad_zero)
    patch_bias = column_sum(grad_zero)
    grad_patch_mods = jnp.concatenate(
        [
            grad_shift_one,
            grad_scale_one,
            grad_gate_one,
            grad_shift_two,
            grad_scale_two,
            grad_gate_two,
            grad_fshift,
            grad_fscale,
        ],
        axis=-1,
    )
    grad_slots = jnp.einsum("rns,rnk->rsk", slot_hot, grad_patch_mods, precision=HIGHEST).reshape(
        rows_here * SLOTS, 8 * D
    )
    grad_owned_slots = lax.psum_scatter(
        grad_slots.astype(jnp.bfloat16), "band", scatter_dimension=0, tiled=True
    ).astype(jnp.float32)
    owned_count = grad_owned_slots.shape[0]
    owned_start = lax.axis_index("band") * owned_count

    def owned(per_slot):
        flat = per_slot.reshape((rows_here * SLOTS,) + per_slot.shape[2:])
        return lax.dynamic_slice_in_dim(flat, owned_start, owned_count, 0)

    grad_mods_low = grad_owned_slots[:, : 6 * D].astype(jnp.bfloat16)
    grad_final_low = grad_owned_slots[:, 6 * D :].astype(jnp.bfloat16)
    cond_owned = owned(cond_act)
    adaptive_grad = outer_sum(cond_owned, grad_mods_low)
    final_grad = outer_sum(cond_owned, grad_final_low)
    grad_cond_act = matmul_back(grad_mods_low, pieces_map["adaptive"]) + matmul_back(
        grad_final_low, pieces_map["final_adaptive"]
    )
    grad_condition = silu_back(owned(condition), grad_cond_act).astype(jnp.bfloat16)
    time_out_grad = outer_sum(owned(time_act), grad_condition)
    class_grad = outer_sum(owned(label_hot), grad_condition)
    grad_time_pre = silu_back(
        owned(time_pre), matmul_back(grad_condition, pieces_map["time_out"])
    ).astype(jnp.bfloat16)
    time_in_grad = outer_sum(owned(frequency), grad_time_pre)
    grad_wide = jnp.concatenate([triple_grad, upward_grad, adaptive_grad, final_grad], axis=1)
    grad_square = jnp.concatenate([output_grad, time_out_grad], axis=1)
    grad_tables = jnp.concatenate([time_in_grad, patch_grad, class_grad], axis=0)
    grad_biases = jnp.concatenate(
        [
            patch_bias[None],
            column_sum(grad_time_pre)[None],
            column_sum(grad_condition)[None],
            column_sum(grad_mods_low).reshape(6, D),
            triple_bias_grad[:D][None],
            triple_bias_grad[2 * D :][None],
            output_bias[None],
            upward_bias.reshape(FF // D, D),
            downward_bias[None],
            column_sum(grad_final_low).reshape(2, D),
        ],
        axis=0,
    )
    owned_grads = (
        lax.psum_scatter(grad_wide, ("rows", "band"), scatter_dimension=0, tiled=True),
        lax.psum_scatter(grad_square, ("rows", "band"), scatter_dimension=0, tiled=True),
        lax.psum_scatter(downward_grad, ("rows", "band"), scatter_dimension=0, tiled=True),
        lax.psum_scatter(grad_tables, ("rows", "band"), scatter_dimension=1, tiled=True),
        lax.psum_scatter(grad_biases, ("rows", "band"), scatter_dimension=1, tiled=True),
    )
    local_squares = sum((jnp.sum(grad_part * grad_part) for grad_part in owned_grads))
    head_total, loss_sum = lax.psum((head_grad, loss_local), ("rows", "band"))
    square_total = lax.psum(local_squares, ("rows", "band"))
    grad_norm = jnp.sqrt(square_total + jnp.sum(head_total * head_total))
    clip_factor = jnp.minimum(1.0, CLIP_NORM / (grad_norm + 1e-06))
    params = (wide_weights, square_weights, down_weights, embed_tables, all_biases, head_weights)
    firsts = (first_wide, first_square, first_down, first_tables, first_biases, first_head)
    seconds = (second_wide, second_square, second_down, second_tables, second_biases, second_head)
    gradients = (
        owned_grads[0],
        owned_grads[1],
        owned_grads[2],
        owned_grads[3],
        owned_grads[4],
        head_total,
    )
    results = [
        adamw_step(
            params[which],
            firsts[which],
            seconds[which],
            gradients[which] * clip_factor,
            LEARN_RATES[which],
        )
        for which in range(6)
    ]
    return (
        results[0][0],
        results[1][0],
        results[2][0],
        results[3][0],
        results[4][0],
        results[5][0],
        results[0][1],
        results[1][1],
        results[2][1],
        results[3][1],
        results[4][1],
        results[5][1],
        results[0][2],
        results[1][2],
        results[2][2],
        results[3][2],
        results[4][2],
        results[5][2],
        results[0][0].astype(jnp.bfloat16),
        results[1][0].astype(jnp.bfloat16),
        results[2][0].astype(jnp.bfloat16),
        results[3][0].astype(jnp.bfloat16),
        results[4][0].astype(jnp.bfloat16),
        results[5][0].astype(jnp.bfloat16),
        grad_norm,
        loss_sum,
        images,
    )


def solution(mesh):
    return jax.shard_map(
        body,
        mesh=mesh,
        in_specs=(
            P("rows", "band", None),
            P("rows", "band", None),
            P("rows"),
            P("rows", None),
            P("rows", None),
            P(("rows", "band"), None),
            P(("rows", "band"), None),
            P(("rows", "band"), None),
            P(None, ("rows", "band")),
            P(None, ("rows", "band")),
            P(),
            P(("rows", "band"), None),
            P(("rows", "band"), None),
            P(("rows", "band"), None),
            P(None, ("rows", "band")),
            P(None, ("rows", "band")),
            P(),
            P(("rows", "band"), None),
            P(("rows", "band"), None),
            P(("rows", "band"), None),
            P(None, ("rows", "band")),
            P(None, ("rows", "band")),
            P(),
        ),
        out_specs=(
            P(("rows", "band"), None),
            P(("rows", "band"), None),
            P(("rows", "band"), None),
            P(None, ("rows", "band")),
            P(None, ("rows", "band")),
            P(),
            P(("rows", "band"), None),
            P(("rows", "band"), None),
            P(("rows", "band"), None),
            P(None, ("rows", "band")),
            P(None, ("rows", "band")),
            P(),
            P(("rows", "band"), None),
            P(("rows", "band"), None),
            P(("rows", "band"), None),
            P(None, ("rows", "band")),
            P(None, ("rows", "band")),
            P(),
            P(("rows", "band"), None),
            P(("rows", "band"), None),
            P(("rows", "band"), None),
            P(None, ("rows", "band")),
            P(None, ("rows", "band")),
            P(),
            P(),
            P(),
            P(),
        ),
        check_vma=False,
    )
```

profile of v0, /device:TPU:0, one launch (start us, length us, event | category | flops | bytes accessed | tf_op | source)
XLA Modules:
  0.0 3558.3 jit_solution(14399154187451285390)
XLA Ops:
  15.8 44.1 %all-gather.1 = bf16[32,36,19]{1,2,0:T(8,128)(2,1)S(1)} all-gather(bf16[1,36,19]{1,2,0:T(8,128)(2,1)S(1)} %convert_bitcast_fusion.3), channel_id=1, replica_groups=mesh['rows'=8,'band'=4] {'rows','band'}, dimensions={0}, use_global_device_ids=true | all-gather | bytes 45144 | tf_op jit(solution)/shard_map/all_gather | solution.py:304
  94.9 48.9 %all-gather.19.cloned.1.call-done = bf16[32,36,2304]{2,1,0:T(8,128)(2,1)} async-done(((bf16[1,36,2304]{2,1,0:T(8,128)(2,1)}), bf16[32,36,2304]{2,1,0:T(8,128)(2,1)}) %all-gather.19.cloned.1.call-update) | async-done | bytes 5308432 | tf_op jit(solution)/shard_map/all_gather | solution.py:301
  155.0 237.5 %all-gather.21.cloned.1.call-done = bf16[32,36,17280]{2,1,0:T(8,128)(2,1)} async-done(((bf16[1,36,17280]{2,1,0:T(8,128)(2,1)}), bf16[32,36,17280]{2,1,0:T(8,128)(2,1)}) %all-gather.21.cloned.1.call-update) | async-done | bytes 39813136 | tf_op jit(solution)/shard_map/all_gather | solution.py:300
  392.5 34.1 reshape.650
  473.8 19.9 psum.28
  511.7 20.8 all-gather.13.cloned.1.call-done
  545.3 52.9 %all-gather.11.cloned.1.call-done = bf16[4,1024,1152]{2,1,0:T(8,128)(2,1)} async-done(((bf16[4,256,1152]{2,1,0:T(8,128)(2,1)}), bf16[4,1024,1152]{2,1,0:T(8,128)(2,1)}) %all-gather.11.cloned.1.call-update) | async-done | bytes 9437200 | tf_op jit(solution)/shard_map/all_gather | solution.py:352
  610.9 75.2 %while.26 = (s32[]{:T(128)}, bf16[4,256,1152]{1,2,0:T(8,128)(2,1)}, f32[4,16,256]{2,1,0:T(8,128)}, bf16[4,1024,1152]{1,2,0:T(8,128)(2,1)}, s32[4,256]{1,0:T(4,12...) while((s32[]{:T(128)}, bf16[4,256,1152]{1,2,0:T(8,128)(2,1)}, ...), condition=%wide.region_10.11_spmd, body=%wide.region_7.10_spmd.sunk | while | flops 1258549248 | bytes 69221488 | solution.py:357
  726.3 25.2 fusion.158
  771.2 29.9 convert_reduce_fusion
  801.2 21.2 multiply_reduce_fusion.2
  838.9 285.3 %while.27 = (s32[]{:T(128)}, bf16[4,256,1152]{2,1,0:T(8,128)(2,1)}, bf16[4,1024,1152]{2,1,0:T(8,128)(2,1)}, bf16[4,1024,1152]{2,1,0:T(8,128)(2,1)}, bf16[4,1024,...) while((s32[]{:T(128)}, bf16[4,256,1152]{2,1,0:T(8,128)(2,1)}, ...), condition=%wide.region_23.24_spmd, body=%wide.region_21.23_spmd.sunk | while | flops 3060854784 | bytes 285506784 | solution.py:401
  1140.6 62.3 %reduce-scatter.11.cloned.1.call-done = bf16[4,256,1152]{2,1,0:T(8,128)(2,1)} async-done(((bf16[4,1024,1152]{2,1,0:T(8,128)(2,1)}), bf16[4,256,1152]{2,1,0:T(8,128)(2,1)}) %reduce-scatter.11.cloned.1.call-update) | async-done | bytes 2359312 | tf_op jit(solution)/shard_map/reduce_scatter | solution.py:408
  1202.9 81.0 %reduce-scatter.9.cloned.1.call-done = bf16[4,256,1152]{2,1,0:T(8,128)(2,1)} async-done(((bf16[4,1024,1152]{2,1,0:T(8,128)(2,1)}), bf16[4,256,1152]{2,1,0:T(8,128)(2,1)}) %reduce-scatter.9.cloned.1.call-update) | async-done | bytes 2359312 | tf_op jit(solution)/shard_map/reduce_scatter | solution.py:405
  1369.4 31.0 all-reduce.14.cloned.1.call-done
  1462.3 24.5 convolution_bitcast_fusion
  1523.9 53.3 %pad_maximum_fusion = f32[1152,17280]{1,0:T(8,128)} fusion(f32[1152,2304]{1,0:T(8,128)} %fusion.95, f32[1152,6912]{1,0:T(8,128)} %fusion.75, f32[1152,4608]{1,0:T(8,128)} %convolution_bitcast_fusion.1, f32[1152,3456]{1,0:T(8,128)} %convolution_bitcast_fusion.2), kind=kLoop, calls=%fused_computation.34 | loop fusion | flops 59719680 | bytes 159252480 | tf_op jit(solution)/shard_map/concatenate | solution.py:469
  1577.2 1238.7 %fusion = f32[48,17280]{1,0:T(8,128)S(1)} fusion(f32[1152,17280]{1,0:T(8,128)} %pad_maximum_fusion), kind=kCustom, calls=%all-reduce-scatter | all-reduce-scatter fusion | flops 26542080 | bytes 82944000
  2844.0 50.1 %collective-permute-done.7 = f32[36,17280]{1,0:T(8,128)S(1)} collective-permute-done((f32[36,17280]{1,0:T(8,128)S(1)}, f32[36,17280]{1,0:T(8,128)S(1)}, u32[]{:S(2)}, u32[]{:S(2)}) %collective-permute-start.7) | collective-permute-done | bytes 2488352
  2894.0 134.4 %collective-permute-start.2 = (f32[48,17280]{1,0:T(8,128)S(1)}, f32[48,17280]{1,0:T(8,128)}, u32[]{:S(2)}, u32[]{:S(2)}) collective-permute-start(f32[48,17280]{1,0:T(8,128)S(1)} %fusion), channel_id=1, source_target_pairs={{0,3},{1,4},{2,5},{3,6},{4,7},{5,8},{6,9},{7,10},{8,11},{9,12},{10... | collective-permute-start | bytes 9953288
  3037.2 56.9 %collective-permute-done.3 = f32[48,17280]{1,0:T(8,128)} collective-permute-done((f32[48,17280]{1,0:T(8,128)S(1)}, f32[48,17280]{1,0:T(8,128)}, u32[]{:S(2)}, u32[]{:S(2)}) %collective-permute-start.3) | collective-permute-done | bytes 3317792
  3096.8 71.1 %collective-permute-done.1 = f32[48,17280]{1,0:T(8,128)} collective-permute-done((f32[48,17280]{1,0:T(8,128)S(1)}, f32[48,17280]{1,0:T(8,128)}, u32[]{:S(2)}, u32[]{:S(2)}) %collective-permute-start.1) | collective-permute-done | bytes 3317792
  3167.9 122.5 %concatenate.46 = f32[420,17280]{1,0:T(8,128)} concatenate(f32[36,17280]{1,0:T(8,128)} %copy-done.17, f32[48,17280]{1,0:T(8,128)} %copy-done.14, f32[48,17280]{1,0:T(8,128)} %copy-done.15, f32[48,17280]{1,0:T(8,128)} %collective-permute-done.4, f32[48,17280]{1,0:T(8,128)} %collective-permute-done.3, f32[48,17280]{1,0:T(8,128)} %collective-permute-done.2, ...), dimensions={0} | concatenate | bytes 58060800
  3311.0 222.7 %all-reduce.9 = (f32[]{:T(128)}, f32[]{:T(128)}) all-reduce(f32[]{:T(128)S(6)} %add.491, f32[]{:T(128)} %multiply_reduce_fusion.15), channel_id=1, replica_groups=mesh['rows'=8,'band'=4] {'rows','band'}, use_global_device_ids=true, to_apply=%region_48.49 | all-reduce | flops 2 | bytes 16 | tf_op jit(solution)/shard_map/psum | solution.py:496
  (638 shorter events, 851.0 us)
Async XLA Ops:
  7.2 72.4 %all-gather.17.cloned.1.call-start = ((), (), s32[]{:S(2)}) async-start(), calls=%async_computation.9 | async-start | bytes 3379200 | tf_op jit(solution)/shard_map/all_gather | solution.py:303
  8.9 135.0 %all-gather.19.cloned.1.call-start = ((), (), s32[]{:S(2)}) async-start(), calls=%async_computation.10 | async-start | bytes 6082560 | tf_op jit(solution)/shard_map/all_gather | solution.py:301
  10.6 381.9 %all-gather.21.cloned.1.call-start = ((), (), s32[]{:S(2)}) async-start(), calls=%async_computation.11 | async-start | bytes 45619200 | tf_op jit(solution)/shard_map/all_gather | solution.py:300
  13.7 518.8 %all-gather.13.cloned.1.call-start = ((), (), s32[]{:S(2)}) async-start(), calls=%async_computation.4 | async-start | bytes 11796480 | tf_op jit(solution)/shard_map/all_gather | solution.py:353
  90.6 358.8 %copy-start.64 = (f32[4,256]{1,0:T(4,128)}, f32[4,256]{1,0:T(4,128)S(1)}, u32[]{:S(2)}) copy-start(f32[4,256]{1,0:T(4,128)S(1)} %broadcast_multiply_fusion.4) | copy-start | bytes 12292
  93.6 355.8 %copy-start.72 = (f32[4,256]{1,0:T(4,128)}, f32[4,256]{1,0:T(4,128)S(1)}, u32[]{:S(2)}) copy-start(f32[4,256]{1,0:T(4,128)S(1)} %fusion.126) | copy-start | bytes 12292
  155.0 344.1 %copy-start.46 = (bf16[4,4,1152]{2,1,0:T(4,128)(2,1)}, bf16[4,4,1152]{2,1,0:T(4,128)(2,1)S(1)}, u32[]{:S(2)}) copy-start(bf16[4,4,1152]{2,1,0:T(4,128)(2,1)S(1)} %get-tuple-element.484) | copy-start | bytes 110596
  470.0 128.3 %all-gather.11.cloned.1.call-start = ((), (), s32[]{:S(2)}) async-start(), calls=%async_computation.3 | async-start | bytes 11796480 | tf_op jit(solution)/shard_map/all_gather | solution.py:352
  470.6 255.8 %all-gather.15.cloned.1.call-start = ((), (), s32[]{:S(2)}) async-start(), calls=%async_computation.5 | async-start | bytes 10948608 | tf_op jit(solution)/shard_map/all_gather | solution.py:302
  471.8 731.0 %reduce-scatter.11.cloned.1.call-start = ((), (), s32[]{:S(2)}) async-start(), calls=%async_computation.7 | async-start | bytes 11796480 | tf_op jit(solution)/shard_map/reduce_scatter | solution.py:408
  1124.3 159.6 %reduce-scatter.9.cloned.1.call-start = ((), (), s32[]{:S(2)}) async-start(), calls=%async_computation.6 | async-start | bytes 11796480 | tf_op jit(solution)/shard_map/reduce_scatter | solution.py:405
  1125.1 275.3 %all-reduce.14.cloned.1.call-start = ((), (), s32[]{:S(2)}) async-start(), calls=%async_computation.12 | async-start | bytes 589824
  1368.0 1925.7 %all-reduce.16.cloned.1.call-start = ((), (), s32[]{:S(2)}) async-start(), calls=%async_computation.13 | async-start | bytes 33579008
  1442.7 1863.5 %reduce-scatter.13.cloned.1.call-start = ((), (), s32[]{:S(2)}) async-start(), calls=%async_computation.8 | async-start | bytes 21897216 | tf_op jit(solution)/shard_map/reduce_scatter | solution.py:490
  2815.9 220.6 %copy-start.102 = (f32[4,256]{1,0:T(4,128)S(1)}, f32[4,256]{1,0:T(4,128)}, u32[]{:S(2)}) copy-start(f32[4,256]{1,0:T(4,128)} %get-tuple-element.344) | copy-start | bytes 12292
  2815.9 212.5 %collective-permute-start.6 = (f32[48,17280]{1,0:T(8,128)S(1)}, f32[48,17280]{1,0:T(8,128)S(1)}, u32[]{:S(2)}, u32[]{:S(2)}) collective-permute-start(f32[48,17280]{1,0:T(8,128)S(1)} %fusion), channel_id=1, source_target_pairs={{0,7},{1,8},{2,9},{3,10},{4,11},{5,12},{6,13},{7,14},{8,15},{9,16}... | collective-permute-start | bytes 9953288
  2817.4 213.9 %collective-permute-start.5 = (f32[48,17280]{1,0:T(8,128)S(1)}, f32[48,17280]{1,0:T(8,128)S(1)}, u32[]{:S(2)}, u32[]{:S(2)}) collective-permute-start(f32[48,17280]{1,0:T(8,128)S(1)} %fusion), channel_id=1, source_target_pairs={{0,6},{1,7},{2,8},{3,9},{4,10},{5,11},{6,12},{7,13},{8,14},{9,15},... | collective-permute-start | bytes 9953288
  2825.9 68.1 %collective-permute-start.7 = (f32[36,17280]{1,0:T(8,128)S(1)}, f32[36,17280]{1,0:T(8,128)S(1)}, u32[]{:S(2)}, u32[]{:S(2)}) collective-permute-start(f32[36,17280]{1,0:T(8,128)S(1)} %slice.135), channel_id=1, source_target_pairs={{0,8},{1,9},{2,10},{3,11},{4,12},{5,13},{6,14},{7,15},{8,16},{9,17... | collective-permute-start | bytes 7464968
  2833.8 203.4 %collective-permute-start.4 = (f32[48,17280]{1,0:T(8,128)S(1)}, f32[48,17280]{1,0:T(8,128)}, u32[]{:S(2)}, u32[]{:S(2)}) collective-permute-start(f32[48,17280]{1,0:T(8,128)S(1)} %fusion), channel_id=1, source_target_pairs={{0,5},{1,6},{2,7},{3,8},{4,9},{5,10},{6,11},{7,12},{8,13},{9,14},{... | collective-permute-start | bytes 9953288
  2839.7 254.4 %collective-permute-start.3 = (f32[48,17280]{1,0:T(8,128)S(1)}, f32[48,17280]{1,0:T(8,128)}, u32[]{:S(2)}, u32[]{:S(2)}) collective-permute-start(f32[48,17280]{1,0:T(8,128)S(1)} %fusion), channel_id=1, source_target_pairs={{0,4},{1,5},{2,6},{3,7},{4,8},{5,9},{6,10},{7,11},{8,12},{9,13},{1... | collective-permute-start | bytes 9953288
  2894.0 202.8 %collective-permute-start.2 = (f32[48,17280]{1,0:T(8,128)S(1)}, f32[48,17280]{1,0:T(8,128)}, u32[]{:S(2)}, u32[]{:S(2)}) collective-permute-start(f32[48,17280]{1,0:T(8,128)S(1)} %fusion), channel_id=1, source_target_pairs={{0,3},{1,4},{2,5},{3,6},{4,7},{5,8},{6,9},{7,10},{8,11},{9,12},{10... | collective-permute-start | bytes 9953288
  3028.4 139.5 %collective-permute-start.1 = (f32[48,17280]{1,0:T(8,128)S(1)}, f32[48,17280]{1,0:T(8,128)}, u32[]{:S(2)}, u32[]{:S(2)}) collective-permute-start(f32[48,17280]{1,0:T(8,128)S(1)} %fusion), channel_id=1, source_target_pairs={{0,2},{1,3},{2,4},{3,5},{4,6},{5,7},{6,8},{7,9},{8,10},{9,11},{10,... | collective-permute-start | bytes 9953288
  3033.1 134.8 %collective-permute-start = (f32[48,17280]{1,0:T(8,128)S(1)}, f32[48,17280]{1,0:T(8,128)}, u32[]{:S(2)}, u32[]{:S(2)}) collective-permute-start(f32[48,17280]{1,0:T(8,128)S(1)} %fusion), channel_id=1, source_target_pairs={{0,1},{1,2},{2,3},{3,4},{4,5},{5,6},{6,7},{7,8},{8,9},{9,10},{10,1... | collective-permute-start | bytes 9953288
  3290.4 244.7 %copy-start.13 = (f32[36,17280]{1,0:T(8,128)S(1)}, f32[36,17280]{1,0:T(8,128)}, u32[]{:S(2)}) copy-start(f32[36,17280]{1,0:T(8,128)} %param.32) | copy-start | bytes 7464964
  (145 other events, 2324.8 us)
Sparse Core Ops, SparseCore 0:
  11.5 62.1 all-gather.16
  77.1 66.7 all-gather.18
  147.3 245.1 all-gather.20
  470.1 62.4 all-gather.12
  534.0 64.2 all-gather.10
  601.6 87.3 all-gather.14
  1124.4 78.3 reduce-scatter.10
  1205.4 78.4 reduce-scatter.8
  1368.2 32.1 all-reduce.13
  1442.8 363.1 all-reduce.15
  1812.4 333.2 reduce-scatter.12
where the time goes:
time: 3580 us; the launch traced here: 3560 us
  blocking collectives  1530 us (43%)
  waiting for transfers between devices  717 us (20%)
  matrix products  479 us (13%)
  local copies, waits for them, and re-layouts  367 us (10%)
  other arithmetic  277 us (8%)
  starting transfers between devices  169 us (5%)
    unnamed x1, blocking collectives  1240 us
    all_gather x1, waiting for transfers between devices, body(): lax.all_gather(wide_weights.astype(jnp.bfloat16), ('rows', 'band'), axis=...  238 us
    psum x1, blocking collectives, body(): square_total = lax.psum(local_squares, ('rows', 'band'))  223 us
    unnamed x21, waiting for transfers between devices  213 us
    unnamed x291, local copies, waits for them, and re-layouts  201 us
    unnamed x10, starting transfers between devices  169 us
    dot_general x11, matrix products, outer_sum(): jnp.einsum('ni,nj->ij', operand.reshape(-1, operand.shape[-1]), gradient....  96 us
    dot_general x8, matrix products, matmul_back(): jnp.einsum('...j,ij->...i', gradient, weights, preferred_element_type=jnp...  90.3 us
  transfers between devices with their start and end apart: 19, of which 11 were waited for; matrix products, arithmetic and copies ran while one was open for 49% of the time, Pallas kernels for 0%

commit v1 on v0

v1 whole, which is shorter than its diff:
```python
import functools
import math

import jax
import jax.numpy as jnp
from jax import lax
from jax.experimental import pallas as pl
from jax.experimental.pallas import tpu as pltpu
from jax.sharding import PartitionSpec as P

D = 1152
FF = 4608
HEADS = 16
HEAD_DIM = D // HEADS
CLASSES = 1001
FREQ = 256
PATCH_IN = 16
GRID = 32
PATCHES = GRID * GRID
SLOTS = 4
SEGMENT = PATCHES // SLOTS
TIMESTEPS = 1000
STEP = 10

BETA_LOW = 0.0001
BETA_HIGH = 0.02
NORM_EPS = 1e-06
CLIP_NORM = 0.1
DECAY_FIRST = 0.9
DECAY_SECOND = 0.999
ADAM_EPS = 1e-08
LEARN_RATES = (0.1, 0.1, 0.05, 0.2, 0.3, 0.1)

AXES = ("rows", "band")
WINDOW = 256
SCALE = HEAD_DIM ** (-0.5)
NT = (((1,), (1,)), ((), ()))
TN = (((0,), (0,)), ((), ()))
NN = (((1,), (0,)), ((), ()))
BF16 = jnp.bfloat16
F32 = jnp.float32


def dot(left, right, dims):
    return lax.dot_general(left, right, dims, preferred_element_type=F32)


def head_window(head):
    start = jnp.minimum(head * HEAD_DIM // 128, (D - WINDOW) // 128) * 128
    return pl.multiple_of(start, 128), head * HEAD_DIM - start


def head_mask(rows, offset):
    lane = lax.broadcasted_iota(jnp.int32, (rows, WINDOW), 1)
    return (lane >= offset) & (lane < offset + HEAD_DIM)


def attend_head(head, apart, q_ref, k_ref, v_ref, out_ref, log_ref, q_block):
    q_len, k_len = q_ref.shape[0], k_ref.shape[0]
    start, offset = head_window(head)
    window = pl.ds(start, WINDOW)
    for at in range(0, q_len, q_block):
        rows = pl.ds(at, q_block)
        mask = head_mask(q_block, offset)
        query = jnp.where(mask, q_ref[rows, window], 0).astype(BF16)
        scores = jnp.concatenate(
            [
                dot(k_ref[pl.ds(k_at, SEGMENT), window], query, NT)
                + apart[pl.ds(k_at // SEGMENT, 1), rows]
                for k_at in range(0, k_len, SEGMENT)
            ],
            axis=0,
        )
        top = jnp.max(scores, axis=0, keepdims=True)
        weights = jnp.exp((scores - top) * SCALE)
        total = jnp.sum(weights, axis=0, keepdims=True)
        weights = (weights * (1.0 / total)).astype(BF16)
        mixed = dot(weights, v_ref[:, window], TN).astype(BF16)
        out_ref[rows, window] = jnp.where(mask, mixed, out_ref[rows, window])
        log_ref[pl.ds(head, 1), rows] = top * SCALE + jnp.log(total)


def attend_back_head(
    head, apart, q_ref, k_ref, v_ref, grad_ref, log_ref, dq_ref, dk_ref, dv_ref
):
    q_len, k_len = q_ref.shape[0], k_ref.shape[0]
    start, offset = head_window(head)
    window = pl.ds(start, WINDOW)
    mask = head_mask(q_len, offset)
    query = jnp.where(mask, q_ref[:, window], 0).astype(BF16)
    grad = jnp.where(mask, grad_ref[:, window], 0).astype(BF16)
    key = k_ref[:, window]
    log_total = log_ref[pl.ds(head, 1), :]
    probs = jnp.concatenate(
        [
            jnp.exp(
                dot(k_ref[pl.ds(k_at, SEGMENT), window], query, NT) * SCALE
                + (apart[pl.ds(k_at // SEGMENT, 1), :] - log_total)
            )
            for k_at in range(0, k_len, SEGMENT)
        ],
        axis=0,
    )
    both = probs * dot(v_ref[:, window], grad, NT)
    inner = jnp.sum(both, axis=0, keepdims=True)
    grad_scores = (both - probs * inner).astype(BF16)
    grad_value = dot(probs.astype(BF16), grad, NN)
    grad_key = dot(grad_scores, query, NN) * SCALE
    grad_query = (dot(grad_scores, key, TN) * SCALE).astype(BF16)
    dq_ref[:, window] = jnp.where(mask, grad_query, dq_ref[:, window])
    mask = head_mask(k_len, offset)
    dk_ref[:, window] = jnp.where(mask, grad_key.astype(BF16), dk_ref[:, window])
    dv_ref[:, window] = jnp.where(mask, grad_value.astype(BF16), dv_ref[:, window])


def whole_block(shape):
    return pl.BlockSpec(shape, lambda step: (0,) * len(shape))


def at_step(head, step, do):
    pl.when(head == step)(do)


MESH_ID = pl.DeviceIdType.MESH
BLOCK = 144
LINE = 4
SPLIT = (80, 64, 80)
ROWS_AXIS = 8
DEVICES = 32
OWN = D // DEVICES
PADDED = 48
PART = 384
OWNERS = 24
OWNER_OF = 7


class Place:
    def __init__(self):
        self.r, self.b = lax.axis_index("rows"), lax.axis_index("band")
        self.me = 4 * self.r + self.b
        self.z, self.x = self.r // 2, self.r % 2
        self.y, self.c = self.b // 2, self.b % 2
        self.other_x, self.other_b = 1 - self.x, self.b + 2 - 4 * self.y
        self.across_x = (self.r + 1 - 2 * self.x, self.b)
        self.across_y = (self.r, self.other_b)
        self.sibling = (self.r, self.b + 1 - 2 * self.c)
        self.right = (self.r + 2, self.b)
        self.left = (self.r - 2, self.b)

    def others(self, do):
        def step(i, carry):
            device = (self.me + i) % DEVICES
            do(device, (device // 4, device % 4))
            return carry

        lax.fori_loop(1, DEVICES, step, 0)

    def greet(self):
        barrier = pltpu.get_barrier_semaphore()
        self.others(
            lambda _, device: pl.semaphore_signal(
                barrier, inc=1, device_id=device, device_id_type=MESH_ID
            )
        )
        pl.semaphore_wait(barrier, DEVICES - 1)

    def each_source(self, do):
        do(self.z)
        for step in range(1, LINE):
            pl.when(self.z - step >= 0)(functools.partial(do, self.z - step))
            pl.when(self.z + step < LINE)(functools.partial(do, self.z + step))


def remote(source, target, send, receive, device):
    return pltpu.make_async_remote_copy(
        source, target, send, receive, device_id=device, device_id_type=MESH_ID
    )


class Spread:
    def __init__(self, at, place, own, rows, width, cut, dummy, sems):
        self.at, self.place, self.own = at, place, own
        self.rows, self.width, self.cut, self.dummy = rows, width, cut, dummy
        self.line_send, self.line_recv, self.sem = sems


    def block(self, r, b, start=0, size=None):
        return self.place(r, b, start, self.rows if size is None else size)

    def to_sibling(self, source, target):
        return remote(source, target, self.sem.at[3], self.sem.at[4], self.at.sibling)

    def to_x(self, source, target, slot):
        return remote(source, target, self.sem.at[1], self.sem.at[slot], self.at.across_x)

    def to_y(self, source, target, slot):
        return remote(source, target, self.sem.at[2], self.sem.at[slot], self.at.across_y)

    def line_copy(self, way, z, source=None):
        target = self.block(2 * z + self.at.x, self.at.b)
        return remote(
            target if source is None else source,
            target,
            self.line_send.at[way, z],
            self.line_recv.at[way, z],
            self.at.right if way == 0 else self.at.left,
        )

    def fan(self, z, source=None):
        target = self.block(2 * z + self.at.x, self.at.b)
        source = target if source is None else source
        self.to_x(source, target, 5 + z).start()
        self.to_y(source, target, 9 + z).start()
        self.to_sibling(source, target).start()

    def local(self):
        return pltpu.make_async_copy(self.own, self.block(self.at.r, self.at.b), self.sem.at[0])

    def open(self):
        at = self.at
        self.local().start()
        pl.when(at.z < LINE - 1)(lambda: self.line_copy(0, at.z, self.own).start())
        pl.when(at.z > 0)(lambda: self.line_copy(1, at.z, self.own).start())
        self.fan(at.z, self.own)

    def along_line(self, steps=(1, 2, 3)):
        at = self.at
        for step in steps:
            for way in (0, 1):
                z = at.z - step if way == 0 else at.z + step

                @pl.when(z >= 0 if way == 0 else z < LINE)
                def _(way=way, z=z):
                    copy = self.line_copy(way, z)
                    copy.wait_recv()
                    onward = at.z < LINE - 1 if way == 0 else at.z > 0
                    pl.when(onward)(lambda: copy.start())
                    self.fan(z)

    def around_square(self):
        at, cut = self.at, self.cut

        def do(z):
            ref = self.block(2 * z + at.other_x, at.b)
            self.to_x(ref, ref, 5 + z).wait_recv()
            part = self.block(2 * z + at.other_x, at.b, 0, cut)
            self.to_y(part, part, 17 + z).start()
            self.to_sibling(ref, ref).start()
            ref = self.block(2 * z + at.x, at.other_b)
            self.to_y(ref, ref, 9 + z).wait_recv()
            part = self.block(2 * z + at.x, at.other_b, cut, self.rows - cut)
            self.to_x(part, part, 13 + z).start()
            self.to_sibling(ref, ref).start()

        at.each_source(do)

    def close_square(self):
        at, cut = self.at, self.cut

        def do(z):
            part = self.block(2 * z + at.other_x, at.other_b, 0, cut)
            self.to_y(part, part, 17 + z).wait_recv()
            part = self.block(2 * z + at.other_x, at.other_b, cut, self.rows - cut)
            self.to_x(part, part, 13 + z).wait_recv()
            ref = self.block(2 * z + at.other_x, at.other_b)
            self.to_sibling(ref, ref).start()

        at.each_source(do)

    def counted(self, rows):
        if self.width >= 128:
            return self.dummy(rows, self.width)
        return self.dummy(rows * self.width // D, D)

    def arrive(self):
        self.local().wait()
        rows = self.counted(4 * LINE * self.rows)
        self.to_sibling(rows, rows).wait_recv()

    def finish(self):
        at, cut = self.at, self.cut
        pl.when(at.z < LINE - 1)(lambda: self.line_copy(0, at.z).wait_send())
        pl.when(at.z > 0)(lambda: self.line_copy(1, at.z).wait_send())
        for step in range(1, LINE):
            go = jnp.logical_and(at.z - step >= 0, at.z < LINE - 1)
            pl.when(go)(lambda: self.line_copy(0, at.z - step).wait_send())
            go = jnp.logical_and(at.z + step < LINE, at.z > 0)
            pl.when(go)(lambda: self.line_copy(1, at.z + step).wait_send())
        rows = self.counted(LINE * (2 * self.rows - cut))
        self.to_x(rows, rows, 5).wait_send()
        rows = self.counted(LINE * (self.rows + cut))
        self.to_y(rows, rows, 9).wait_send()
        rows = self.counted(4 * LINE * self.rows)
        self.to_sibling(rows, rows).wait_send()


def spread_sems(count):
    dma = pltpu.SemaphoreType.DMA
    return [dma((count, 2, LINE)), dma((count, 2, LINE)), dma((count, 21))]


def compact(target, pieces, first_row):
    for device in range(DEVICES):
        rows = pieces[device, first_row : first_row + PADDED, :].astype(F32)
        target[OWN * device : OWN * (device + 1), :] = rows[:OWN]


def loosen(target, rows):
    for device in range(DEVICES):
        own = rows[OWN * device : OWN * (device + 1), :]
        target[PADDED * device : PADDED * device + OWN, :] = own
        target[PADDED * device + OWN : PADDED * (device + 1), :] = jnp.zeros(
            (PADDED - OWN, rows.shape[1]), F32
        )


def gather_kernel(
    own,
    time_own,
    mods_own,
    features_own,
    labels_own,
    time_in,
    time_bias,
    classes,
    small_own,
    given_own,
    first,
    mods,
    condition_out,
    small_out,
    time_act_out,
    time_pre_out,
    features,
    labels,
    given,
    piece,
    pieces,
    time_weights,
    mods_weights,
    tall,
    loose,
    mods_part,
    given_send,
    given_recv,
    code_sems,
    mods_send,
    mods_recv,
    part_sems,
    line_send,
    line_recv,
    spread_sem,
):
    at = Place()
    at.greet()

    def rows_at(r, start, size):
        return pl.ds(pl.multiple_of(r * BLOCK + start, 16), size)

    def in_first(r, b, start, size):
        return first.at[b, rows_at(r, start, size)]

    def in_time(r, b, start, size):
        return time_weights.at[pl.ds(pl.multiple_of((4 * r + b) * PADDED + start, 16), size)]

    def in_pieces(r, b, start, size):
        return pieces.at[4 * r + b, pl.ds(start, size)]

    def spread(index, place, source, rows, width, cut):
        sems = line_send.at[index], line_recv.at[index], spread_sem.at[index]
        return Spread(at, place, source, rows, width, cut, bytes_of, sems)

    def bytes_of(rows, width):
        if rows <= D:
            return first.at[0, pl.ds(0, rows), pl.ds(0, width)]
        return first.at[:, pl.ds(0, rows // 4), pl.ds(0, width)]

    of_first = spread(0, in_first, own, BLOCK, D, SPLIT[0])
    of_time = spread(1, in_time, time_own, PADDED, D, 16)
    of_piece = spread(2, in_pieces, piece, BLOCK, 128, SPLIT[0])

    def code_copies(i):
        r = (at.r + i) % ROWS_AXIS
        mine = pl.ds(pl.multiple_of(at.r * 16, 16), 16)
        device = (r, at.b)
        return (
            remote(features_own, features.at[mine], code_sems.at[0, i], code_sems.at[1, i], device),
            remote(labels_own, labels.at[mine], code_sems.at[2, i], code_sems.at[3, i], device),
        )

    for i in range(1, ROWS_AXIS):
        for copy in code_copies(i):
            copy.start()
    mine = pl.ds(pl.multiple_of(at.r * 16, 16), 16)
    features[mine, :] = features_own[...]
    labels[mine, :] = labels_own[...]
    of_time.open()

    patches = given_own.shape[2]

    def given_copy(i):
        b = (at.b + i) % 4
        columns = pl.ds(pl.multiple_of(at.b * patches, 128), patches)
        return remote(
            given_own.at[b], given.at[:, columns], given_send.at[i], given_recv.at[i], (at.r, b)
        )

    for i in range(1, 4):
        given_copy(i).start()
    mine = pl.ds(pl.multiple_of(at.b * patches, 128), patches)
    given[:, mine] = given_own[at.b]

    padded_rows = pl.ds(pl.multiple_of(at.me * PADDED, 16), PADDED)

    def mods_copy(owner):
        columns = pl.ds(pl.multiple_of(owner * PART, 128), PART)
        return remote(
            mods_own.at[:, columns],
            mods_weights.at[padded_rows],
            mods_send.at[0],
            mods_recv.at[0],
            (owner % ROWS_AXIS, owner // ROWS_AXIS),
        )

    def to_owner(i, carry):
        owner = (OWNER_OF * at.me + i) % OWNERS
        own_it = jnp.logical_and(owner % ROWS_AXIS == at.r, owner // ROWS_AXIS == at.b)

        @pl.when(own_it)
        def _():
            columns = pl.ds(pl.multiple_of(owner * PART, 128), PART)
            pltpu.make_async_copy(
                mods_own.at[:, columns], mods_weights.at[padded_rows], mods_recv.at[0]
            ).start()

        pl.when(jnp.logical_not(own_it))(lambda: mods_copy(owner).start())
        return carry

    lax.fori_loop(0, OWNERS, to_owner, 0)
    owner = at.b * ROWS_AXIS + at.r
    owns = at.b < OWNERS // ROWS_AXIS

    for i in range(1, ROWS_AXIS):
        for copy in code_copies(i):
            copy.wait_recv()

    time_pre = dot(time_in[...], features[...], NT) + time_bias[...]
    time_pre_out[...] = time_pre
    piece[0:PADDED, :] = jax.nn.silu(time_pre).astype(BF16)
    lane = lax.broadcasted_iota(jnp.int32, (128, 128), 1)
    class_rows = jnp.zeros((PADDED, 128), F32)
    for k in range(classes.shape[1] // 128):
        hot = ((labels[...] & 1023) == lane + 128 * k).astype(F32).astype(BF16)
        class_rows = class_rows + dot(classes[:, 128 * k : 128 * (k + 1)], hot, NT)
    piece[PADDED : 2 * PADDED, :] = class_rows.astype(BF16)
    piece[2 * PADDED : 3 * PADDED, :] = small_own[...]
    of_piece.open()
    of_first.open()
    of_time.along_line()
    of_piece.along_line()
    of_time.around_square()
    of_piece.around_square()
    of_time.close_square()
    of_piece.close_square()
    of_first.along_line()
    of_time.arrive()
    of_piece.arrive()

    for device in range(DEVICES):
        rows = pl.ds(PADDED * device, PADDED)
        loose[rows, :] = pieces[device, 0:PADDED, :].astype(F32)
    time_act = jnp.transpose(loose[...]).astype(BF16)
    compact(tall, pieces, 0)
    time_act_out[...] = jnp.transpose(tall[...]).astype(BF16)
    compact(tall, pieces, 2 * PADDED)
    small = jnp.transpose(tall[...])
    small_out[...] = small
    compact(tall, pieces, PADDED)
    condition = dot(time_act, time_weights[...], NN) + small[2:3, :] + jnp.transpose(tall[...])
    condition_out[...] = condition

    def part_copy(device, place):
        chip = pl.ds(pl.multiple_of(device // 2 * 8, 8), 8)
        columns = pl.ds(pl.multiple_of(owner * PART, 128), PART)
        return remote(
            mods_part.at[chip], mods.at[:, columns], part_sems.at[0], part_sems.at[1], place
        )

    @pl.when(owns)
    def _():
        tall[...] = jnp.transpose(jax.nn.silu(condition))
        loosen(loose, tall)
        pltpu.make_async_copy(mods_weights, mods_weights, mods_recv.at[0]).wait()
        mods_part[...] = dot(loose[...].astype(BF16), mods_weights[...], TN)
        at.others(lambda device, place: part_copy(device, place).start())
        chip = pl.ds(pl.multiple_of(at.me // 2 * 8, 8), 8)
        columns = pl.ds(pl.multiple_of(owner * PART, 128), PART)
        pltpu.make_async_copy(mods_part.at[chip], mods.at[:, columns], part_sems.at[1]).start()

    of_first.around_square()
    of_first.close_square()
    of_first.arrive()
    pltpu.make_async_copy(mods, mods, part_sems.at[1]).wait()
    for i in range(1, ROWS_AXIS):
        for copy in code_copies(i):
            copy.wait_send()
    for i in range(1, 4):
        given_copy(i).wait()

    @pl.when(owns)
    def _():
        sent = time_weights.at[pl.ds(0, (OWNERS - 1) * PADDED // 3)]
        remote(sent, sent, mods_send.at[0], mods_recv.at[0], at.sibling).wait_send()

    @pl.when(jnp.logical_not(owns))
    def _():
        sent = time_weights.at[pl.ds(0, OWNERS * PADDED // 3)]
        remote(sent, sent, mods_send.at[0], mods_recv.at[0], at.sibling).wait_send()

    @pl.when(owns)
    def _():
        sent = first.at[0, pl.ds(0, (DEVICES - 1) * 16), pl.ds(0, PART)]
        remote(sent, sent, part_sems.at[0], part_sems.at[1], at.sibling).wait_send()

    for group in (of_piece, of_time, of_first):
        group.finish()


def gather_weights(*operands):
    dma = pltpu.SemaphoreType.DMA
    anywhere, inside = (
        pl.BlockSpec(memory_space=pl.ANY),
        pl.BlockSpec(memory_space=pltpu.VMEM),
    )
    return pl.pallas_call(
        gather_kernel,
        in_specs=[anywhere] * 3 + [inside] * 7,
        out_specs=[anywhere] + [inside] * 8,
        out_shape=[
            jax.ShapeDtypeStruct((4, D, D), BF16),
            jax.ShapeDtypeStruct((8, 8 * D), F32),
            jax.ShapeDtypeStruct((128, D), F32),
            jax.ShapeDtypeStruct((128, D), F32),
            jax.ShapeDtypeStruct((128, D), BF16),
            jax.ShapeDtypeStruct((PADDED, 128), F32),
            jax.ShapeDtypeStruct((128, FREQ), BF16),
            jax.ShapeDtypeStruct((128, 128), jnp.int32),
            jax.ShapeDtypeStruct((2 * PATCH_IN, PATCHES), F32),
        ],
        scratch_shapes=[
            pltpu.VMEM((BLOCK, 128), BF16),
            pltpu.VMEM((DEVICES, BLOCK, 128), BF16),
            pltpu.VMEM((DEVICES * PADDED, D), BF16),
            pltpu.VMEM((DEVICES * PADDED, PART), BF16),
            pltpu.VMEM((D, 128), F32),
            pltpu.VMEM((DEVICES * PADDED, 128), F32),
            pltpu.VMEM((128, PART), F32),
            dma((4,)),
            dma((4,)),
            dma((4, ROWS_AXIS)),
            dma((1,)),
            dma((1,)),
            dma((2,)),
            *spread_sems(3),
        ],
        compiler_params=pltpu.CompilerParams(
            collective_id=0, has_side_effects=True, vmem_limit_bytes=32 << 20
        ),
        name="gather_weights",
    )(*operands)


class Collect:
    def __init__(self, at, part, out, buffers, sems, cut):
        self.at, self.part, self.out, self.cut = at, part, out, cut
        self.own, self.got, self.near, self.far, self.line = buffers
        (
            self.own_sem,
            self.core_send,
            self.core_recv,
            self.near_send,
            self.near_recv,
            self.far_send,
            self.far_recv,
            self.line_send,
            self.line_recv,
        ) = sems
        self.other_y = 1 - at.y

    def start(self):
        at = self.at
        for y in (0, 1):
            for core in (0, 1):

                def begin(keep, y=y, b=2 * y + core):
                    for source, first, rows in self.part(b):
                        self.move(y, pl.ds(first, rows), source, keep).start()

                pl.when(at.c == core)(functools.partial(begin, True))
                pl.when(at.c != core)(functools.partial(begin, False))

    def move(self, y, rows, source, keep):
        if keep:
            return pltpu.make_async_copy(source, self.own.at[y, rows], self.own_sem.at[y])
        return remote(
            source,
            self.got.at[y, rows],
            self.core_send.at[y],
            self.core_recv.at[y],
            self.at.sibling,
        )

    def arrive(self):
        for y in (0, 1):
            self.move(y, pl.ds(0, D), self.got.at[y], True).wait()
            self.move(y, pl.ds(0, D), self.got.at[y], False).wait_recv()

    @staticmethod
    def rows_of(r, start, size):
        return pl.ds(pl.multiple_of(r * BLOCK + start, 16), size)

    @staticmethod
    def add(target, sources, size):
        def step(i, carry):
            total = None
            for ref, index, start in sources:
                tile = ref[index + (pl.ds(pl.multiple_of(start + 16 * i, 16), 16),)].astype(F32)
                total = tile if total is None else total + tile
            ref, index, start = target
            ref[index + (pl.ds(pl.multiple_of(start + 16 * i, 16), 16),)] = total.astype(ref.dtype)
            return carry

        lax.fori_loop(0, size // 16, step, 0)

    def near_copy(self, route, i):
        at, cut = self.at, self.cut
        if route == 0:
            source = self.own.at[self.other_y, self.rows_of(i, 0, cut)]
            target = self.near.at[i, pl.ds(0, cut)]
            device = at.across_y
        else:
            rows = self.rows_of(2 * (i // 2) + at.other_x, cut, BLOCK - cut)
            source = self.own.at[i % 2, rows]
            target = self.near.at[i, pl.ds(cut, BLOCK - cut)]
            device = at.across_x
        return remote(
            source, target, self.near_send.at[route], self.near_recv.at[route, i], device
        )

    def far_copy(self, route, z):
        at, cut = self.at, self.cut
        if route == 0:
            source = self.own.at[at.y, self.rows_of(2 * z + at.other_x, 0, cut)]
            target = self.far.at[z, pl.ds(0, cut)]
            device = at.across_x
        else:
            source = self.own.at[self.other_y, self.rows_of(2 * z + at.x, cut, BLOCK - cut)]
            target = self.far.at[z, pl.ds(cut, BLOCK - cut)]
            device = at.across_y
        return remote(source, target, self.far_send.at[route], self.far_recv.at[route, z], device)

    def near_stage(self, begin, end):
        at, cut, own, got = self.at, self.cut, self.own, self.got

        def step(i, carry):
            for y, start, size, route in (
                (self.other_y, i * BLOCK, cut, 0),
                (i % 2, (2 * (i // 2) + at.other_x) * BLOCK + cut, BLOCK - cut, 1),
            ):
                self.add((own, (y,), start), [(own, (y,), start), (got, (y,), start)], size)
                self.near_copy(route, i).start()
            return carry

        lax.fori_loop(begin, end, step, 0)

    def far_stage(self, begin, end):
        at, cut, own, got = self.at, self.cut, self.own, self.got

        def step(z, carry):
            r, i = 2 * z + at.other_x, 2 * z + self.other_y
            for y, start, size, route, index, first in (
                (at.y, r * BLOCK, cut, 0, r, 0),
                (self.other_y, (2 * z + at.x) * BLOCK + cut, BLOCK - cut, 1, i, cut),
            ):
                self.near_copy(route, index).wait_recv()
                sources = [(own, (y,), start), (got, (y,), start), (self.near, (index,), first)]
                self.add((own, (y,), start), sources, size)
                self.far_copy(route, z).start()
            return carry

        lax.fori_loop(begin, end, step, 0)

    def line_copy(self, way, z):
        source = self.own.at[self.at.y, self.rows_of(2 * z + self.at.x, 0, BLOCK)]
        slot = z - 1 if way == 0 else z
        return remote(
            source,
            self.line.at[way, slot],
            self.line_send.at[way, slot],
            self.line_recv.at[way, slot],
            self.at.right if way == 0 else self.at.left,
        )

    def arrivals(self, z):
        self.near_copy(0, 2 * z + self.at.x).wait_recv()
        self.near_copy(1, 2 * z + self.at.y).wait_recv()
        self.far_copy(0, z).wait_recv()
        self.far_copy(1, z).wait_recv()

    def total(self, z, target, ways):
        at, cut = self.at, self.cut
        start = (2 * z + at.x) * BLOCK
        for route, begin, size in ((0, 0, cut), (1, cut, BLOCK - cut)):
            index = 2 * z + (at.x if route == 0 else at.y)
            sources = [
                (self.own, (at.y,), start + begin),
                (self.got, (at.y,), start + begin),
                (self.near, (index,), begin),
                (self.far, (z,), begin),
            ]
            for way in ways:
                sources.append((self.line, (way, z - 1 if way == 0 else z), begin))
            ref, place, base = target
            self.add((ref, place, base + begin), sources, size)

    def pass_on(self, way, z):
        at = self.at
        ahead = at.z > 0 if way == 0 else at.z < LINE - 1
        target = (self.own, (at.y,), (2 * z + at.x) * BLOCK)
        self.arrivals(z)

        @pl.when(ahead)
        def _():
            self.line_copy(way, z).wait_recv()
            self.total(z, target, (way,))

        pl.when(jnp.logical_not(ahead))(lambda: self.total(z, target, ()))
        self.line_copy(way, z).start()

    def line_stage(self, step):
        z = LINE - 1 - step
        pl.when(self.at.z < z)(functools.partial(self.pass_on, 0, z))
        pl.when(self.at.z > step)(functools.partial(self.pass_on, 1, step))

    def last(self):
        at = self.at
        self.arrivals(at.z)
        for z in range(LINE):
            ways = ((0,) if z > 0 else ()) + ((1,) if z < LINE - 1 else ())

            @pl.when(at.z == z)
            def _(z=z, ways=ways):
                for way in ways:
                    self.line_copy(way, z).wait_recv()
                self.total(z, (self.out, (), 0), ways)

    def finish(self):
        at, cut = self.at, self.cut
        for y in (0, 1):
            self.move(y, pl.ds(0, D), self.got.at[y], False).wait_send()
        for route, size in ((0, cut), (1, BLOCK - cut)):
            rows = self.own.at[0, pl.ds(0, 2 * LINE * size)]
            sems = self.near_send.at[route], self.near_recv.at[route, 0]
            remote(rows, rows, *sems, at.sibling).wait_send()
            rows = self.own.at[0, pl.ds(0, LINE * size)]
            sems = self.far_send.at[route], self.far_recv.at[route, 0]
            remote(rows, rows, *sems, at.sibling).wait_send()
        for step in range(LINE - 1):
            z = LINE - 1 - step
            pl.when(at.z < z)(lambda: self.line_copy(0, z).wait_send())
            pl.when(at.z > step)(lambda: self.line_copy(1, step).wait_send())


def collect_scratch():
    dma = pltpu.SemaphoreType.DMA
    return [
        pltpu.VMEM((2, D, D), BF16),
        pltpu.VMEM((2, D, D), BF16),
        pltpu.VMEM((2 * LINE, BLOCK, D), BF16),
        pltpu.VMEM((LINE, BLOCK, D), BF16),
        pltpu.VMEM((2, LINE - 1, BLOCK, D), BF16),
        dma((2,)),
        dma((2,)),
        dma((2,)),
        dma((2,)),
        dma((2, 2 * LINE)),
        dma((2,)),
        dma((2, LINE)),
        dma((2, LINE - 1)),
        dma((2, LINE - 1)),
    ]


def scatter_kernel(
    query,
    key,
    value,
    output,
    slots_own,
    mods_weights,
    condition,
    totals_own,
    out,
    slots,
    grad_condition,
    totals,
    quarters,
    slots_block,
    piece,
    pieces,
    tall,
    totals_got,
    band_send,
    band_recv,
    totals_send,
    totals_recv,
    slot_line_send,
    slot_line_recv,
    slot_sem,
    *rest,
):
    at = Place()
    at.greet()
    own = rest[0]
    of_first = Collect(
        at, lambda b: [((query, key, value, output)[b], 0, D)], out, rest[:5], rest[5:], SPLIT[0]
    )
    of_first.start()

    def band_copy(i):
        b = (at.b + i) % 4
        columns = pl.ds(pl.multiple_of(b * 2 * D, 128), 2 * D)
        return remote(
            slots_own.at[:, columns],
            quarters.at[at.b],
            band_send.at[i],
            band_recv.at[i],
            (at.r, b),
        )

    def band_arrival(i):
        source = quarters.at[(at.b + 4 - i) % 4]
        return remote(source, source, band_send.at[i], band_recv.at[i], at.sibling)

    def in_slots(r, b, start, size):
        columns = pl.ds(pl.multiple_of(b * 2 * D + start, 128), size)
        return slots.at[pl.ds(pl.multiple_of(r * 16, 16), 16), columns]

    def in_pieces(r, b, start, size):
        return pieces.at[4 * r + b, pl.ds(start, size)]

    def sems(index):
        return slot_line_send.at[index], slot_line_recv.at[index], slot_sem.at[index]

    def bytes_of(rows, width):
        return own.at[0, pl.ds(0, rows), pl.ds(0, width)]

    of_slots = Spread(at, in_slots, slots_block, 2 * D, 16, D, bytes_of, sems(0))
    of_piece = Spread(at, in_pieces, piece, PADDED, 128, 16, bytes_of, sems(1))

    def share_slots():
        mine = pl.ds(pl.multiple_of(at.b * 2 * D, 128), 2 * D)
        total = slots_own[:, mine].astype(F32)
        for i in range(1, 4):
            band_arrival(i).wait_recv()
        for i in range(1, 4):
            total = total + quarters[(at.b + 4 - i) % 4].astype(F32)
        slots_block[...] = total.astype(BF16)
        of_slots.open()

    def condition_back():
        of_slots.arrive()
        grad = dot(mods_weights[...], slots[...], NT)
        sigmoid = 1.0 / (1.0 + jnp.exp(-condition[...]))
        grad = grad * (sigmoid * (1.0 + condition[...] * (1.0 - sigmoid)))
        piece[...] = grad.astype(BF16)
        of_piece.open()

    def condition_arrives():
        of_piece.arrive()
        compact(tall, pieces, 0)
        grad_condition[...] = jnp.transpose(tall[...]).astype(BF16)

    def near_line():
        return (at.r + 2 - 4 * (at.z % 2), at.b)

    def far_line():
        return (at.r + 4 - 8 * (at.z // 2), at.b)

    partners = (at.sibling, at.across_x, at.across_y, near_line(), far_line())

    def totals_copy(step):
        return remote(
            totals_own if step == 0 else totals.at[step - 1],
            totals_got.at[step],
            totals_send.at[step],
            totals_recv.at[step],
            partners[step],
        )

    def totals_step(step):
        totals_copy(step).wait_recv()
        before = totals_own[...] if step == 0 else totals[step - 1]
        totals[step] = before + totals_got[step]
        if step + 1 < len(partners):
            totals_copy(step + 1).start()

    for i in range(1, 4):
        band_copy(i).start()
    totals_copy(0).start()
    share_slots()
    of_first.arrive()
    of_first.near_stage(0, 4)
    totals_step(0)
    of_slots.along_line()
    of_first.near_stage(4, 8)
    of_slots.around_square()
    totals_step(1)
    of_slots.close_square()
    of_first.far_stage(0, 2)
    condition_back()
    of_first.far_stage(2, 4)
    totals_step(2)
    of_piece.along_line()
    of_first.line_stage(0)
    of_piece.around_square()
    totals_step(3)
    of_first.line_stage(1)
    of_piece.close_square()
    of_first.line_stage(2)
    totals_step(4)
    condition_arrives()
    of_first.last()
    of_first.finish()
    for i in range(1, 4):
        band_copy(i).wait_send()
    for step in range(len(partners)):
        totals_copy(step).wait_send()
    of_slots.finish()
    of_piece.finish()


def scatter_sums(matrices, slots_own, mods_weights, condition, totals_own):
    dma = pltpu.SemaphoreType.DMA
    anywhere, inside = (
        pl.BlockSpec(memory_space=pl.ANY),
        pl.BlockSpec(memory_space=pltpu.VMEM),
    )
    steps = 5
    return pl.pallas_call(
        scatter_kernel,
        in_specs=[anywhere] * 4 + [inside] * 4,
        out_specs=[inside] * 4,
        out_shape=[
            jax.ShapeDtypeStruct((BLOCK, D), F32),
            jax.ShapeDtypeStruct((128, 8 * D), BF16),
            jax.ShapeDtypeStruct((128, D), BF16),
            jax.ShapeDtypeStruct((steps, *totals_own.shape), F32),
        ],
        scratch_shapes=[
            pltpu.VMEM((4, 16, 2 * D), BF16),
            pltpu.VMEM((16, 2 * D), BF16),
            pltpu.VMEM((PADDED, 128), BF16),
            pltpu.VMEM((DEVICES, PADDED, 128), BF16),
            pltpu.VMEM((D, 128), F32),
            pltpu.VMEM((steps, *totals_own.shape), F32),
            dma((4,)),
            dma((4,)),
            dma((steps,)),
            dma((steps,)),
            *spread_sems(2),
            *collect_scratch(),
        ],
        compiler_params=pltpu.CompilerParams(
            collective_id=1, has_side_effects=True, vmem_limit_bytes=61 << 20
        ),
        name="scatter_sums",
    )(*matrices, slots_own, mods_weights, condition, totals_own)


def attend_kernel(apart, q_ref, k_ref, v_ref, *rest, travels):
    head = pl.program_id(0)
    if travels:
        up_own, out_ref, log_ref, up, line_send, line_recv, spread_sem = rest
        at = Place()

        def in_up(r, b, start, size):
            rows = pl.ds(pl.multiple_of(r * BLOCK + start, 16), size)
            return up.at[rows, pl.ds(pl.multiple_of(b * D, 128), D)]

        def bytes_of(rows, width):
            return up.at[pl.ds(0, rows // 4), :]

        sems = line_send.at[0], line_recv.at[0], spread_sem.at[0]
        of_up = Spread(at, in_up, up_own, BLOCK, D, SPLIT[1], bytes_of, sems)

        def begin():
            at.greet()
            of_up.open()

        at_step(head, 0, begin)
        at_step(head, 3, lambda: of_up.along_line((1,)))
        at_step(head, 5, lambda: of_up.along_line((2,)))
        at_step(head, 7, lambda: of_up.along_line((3,)))
        at_step(head, 10, of_up.around_square)
        at_step(head, 14, of_up.close_square)
    else:
        out_ref, log_ref = rest
    attend_head(head, apart, q_ref, k_ref, v_ref, out_ref, log_ref, min(512, q_ref.shape[0]))
    if travels:

        def end():
            of_up.arrive()
            of_up.finish()

        at_step(head, HEADS - 1, end)


def attend_back_kernel(apart, q_ref, k_ref, v_ref, grad_ref, log_ref, *rest, travels):
    head = pl.program_id(0)
    if travels:
        up_grad, dq_ref, dk_ref, dv_ref, up_sum, *rest = rest
        at = Place()

        def part(b):
            return [(up_grad.at[:, pl.ds(b * D, D)], 0, D)]

        of_up = Collect(at, part, up_sum, rest[:5], rest[5:], SPLIT[1])

        def begin():
            at.greet()
            of_up.start()

        at_step(head, 0, begin)
        at_step(head, 1, of_up.arrive)
        for step in range(4):
            at_step(head, 1 + step, lambda: of_up.near_stage(2 * step, 2 * step + 2))
            at_step(head, 6 + step, lambda: of_up.far_stage(step, step + 1))
        for step in range(3):
            at_step(head, 11 + step, lambda: of_up.line_stage(step))
    else:
        dq_ref, dk_ref, dv_ref = rest
    attend_back_head(
        head, apart, q_ref, k_ref, v_ref, grad_ref, log_ref, dq_ref, dk_ref, dv_ref
    )
    if travels:

        def end():
            of_up.last()
            of_up.finish()

        at_step(head, HEADS - 1, end)


def attend(apart, queries, keys, values, up_own):
    q_len, k_len = queries.shape[0], keys.shape[0]
    travels = up_own is not None
    anywhere = pl.BlockSpec(memory_space=pl.ANY)
    return pl.pallas_call(
        functools.partial(attend_kernel, travels=travels),
        grid=(HEADS,),
        in_specs=[
            whole_block(apart.shape),
            whole_block((q_len, D)),
            whole_block((k_len, D)),
            whole_block((k_len, D)),
        ]
        + [anywhere] * travels,
        out_specs=[whole_block((q_len, D)), whole_block((HEADS, q_len))] + [anywhere] * travels,
        out_shape=[
            jax.ShapeDtypeStruct((q_len, D), BF16),
            jax.ShapeDtypeStruct((HEADS, q_len), F32),
        ]
        + [jax.ShapeDtypeStruct((D, FF), BF16)] * travels,
        scratch_shapes=spread_sems(1) if travels else [],
        compiler_params=pltpu.CompilerParams(
            vmem_limit_bytes=56 << 20,
            **(dict(collective_id=2, has_side_effects=True) if travels else {}),
        ),
        name="attend_rows",
    )(apart, queries, keys, values, *((up_own,) if travels else ()))


def attend_back(apart, queries, keys, values, grads, log_total, up_grad):
    q_len, k_len = queries.shape[0], keys.shape[0]
    travels = up_grad is not None
    anywhere = pl.BlockSpec(memory_space=pl.ANY)
    return pl.pallas_call(
        functools.partial(attend_back_kernel, travels=travels),
        grid=(HEADS,),
        in_specs=[
            whole_block(apart.shape),
            whole_block((q_len, D)),
            whole_block((k_len, D)),
            whole_block((k_len, D)),
            whole_block((q_len, D)),
            whole_block((HEADS, q_len)),
        ]
        + [anywhere] * travels,
        out_specs=[whole_block((q_len, D)), whole_block((k_len, D)), whole_block((k_len, D))]
        + [whole_block((BLOCK, D))] * travels,
        out_shape=[
            jax.ShapeDtypeStruct((q_len, D), BF16),
            jax.ShapeDtypeStruct((k_len, D), BF16),
            jax.ShapeDtypeStruct((k_len, D), BF16),
        ]
        + [jax.ShapeDtypeStruct((BLOCK, D), F32)] * travels,
        scratch_shapes=collect_scratch() if travels else [],
        compiler_params=pltpu.CompilerParams(
            vmem_limit_bytes=61 << 20,
            **(dict(collective_id=3, has_side_effects=True) if travels else {}),
        ),
        name="attend_rows_back",
    )(apart, queries, keys, values, grads, log_total, *((up_grad,) if travels else ()))


def matmul(operand, weights):
    return jnp.einsum("...i,ij->...j", operand, weights, preferred_element_type=F32)


def matmul_back(gradient, weights):
    return jnp.einsum("...j,ij->...i", gradient, weights, preferred_element_type=F32)


def outer_sum(operand, gradient):
    return jnp.einsum(
        "ni,nj->ij",
        operand.reshape(-1, operand.shape[-1]),
        gradient.reshape(-1, gradient.shape[-1]),
        preferred_element_type=F32,
    )


def column_sum(gradient):
    return jnp.sum(gradient.reshape(-1, gradient.shape[-1]), axis=0, dtype=F32)


def silu_back(values, gradient):
    return jax.vjp(jax.nn.silu, values)[1](gradient)[0]


def plan(time_steps):
    steps_all = jnp.arange(TIMESTEPS, dtype=jnp.int32)
    betas = BETA_LOW + (BETA_HIGH - BETA_LOW) * steps_all.astype(F32) / (TIMESTEPS - 1)
    cumulate = jnp.cumsum(jnp.log1p(-betas))
    pick_now = (time_steps[..., None] == steps_all).astype(F32)
    pick_prev = (time_steps[..., None] - 1 == steps_all).astype(F32)
    return jnp.stack(
        [
            jnp.sum(pick_now * betas, axis=-1),
            jnp.sum(pick_now * cumulate, axis=-1),
            jnp.sum(pick_prev * cumulate, axis=-1),
        ],
        axis=-1,
    )


def time_features(time_steps):
    half_width = FREQ // 2
    frequency = jnp.exp(-math.log(10000.0) * jnp.arange(half_width).astype(F32) / half_width)
    angles = time_steps.astype(F32)[..., None] * frequency
    return jnp.concatenate([jnp.cos(angles), jnp.sin(angles)], axis=-1)


def positions(four_way):
    quarter = D // 4
    omegas = jnp.exp(-math.log(10000.0) * jnp.arange(quarter).astype(F32) / quarter)
    angles = jnp.arange(GRID).astype(F32)[:, None] * omegas
    table = jnp.concatenate([jnp.sin(angles), jnp.cos(angles)], axis=-1)

    def grid(side):
        shape = (PATCHES // side**2, side, side, D // 2)
        down = jnp.broadcast_to(table[None, :side, None], shape)
        across = jnp.broadcast_to(table[None, None, :side], shape)
        return jnp.concatenate([down, across], axis=-1).reshape(SLOTS, SEGMENT, D)

    return jnp.where(four_way, grid(GRID // 2), grid(GRID))


def layer_norm(values):
    centered = values - jnp.mean(values, axis=-1, keepdims=True)
    return centered * lax.rsqrt(jnp.mean(centered * centered, axis=-1, keepdims=True) + NORM_EPS)


def modulate(values, shift, scaling):
    return layer_norm(values) * (1.0 + scaling) + shift


def patch_loss(output, target_noise, patch_sched):
    beta = patch_sched[..., 0:1]
    log_now = patch_sched[..., 1:2]
    log_prev = patch_sched[..., 2:3]
    error = output[..., :PATCH_IN] - target_noise
    log_beta = jnp.log(beta)
    keep_now = -jnp.expm1(log_now)
    log_post = log_beta + jnp.log(-jnp.expm1(log_prev)) - jnp.log(keep_now)
    coefficient = beta * lax.rsqrt(keep_now * (1.0 - beta))
    fraction = 0.5 * (output[..., PATCH_IN:] + 1.0)
    log_model = fraction * log_beta + (1.0 - fraction) * log_post
    diverge = 0.5 * (
        -1.0
        + log_model
        - log_post
        + jnp.exp(log_post - log_model)
        + (coefficient * error) ** 2 * jnp.exp(-log_model)
    )
    return jnp.mean(error * error, axis=-1) + jnp.mean(diverge, axis=-1) / math.log(2.0)


def adamw_step(weight, first_old, second_old, gradient, step_rate):
    first_new = DECAY_FIRST * first_old + (1.0 - DECAY_FIRST) * gradient
    second_new = DECAY_SECOND * second_old + (1.0 - DECAY_SECOND) * gradient * gradient
    first_hat = first_new / (1.0 - DECAY_FIRST**STEP)
    second_hat = second_new / (1.0 - DECAY_SECOND**STEP)
    return (
        weight - step_rate * first_hat / (jnp.sqrt(second_hat) + ADAM_EPS),
        first_new,
        second_new,
    )


def body(
    sizes,
    latents,
    gauss_noise,
    image_counts,
    timesteps,
    labels,
    wide_weights,
    square_weights,
    down_weights,
    embed_tables,
    all_biases,
    head_weights,
    first_wide,
    first_square,
    first_down,
    first_tables,
    first_biases,
    first_head,
    second_wide,
    second_square,
    second_down,
    second_tables,
    second_biases,
    second_head,
):
    n_rows, n_band = sizes
    n_all = n_rows * n_band
    rows_here, band_len, _ = latents.shape
    share = n_band // rows_here
    part_len = PATCHES // share
    at_row, at_band = lax.axis_index("rows"), lax.axis_index("band")
    own_row = at_band // share
    part_start = (at_band % share) * part_len
    n_slots = n_rows * rows_here * SLOTS
    groups = [[row * share + i for i in range(share)] for row in range(rows_here)]

    def in_row_gather(array):
        if share == 1:
            return array
        return lax.all_gather(array, "band", axis=0, tiled=True, axis_index_groups=groups)

    def in_row_scatter(array):
        if share == 1:
            return array
        return lax.psum_scatter(
            array, "band", scatter_dimension=0, tiled=True, axis_index_groups=groups
        )

    def in_row_sum(array):
        if share == 1:
            return array
        return lax.psum(array, "band", axis_index_groups=groups)

    tuned = sizes == (ROWS_AXIS, DEVICES // ROWS_AXIS)
    n_seg = part_len // SEGMENT
    given = jnp.concatenate([latents, gauss_noise], axis=-1)
    count = lax.dynamic_slice_in_dim(image_counts, own_row, 1)[0]
    four_way = count == SLOTS
    seg_first = part_start // SEGMENT + jnp.arange(n_seg)
    seg_slot = jnp.where(four_way, seg_first, 0)
    seg_hot = (seg_slot[:, None] == jnp.arange(SLOTS)).astype(F32)

    def by_segment(per_slot):
        return jnp.sum(seg_hot[:, :, None] * per_slot[None], axis=1)[:, None]

    wide_low = wide_weights.astype(BF16)
    square_low = square_weights.astype(BF16)
    down_low = down_weights.astype(BF16)
    tables_low = embed_tables.astype(BF16)
    biases_low = all_biases.astype(BF16)
    mods_low = wide_low[:, 3 * D + FF :]
    time_out_low = square_low[:, D:]
    first_group = jnp.concatenate([wide_low[:, : 3 * D], square_low[:, :D]], axis=1)
    up_group = wide_low[:, 3 * D : 3 * D + FF]
    head_low = head_weights.astype(BF16)
    head_matrix = head_low[:D]
    small_rows = jnp.concatenate([biases_low, tables_low[FREQ : FREQ + PATCH_IN]], axis=0)
    device = at_row * n_band + at_band
    if tuned:
        padded = lambda array: jnp.pad(array, ((0, PADDED - OWN), (0, 0)))
        regroup = functools.partial(
            lax.all_to_all, axis_name="band", split_axis=1, concat_axis=0, tiled=True
        )
        own_times = timesteps.reshape(-1)
        codes = (labels + 1024 * image_counts[:, None]).reshape(-1, 1)
        own_codes = jnp.broadcast_to(codes, (rows_here * SLOTS, 128))
        class_columns = jnp.pad(tables_low[FREQ + PATCH_IN :].T, ((0, 0), (0, 1024 - CLASSES)))
        (
            first_all,
            mods,
            condition_all,
            small_all,
            time_act_all,
            time_pre,
            frequency,
            codes,
            given,
        ) = gather_weights(
            regroup(first_group.reshape(-1, 4, D))[:, 0],
            padded(time_out_low),
            padded(mods_low),
            time_features(own_times).astype(BF16),
            own_codes,
            padded(tables_low[:FREQ].T),
            jnp.broadcast_to(padded(biases_low[1][:, None].astype(F32)), (PADDED, 128)),
            padded(class_columns),
            jnp.pad(small_rows.T, ((0, PADDED - OWN), (0, 128 - small_rows.shape[0]))),
            given.transpose(0, 2, 1),
        )
        given = given.T
        up_own = regroup(up_group.reshape(-1, 4, D))[:, 0]
        down_own, first_all = lax.optimization_barrier((down_low, first_all))
        down_all = lax.all_gather(down_own, AXES, axis=0, tiled=True)
        weight_q, weight_k, weight_v, weight_o = first_all
        biases = small_all[: all_biases.shape[0]]
        patch_in = small_all[all_biases.shape[0] :][:PATCH_IN].astype(BF16)
        mods = lax.dynamic_slice_in_dim(mods, (at_band % 2) * SLOTS, SLOTS, 0)
        own_columns = lambda array: lax.dynamic_slice_in_dim(array, device * OWN, OWN, 1)
        condition = own_columns(condition_all)
        time_act = own_columns(time_act_all)
        time_pre = time_pre[:OWN].T
        labels_all = codes[:, 0] & 1023
        images = (jnp.sum(codes[:, 0] >> 10) // SLOTS).astype(F32)
        cond_act = jax.nn.silu(condition).astype(BF16)
    else:
        given = lax.all_gather(given, "band", axis=1, tiled=True)
        given = lax.dynamic_slice_in_dim(given, own_row, 1, 0)[0]
        given = lax.dynamic_slice_in_dim(given, part_start, part_len, 0)
        codes = jnp.concatenate([timesteps, labels, image_counts[:, None]], axis=1)
        codes = lax.all_gather(codes, "rows", axis=0, tiled=True)
        labels_all = codes[:, SLOTS : 2 * SLOTS].reshape(n_slots)
        images = jnp.sum(codes[:, 2 * SLOTS]).astype(F32)
        frequency = time_features(codes[:, :SLOTS].reshape(n_slots)).astype(BF16)
        first_all = lax.all_gather(first_group, AXES, axis=0, tiled=True)
        up_all = lax.all_gather(up_group, AXES, axis=0, tiled=True)
        down_all = lax.all_gather(down_low, AXES, axis=0, tiled=True)
        weight_q, weight_k, weight_v, weight_o = jnp.split(first_all, 4, axis=1)
        small_all = lax.all_gather(small_rows, AXES, axis=1, tiled=True)
        biases = small_all[: all_biases.shape[0]].astype(F32)
        patch_in = small_all[all_biases.shape[0] :]
        own_biases = biases_low.astype(F32)
        time_pre = matmul(frequency, tables_low[:FREQ]) + own_biases[1]
        time_act = jax.nn.silu(time_pre).astype(BF16)
        class_rows = tables_low[FREQ + PATCH_IN :]
        class_part = class_rows[labels_all].astype(F32)
        time_out_columns = lax.all_to_all(
            time_out_low, AXES, split_axis=1, concat_axis=0, tiled=True
        )
        time_act_all = lax.all_gather(time_act, AXES, axis=1, tiled=True)
        condition = matmul(time_act_all, time_out_columns) + own_biases[2] + class_part
        cond_act = jax.nn.silu(condition).astype(BF16)
        mods_columns = lax.all_to_all(mods_low, AXES, split_axis=1, concat_axis=0, tiled=True)
        cond_act_all = lax.all_gather(cond_act, AXES, axis=1, tiled=True)
        mods_part = matmul(cond_act_all, mods_columns)
        mods_part = mods_part.reshape(n_rows * rows_here, SLOTS, -1)
        if share > 1:
            mods_part = jnp.repeat(mods_part, share, axis=0)
        mods = lax.all_to_all(mods_part, AXES, split_axis=0, concat_axis=2, tiled=True)[0]
    label_hot = (labels_all[:, None] == jnp.arange(CLASSES, dtype=jnp.int32)).astype(BF16)
    mods_bias = jnp.concatenate([biases[3:9].reshape(-1), biases[17:19].reshape(-1)])
    seg_mods = by_segment(mods + mods_bias)
    (
        shift_one,
        scale_one,
        gate_one,
        shift_two,
        scale_two,
        gate_two,
        final_shift,
        final_scale,
    ) = jnp.split(seg_mods, 8, axis=-1)

    given = given.reshape(n_seg, SEGMENT, 2 * PATCH_IN)
    row_latents, row_noise = given[..., :PATCH_IN], given[..., PATCH_IN:]
    own_times = lax.dynamic_slice_in_dim(timesteps, own_row, 1, 0)[0]
    patch_sched = by_segment(plan(own_times))
    log_now = patch_sched[..., 1:2]
    noisy = (
        jnp.exp(0.5 * log_now) * row_latents + jnp.sqrt(-jnp.expm1(log_now)) * row_noise
    ).astype(BF16)
    position = lax.dynamic_slice_in_dim(positions(four_way), part_start // SEGMENT, n_seg, 0)
    hidden_zero = matmul(noisy, patch_in) + biases[0] + position
    normed_one = modulate(hidden_zero, shift_one, scale_one).astype(BF16)
    flat = lambda array: array.reshape(part_len, array.shape[-1])
    deep = lambda array: array.reshape(n_seg, SEGMENT, array.shape[-1])
    queries = flat(matmul(normed_one, weight_q) + biases[9]).astype(BF16)
    keys = flat(matmul(normed_one, weight_k)).astype(BF16)
    values = flat(matmul(normed_one, weight_v) + biases[10]).astype(BF16)
    keys, values = in_row_gather(keys), in_row_gather(values)
    key_seg = jnp.where(four_way, jnp.arange(SLOTS), 0)
    apart = jnp.where(key_seg[:, None] == jnp.repeat(seg_slot, SEGMENT), 0.0, -1e30).astype(F32)
    if tuned:
        attended, log_total, up_all = attend(apart, queries, keys, values, up_own)
    else:
        attended, log_total = attend(apart, queries, keys, values, None)
    attended = deep(attended)
    branch_one = matmul(attended, weight_o) + biases[11]
    hidden_one = hidden_zero + gate_one * branch_one
    normed_two = modulate(hidden_one, shift_two, scale_two).astype(BF16)
    upward = matmul(normed_two, up_all) + biases[12:16].reshape(-1)
    active = jax.nn.gelu(upward, approximate=True).astype(BF16)
    branch_two = matmul(active, down_all) + biases[16]
    hidden_two = hidden_one + gate_two * branch_two
    normed_out = modulate(hidden_two, final_shift, final_scale).astype(BF16)
    output = matmul(normed_out, head_matrix) + head_low[D].astype(F32)
    patch_share = jnp.where(four_way, 1.0 / SEGMENT, 1.0 / PATCHES)
    losses, loss_back = jax.vjp(lambda at: patch_loss(at, row_noise, patch_sched), output)
    loss_local = jnp.sum(patch_share * losses)

    grad_out = loss_back(jnp.broadcast_to(patch_share / images, losses.shape))[0].astype(BF16)
    grad_two, grad_fshift, grad_fscale = jax.vjp(modulate, hidden_two, final_shift, final_scale)[1](
        matmul_back(grad_out, head_matrix)
    )
    seg_sum = lambda array: jnp.sum(array, axis=1, keepdims=True)
    grad_gate_two = seg_sum(grad_two * branch_two)
    grad_branch_two = (gate_two * grad_two).astype(BF16)
    down_grad = outer_sum(active, grad_branch_two)
    grad_active = matmul_back(grad_branch_two, down_all)
    grad_upward = jax.vjp(lambda at: jax.nn.gelu(at, approximate=True), upward)[1](grad_active)[
        0
    ].astype(BF16)
    up_grad = outer_sum(normed_two, grad_upward)
    grad_one_part, grad_shift_two, grad_scale_two = jax.vjp(
        modulate, hidden_one, shift_two, scale_two
    )[1](matmul_back(grad_upward, up_all))
    grad_one = grad_two + grad_one_part
    grad_gate_one = seg_sum(grad_one * branch_one)
    grad_branch_one = (gate_one * grad_one).astype(BF16)
    output_grad = outer_sum(attended, grad_branch_one)
    grad_attended = flat(matmul_back(grad_branch_one, weight_o).astype(BF16))
    if tuned:
        grad_query, grad_key, grad_value, up_sum = attend_back(
            apart, queries, keys, values, grad_attended, log_total, up_grad.astype(BF16)
        )
    else:
        grad_query, grad_key, grad_value = attend_back(
            apart, queries, keys, values, grad_attended, log_total, None
        )
    grad_key, grad_value = in_row_scatter(grad_key), in_row_scatter(grad_value)
    q_grad = outer_sum(normed_one, grad_query)
    k_grad = outer_sum(normed_one, grad_key)
    v_grad = outer_sum(normed_one, grad_value)
    grad_normed = deep(
        matmul_back(grad_query, weight_q)
        + matmul_back(grad_key, weight_k)
        + matmul_back(grad_value, weight_v)
    )
    grad_zero_part, grad_shift_one, grad_scale_one = jax.vjp(
        modulate, hidden_zero, shift_one, scale_one
    )[1](grad_normed)
    grad_zero = (grad_one + grad_zero_part).astype(BF16)
    patch_grad = outer_sum(noisy, grad_zero)

    seg_grads = jnp.concatenate(
        [
            grad_shift_one,
            grad_scale_one,
            grad_gate_one,
            grad_shift_two,
            grad_scale_two,
            grad_gate_two,
            grad_fshift,
            grad_fscale,
        ],
        axis=-1,
    )
    slot_grads = in_row_sum(jnp.sum(seg_hot[:, :, None] * seg_grads, axis=0)).astype(BF16)
    last_row = jnp.concatenate([column_sum(grad_out), loss_local[None]])
    totals = jnp.concatenate(
        [
            column_sum(grad_zero)[None],
            column_sum(grad_query)[None],
            column_sum(grad_value)[None],
            column_sum(grad_branch_one)[None],
            column_sum(grad_upward).reshape(FF // D, D),
            column_sum(grad_branch_two)[None],
            patch_grad,
            outer_sum(grad_out, normed_out),
            jnp.pad(last_row, (0, D - last_row.shape[0]))[None],
        ],
        axis=0,
    )
    if tuned:
        slots_own = jnp.where(
            (jnp.arange(4 * SLOTS) // SLOTS == at_band)[:, None], jnp.tile(slot_grads, (4, 1)), 0
        ).astype(BF16)
        regroup_back = functools.partial(
            lax.all_to_all, axis_name="band", split_axis=0, concat_axis=1, tiled=True
        )
        up_squares = jnp.sum(up_sum * up_sum)
        up_grad = regroup_back(up_sum[:, None]).reshape(-1, FF)
        matrices = (q_grad, k_grad, v_grad, output_grad)
        down_grad = lax.psum_scatter(
            down_grad.astype(BF16), AXES, scatter_dimension=0, tiled=True
        )
        slots_own, down_grad = lax.optimization_barrier((slots_own, down_grad))
        down_grad = down_grad.astype(F32)
        sums, slot_grads, grad_condition_all, totals = scatter_sums(
            [array.astype(BF16) for array in matrices],
            slots_own,
            padded(mods_low),
            padded(condition.T),
            jnp.pad(totals, ((0, -totals.shape[0] % 8), (0, 0))),
        )
        totals = totals[-1]
        first_grad = regroup_back(sums[:, None]).reshape(-1, 4 * D)
        local_squares = jnp.sum(sums * sums) + up_squares + jnp.sum(down_grad * down_grad)
        grad_condition = own_columns(grad_condition_all)
    else:
        slot_grads = lax.all_gather(slot_grads, AXES, axis=0, tiled=True)
        if share > 1:
            slot_grads = slot_grads.reshape(-1, share, SLOTS, 8 * D)[:, 0].reshape(n_slots, 8 * D)
        grad_condition = silu_back(condition, matmul_back(slot_grads, mods_low)).astype(BF16)
        grad_condition_all = lax.all_gather(grad_condition, AXES, axis=1, tiled=True)

        def scatter(array):
            return lax.psum_scatter(array, AXES, scatter_dimension=0, tiled=True)

        first_grad = scatter(jnp.concatenate([q_grad, k_grad, v_grad, output_grad], axis=1))
        up_grad = scatter(up_grad)
        down_grad = scatter(down_grad)
        local_squares = sum(jnp.sum(array * array) for array in (first_grad, up_grad, down_grad))
        totals = lax.psum(totals, AXES)
    mods_grad = outer_sum(cond_act, slot_grads)
    mods_bias_grad = column_sum(slot_grads).reshape(8, n_all, -1)
    time_out_grad = outer_sum(time_act, grad_condition_all)
    class_grad = outer_sum(label_hot, grad_condition)
    grad_time_pre = silu_back(time_pre, matmul_back(grad_condition_all, time_out_low)).astype(BF16)
    time_in_grad = outer_sum(frequency, grad_time_pre)
    n_sums = 9 + PATCH_IN
    own_width = D // n_all
    row_grads = lax.dynamic_slice_in_dim(totals[:n_sums], device * own_width, own_width, 1)
    head_total = jnp.concatenate(
        [totals[n_sums : n_sums + 32].T, totals[n_sums + 32, :32][None]], axis=0
    )
    loss_sum = totals[n_sums + 32, 32]
    own_mods_bias = lax.dynamic_index_in_dim(mods_bias_grad, device, 1, keepdims=False)
    grad_wide = jnp.concatenate([first_grad[:, : 3 * D], up_grad, mods_grad], axis=1)
    grad_square = jnp.concatenate([first_grad[:, 3 * D :], time_out_grad], axis=1)
    grad_tables = jnp.concatenate([time_in_grad, row_grads[9:], class_grad], axis=0)
    grad_biases = jnp.concatenate(
        [
            row_grads[:1],
            column_sum(grad_time_pre)[None],
            column_sum(grad_condition)[None],
            own_mods_bias[:6],
            row_grads[1:9],
            own_mods_bias[6:],
        ],
        axis=0,
    )
    owned_grads = (grad_wide, grad_square, down_grad, grad_tables, grad_biases)
    for array in (mods_grad, time_out_grad, grad_tables, grad_biases):
        local_squares = local_squares + jnp.sum(array * array)
    squares = lax.all_to_all(
        jnp.broadcast_to(local_squares, (n_all, 1, 128)), AXES, split_axis=0, concat_axis=1, tiled=True
    )
    grad_norm = jnp.sqrt(jnp.sum(squares[0, :, 0]) + jnp.sum(head_total * head_total))
    clip_factor = jnp.minimum(1.0, CLIP_NORM / (grad_norm + 1e-06))
    params = (wide_weights, square_weights, down_weights, embed_tables, all_biases, head_weights)
    firsts = (first_wide, first_square, first_down, first_tables, first_biases, first_head)
    seconds = (second_wide, second_square, second_down, second_tables, second_biases, second_head)
    gradients = owned_grads + (head_total,)
    results = [
        adamw_step(
            params[which],
            firsts[which],
            seconds[which],
            gradients[which] * clip_factor,
            LEARN_RATES[which],
        )
        for which in range(6)
    ]
    return (
        tuple(result[0] for result in results)
        + tuple(result[1] for result in results)
        + tuple(result[2] for result in results)
        + tuple(result[0].astype(BF16) for result in results)
        + (grad_norm, loss_sum, images)
    )


def solution(mesh):
    sizes = (mesh.shape["rows"], mesh.shape["band"])
    by_row, by_column, copied = P(AXES, None), P(None, AXES), P()
    params = (by_row, by_row, by_row, by_column, by_column, copied)
    patches = P("rows", "band", None)
    return jax.shard_map(
        functools.partial(body, sizes),
        mesh=mesh,
        in_specs=(patches, patches, P("rows"), P("rows", None), P("rows", None)) + 3 * params,
        out_specs=4 * params + (copied, copied, copied),
        check_vma=False,
    )
```

time: 3580 us -> 862 us (0.24)
  blocking collectives: 1530 us -> 0 us
  waiting for transfers between devices: 717 us -> 4.84 us
  Pallas kernels: 0 us -> 453 us
  local copies, waits for them, and re-layouts: 367 us -> 36.3 us
  matrix products: 479 us -> 224 us
  other arithmetic: 277 us -> 85.2 us
  starting transfers between devices: 169 us -> 23.9 us
    unnamed x1 -> x0, blocking collectives: 1240 us -> none
    pallas_call x0 -> x4, Pallas kernels: none -> 453 us  [the longest x1 134 us: scatter_sums(): pl.pallas_call(scatter_kernel, in_specs=[anywhere] * 4 + [inside] * 4, ou...]
    all_gather x6 -> x1, waiting for transfers between devices: 360 us -> 0.02 us  [body(): down_all = lax.all_gather(down_own, AXES, axis=0, tiled=True)]
    psum x2 -> x0, blocking collectives: 243 us -> none  [the longest x1 223 us: body(): square_total = lax.psum(local_squares, ('rows', 'band'))]
    dot_general x51 -> x16, matrix products: 383 us -> 151 us  [the longest x8 79.6 us: matmul_back(): jnp.einsum('...j,ij->...i', gradient, weights, preferred_element_type=F32)]
    unnamed x21 -> x2, waiting for transfers between devices: 213 us -> 0.04 us
    unnamed x291 -> x213, local copies, waits for them, and re-layouts: 201 us -> 10.1 us
    unnamed x10 -> x0, starting transfers between devices: 169 us -> none
  transfers between devices with their start and end apart: 19 -> 7, of which waited for: 11 -> 3; matrix products, arithmetic and copies ran while one was open for 49% -> 21% of each run, Pallas kernels for 0% -> 25%
where the time goes in v1:
time: 862 us; the launch traced here: 855 us
  Pallas kernels  453 us (53%)
  matrix products  224 us (26%)
  other arithmetic  85.2 us (10%)
  local copies, waits for them, and re-layouts  36.3 us (4%)
  between operations  27.5 us (3%)
  starting transfers between devices  23.9 us (3%)
    pallas_call x1, Pallas kernels, scatter_sums(): pl.pallas_call(scatter_kernel, in_specs=[anywhere] * 4 + [inside] * 4, ou...  134 us
    pallas_call x1, Pallas kernels, attend_back(): pl.pallas_call(functools.partial(attend_back_kernel, travels=travels), gr...  128 us
    pallas_call x1, Pallas kernels, gather_weights(): pl.pallas_call(gather_kernel, in_specs=[anywhere] * 3 + [inside] * 7, out...  101 us
    pallas_call x1, Pallas kernels, attend(): pl.pallas_call(functools.partial(attend_kernel, travels=travels), grid=(H...  89.9 us
    dot_general x8, matrix products, matmul_back(): jnp.einsum('...j,ij->...i', gradient, weights, preferred_element_type=F32)  79.6 us
    dot_general x12, matrix products, outer_sum(): jnp.einsum('ni,nj->ij', operand.reshape(-1, operand.shape[-1]), gradient....  73.3 us
    dot_general x8, matrix products, matmul(): jnp.einsum('...i,ij->...j', operand, weights, preferred_element_type=F32)  71.5 us
    reduce_sum x7, other arithmetic, column_sum(): return jnp.sum(gradient.reshape(-1, gradient.shape[-1]), axis=0, dtype=F32)  22.8 us
  transfers between devices with their start and end apart: 7, of which 3 were waited for; matrix products, arithmetic and copies ran while one was open for 21% of the time, Pallas kernels for 25%

profile of v1, /device:TPU:0, one launch (start us, length us, event | category | flops | bytes accessed | tf_op | source)
XLA Modules:
  0.0 855.3 jit_solution(10527772246834260417)
XLA Ops:
  25.6 101.2 %gather_weights.1 = (bf16[4,1152,1152]{2,1,0:T(8,128)(2,1)S(1)}, f32[8,9216]{1,0:T(8,128)S(1)}, f32[128,1152]{1,0:T(8,128)S(1)}, f32[128,1152]{1,0:T(8,128)S(1)}...) custom-call(bf16[144,1152]{1,0:T(8,128)(2,1)S(1)} %squeeze.10.own, ...), custom_call_target="tpu_custom_call" | custom-call | tf_op jit(solution)/shard_map/gather_weights/pallas_call | solution.py:535
  161.0 4.9 convolution_convert_fusion.5.k_ref
  175.4 89.9 %attend_rows.1 = (bf16[1024,1152]{1,0:T(8,128)(2,1)}, f32[16,1024]{1,0:T(8,128)}, bf16[1152,4608]{1,0:T(8,128)(2,1)}) custom-call(f32[4,1024]{1,0:T(4,128)} %compare_select_fusion.apart, bf16[1024,1152]{1,0:T(8,128)(2,1)} %bitcast.263, bf16[1024,1152]{1,0:T(8,128)(2,1)} %convolution_convert_fusion.5.k_ref, bf16[1024,1152]{1,0:T(8,128)(2,1)} %bitcast.261, ...), custom_call_target="tpu_custom_call" | custom-call | tf_op jit(solution)/shard_map/attend_rows/pallas_call | solution.py:1059
  265.3 8.2 fusion.106
  275.7 19.6 %fusion.17 = f32[4,256,4608]{2,1,0:T(8,128)} fusion(bf16[1152,4608]{1,0:T(8,128)(2,1)} %get-tuple-element.57, f32[4,256,1152]{2,1,0:T(8,128)S(1)} %get-tuple-element.138, f32[4,1152]{1,0:T(4,128)S(1)} %get-tuple-element.149, f32[4,1152]{1,0:T(4,128)S(1)} %get-tuple-element.150, f32[4,256]{1,0:T(4,128)S(1)} %fusion.77, f32[4,256]{1,0:T(4,128)S(1)} %broadcast_multiply_fusion.1), kind=kOutput, calls=%fused_computation.21 | convolution fusion | flops 10877534208 | bytes 34254848 | tf_op jit(solution)/shard_map/...i,ij->...j/dot_general | solution.py:1118
  295.3 24.6 %fusion.105 = (f32[4,256]{1,0:T(4,128)S(1)}, f32[4,256,1152]{2,1,0:T(8,128)}, f32[4,256,1152]{2,1,0:T(8,128)}) fusion(f32[4,256,1152]{2,1,0:T(8,128)} %copy-done.6, f32[4,1152]{1,0:T(4,128)S(1)} %get-tuple-element.151, f32[1152]{0:T(1024)S(1)} %get-tuple-element.84, bf16[4608,1152]{1,0:T(8,128)(2,1)} %all-gather.2.cloned.1.call-done, ...), kind=kOutput, calls=%fused_computation.300 | convolution fusion | flops 10923539456 | bytes 43692544 | tf_op jit(solution)/shard_map/...i,ij->...j/dot_general | solution.py:1118
  332.6 22.4 %fusion.1 = bf16[4608,1152]{1,0:T(8,128)(2,1)} fusion(bf16[4,256,1152]{2,1,0:T(8,128)(2,1)S(1)} %get-tuple-element.127, f32[4,256,4608]{2,1,0:T(8,128)} %fusion.17, f32[4608]{0:T(1024)S(1)} %add.443), kind=kOutput, calls=%fused_computation.5 | convolution fusion | flops 10924130304 | bytes 31868928 | tf_op jit(solution)/shard_map/ni,nj->ij/dot_general | solution.py:1126
  355.0 28.7 %convert_reduce_fusion = (f32[4608]{0:T(1024)S(1)}, bf16[4,256,4608]{2,1,0:T(8,128)(2,1)}) fusion(f32[4,256,4608]{2,1,0:T(8,128)} %fusion.17, f32[4608]{0:T(1024)S(1)} %add.443, bf16[4,256,1152]{2,1,0:T(8,128)(2,1)S(1)} %get-tuple-element.127, bf16[4608,1152]{1,0:T(8,128)(2,1)} %all-gather.2.cloned.1.call-done), kind=kOutput, calls=%fused_computation.13 | convolution fusion | flops 10980159488 | bytes 41324544 | tf_op jit(solution)/shard_map/...j,ij->...i/dot_general | solution.py:1122
  383.7 20.4 %multiply_reduce_fusion.5 = (f32[4,256]{1,0:T(4,128)S(1)}, f32[4,256,1152]{2,1,0:T(8,128)}) fusion(f32[4,256,1152]{2,1,0:T(8,128)} %copy-done.6, f32[4,1152]{1,0:T(4,128)S(1)} %copy-done.44, f32[4,256]{1,0:T(4,128)S(1)} %copy-done.59, bf16[4,256,4608]{2,1,0:T(8,128)(2,1)} %get-tuple-element.171, bf16[1152,4608]{1,0:T(8,128)(2,1)} %get-tuple-element.57), kind=kOutput, calls=%fused_computation.55 | convolution fusion | flops 10876353536 | bytes 29517824 | tf_op jit(solution)/shard_map/...j,ij->...i/dot_general | solution.py:1122
  404.1 18.4 %fusion.rest_0_ = bf16[1152,4608]{1,0:T(8,128)(2,1)} fusion(bf16[4,256,4608]{2,1,0:T(8,128)(2,1)} %get-tuple-element.171, f32[4,256,1152]{2,1,0:T(8,128)} %copy-done.6, f32[4,1152]{1,0:T(4,128)S(1)} %copy-done.76, f32[4,1152]{1,0:T(4,128)S(1)} %copy-done.44, f32[4,256]{1,0:T(4,128)S(1)} %copy-done.69, f32[4,256]{1,0:T(4,128)S(1)} %copy-done.59), kind=kOutput, calls=%fused_computation.4 | convolution fusion | flops 10882842624 | bytes 24817664 | tf_op jit(solution)/shard_map/ni,nj->ij/dot_general | solution.py:1126
  422.6 5.0 multiply_reduce_fusion.3
  427.9 6.8 convert_reduce_fusion.3
  434.7 7.6 convolution_convert_fusion.4
  443.8 127.6 %attend_rows_back.1 = (bf16[1024,1152]{1,0:T(8,128)(2,1)}, bf16[1024,1152]{1,0:T(8,128)(2,1)}, bf16[1024,1152]{1,0:T(8,128)(2,1)}, f32[144,1152]{1,0:T(8,128)}) custom-call(f32[4,1024]{1,0:T(4,128)} %compare_select_fusion.apart, bf16[1024,1152]{1,0:T(8,128)(2,1)} %bitcast.264, bf16[1024,1152]{1,0:T(8,128)(2,1)} %convolution_convert_fusion.5.k_ref, ...), custom_call_target="tpu_custom_call" | custom-call | tf_op jit(solution)/shard_map/attend_rows_back/pallas_call | solution.py:1088
  582.1 7.1 fusion.33
  589.3 5.2 fusion.29
  594.5 7.9 bitcast_multiply_fusion
  612.7 7.7 convert_reduce_fusion.6
  627.9 7.3 convolution_convert_fusion.2.key
  640.1 4.8 convolution_convert_fusion.1.value
  645.7 5.1 convolution_convert_fusion.output
  652.3 134.5 %scatter_sums.1 = (f32[144,1152]{1,0:T(8,128)}, bf16[128,9216]{1,0:T(8,128)(2,1)}, bf16[128,1152]{1,0:T(8,128)(2,1)}, f32[5,64,1152]{2,1,0:T(8,128)}) custom-call(bf16[1152,1152]{1,0:T(8,128)(2,1)} %convolution_convert_fusion.3.query, bf16[1152,1152]{1,0:T(8,128)(2,1)} %convolution_convert_fusion.2.key, bf16[1152,1152]{1,0:T(8,128)(2,1)} %convolution_convert_fusion.1.value, ...), custom_call_target="tpu_custom_call" | custom-call | tf_op jit(solution)/shard_map/scatter_sums/pallas_call | solution.py:950
  807.8 6.1 all-to-all-start.4
  839.7 6.3 fusion.102
  (411 shorter events, 150.6 us)
Async XLA Ops:
  12.3 11.4 %all-to-all-start = ((bf16[36,4,1152]{2,0,1:T(8,128)(2,1)}), bf16[36,4,1152]{2,0,1:T(8,128)(2,1)S(1)}, u32[]{:S(2)}, u32[]{:S(2)}) async-start(bf16[36,4,1152]{2,0,1:T(8,128)(2,1)} %copy.110), calls=%async_computation | async-start | bytes 737280 | tf_op jit(solution)/shard_map/all_to_all | solution.py:1321
  16.5 278.8 %all-gather.2.cloned.1.call-start = ((), (), s32[]{:S(2)}) async-start(), calls=%async_computation.6 | async-start | bytes 10948608 | tf_op jit(solution)/shard_map/all_gather | solution.py:1335
  20.4 122.1 %copy-start = (bf16[48,9216]{1,0:T(8,128)(2,1)}, bf16[48,9216]{1,0:T(8,128)(2,1)S(1)}, u32[]{:S(2)}) copy-start(bf16[48,9216]{1,0:T(8,128)(2,1)S(1)} %pad.53.mods_own.mods_weights) | copy-start | bytes 2654212
  133.4 17.2 %all-to-all-start.1 = ((bf16[36,4,1152]{2,0,1:T(8,128)(2,1)}), bf16[36,4,1152]{2,0,1:T(8,128)(2,1)S(1)}, u32[]{:S(2)}, u32[]{:S(2)}) async-start(bf16[36,4,1152]{2,0,1:T(8,128)(2,1)} %copy.114), calls=%async_computation.1 | async-start | bytes 737280 | tf_op jit(solution)/shard_map/all_to_all | solution.py:1333
  137.7 514.5 %reduce-scatter.2.cloned.1.call-start = ((), (), s32[]{:S(2)}) async-start(), calls=%async_computation.7 | async-start | bytes 10948608 | tf_op jit(solution)/shard_map/reduce_scatter | solution.py:1515
  157.5 107.7 %copy-start.3 = (f32[4,256,1152]{2,1,0:T(8,128)}, f32[4,256,1152]{2,1,0:T(8,128)S(1)}, u32[]{:S(2)}) copy-start(f32[4,256,1152]{2,1,0:T(8,128)S(1)} %get-tuple-element.162) | copy-start | bytes 14155780
  158.8 106.5 %copy-start.53 = (f32[4,1152]{1,0:T(4,128)}, f32[4,1152]{1,0:T(4,128)S(1)}, u32[]{:S(2)}) copy-start(f32[4,1152]{1,0:T(4,128)S(1)} %get-tuple-element.152) | copy-start | bytes 55300
  158.8 115.3 %copy-start.43 = (f32[4,1152]{1,0:T(4,128)}, f32[4,1152]{1,0:T(4,128)S(1)}, u32[]{:S(2)}) copy-start(f32[4,1152]{1,0:T(4,128)S(1)} %get-tuple-element.150) | copy-start | bytes 55300
  158.8 115.3 %copy-start.75 = (f32[4,1152]{1,0:T(4,128)}, f32[4,1152]{1,0:T(4,128)S(1)}, u32[]{:S(2)}) copy-start(f32[4,1152]{1,0:T(4,128)S(1)} %get-tuple-element.149) | copy-start | bytes 55300
  158.9 164.2 %copy-start.51 = (f32[4,1152]{1,0:T(4,128)}, f32[4,1152]{1,0:T(4,128)S(1)}, u32[]{:S(2)}) copy-start(f32[4,1152]{1,0:T(4,128)S(1)} %get-tuple-element.148) | copy-start | bytes 55300
  158.9 170.0 %copy-start.39 = (f32[4,1152]{1,0:T(4,128)}, f32[4,1152]{1,0:T(4,128)S(1)}, u32[]{:S(2)}) copy-start(f32[4,1152]{1,0:T(4,128)S(1)} %get-tuple-element.147) | copy-start | bytes 55300
  273.5 21.8 %copy-start.58 = (f32[4,256]{1,0:T(4,128)}, f32[4,256]{1,0:T(4,128)S(1)}, u32[]{:S(2)}) copy-start(f32[4,256]{1,0:T(4,128)S(1)} %broadcast_multiply_fusion.1) | copy-start | bytes 12292
  274.1 21.2 %copy-start.66 = (f32[4,256]{1,0:T(4,128)}, f32[4,256]{1,0:T(4,128)S(1)}, u32[]{:S(2)}) copy-start(f32[4,256]{1,0:T(4,128)S(1)} %multiply_reduce_fusion.8) | copy-start | bytes 12292
  274.1 21.2 %copy-start.68 = (f32[4,256]{1,0:T(4,128)}, f32[4,256]{1,0:T(4,128)S(1)}, u32[]{:S(2)}) copy-start(f32[4,256]{1,0:T(4,128)S(1)} %fusion.77) | copy-start | bytes 12292
  355.0 28.7 %copy-start.44 = (f32[4,1152]{1,0:T(4,128)S(1)}, f32[4,1152]{1,0:T(4,128)}, u32[]{:S(2)}) copy-start(f32[4,1152]{1,0:T(4,128)} %copy-done.43) | copy-start | bytes 55300
  355.0 28.7 %copy-start.59 = (f32[4,256]{1,0:T(4,128)S(1)}, f32[4,256]{1,0:T(4,128)}, u32[]{:S(2)}) copy-start(f32[4,256]{1,0:T(4,128)} %copy-done.58) | copy-start | bytes 12292
  574.2 76.6 %all-to-all-start.3 = ((f32[144,1,1152]{2,1,0:T(1,128)}), f32[144,1,1152]{2,1,0:T(1,128)}, u32[]{:S(2)}, u32[]{:S(2)}) async-start(f32[144,1,1152]{2,1,0:T(1,128)} %copy.120), calls=%async_computation.4 | async-start | bytes 1327104 | tf_op jit(solution)/shard_map/all_to_all | solution.py:1513
  788.9 38.1 %copy-start.31 = (f32[1273,36]{0,1:T(8,128)S(1)}, f32[1273,36]{0,1:T(8,128)}, u32[]{:S(2)}) copy-start(f32[1273,36]{0,1:T(8,128)} %param.31) | copy-start | bytes 549940
  792.9 36.2 %copy-start.15 = (f32[144,1152]{1,0:T(8,128)S(1)}, f32[144,1152]{1,0:T(8,128)}, u32[]{:S(2)}) copy-start(f32[144,1152]{1,0:T(8,128)} %param.30) | copy-start | bytes 1990660
  802.6 29.5 %copy-start.63 = (f32[19,36]{1,0:T(8,128)S(1)}, f32[19,36]{1,0:T(8,128)}, u32[]{:S(2)}) copy-start(f32[19,36]{1,0:T(8,128)} %param.32) | copy-start | bytes 8212
  802.6 29.5 %copy-start.79 = (f32[19,36]{1,0:T(8,128)S(1)}, f32[19,36]{1,0:T(8,128)}, u32[]{:S(2)}) copy-start(f32[19,36]{1,0:T(8,128)} %param.38) | copy-start | bytes 8212
  802.6 29.5 %copy-start.80 = (f32[19,36]{1,0:T(8,128)S(1)}, f32[19,36]{1,0:T(8,128)}, u32[]{:S(2)}) copy-start(f32[19,36]{1,0:T(8,128)} %param.44) | copy-start | bytes 8212
  807.8 13.2 %all-to-all-start.4 = ((f32[32,1,128]{2,1,0:T(1,128)}), f32[32,1,128]{2,1,0:T(1,128)S(1)}, u32[]{:S(2)}, u32[]{:S(2)}) async-start(f32[32,1,128]{2,1,0:T(1,128)} %broadcast_in_dim.209), calls=%async_computation.5 | async-start | bytes 32768 | tf_op jit(solution)/shard_map/all_to_all | solution.py:1577
  820.9 14.6 %all-to-all-start.2 = ((f32[144,1,1152]{2,1,0:T(1,128)}), f32[144,1,1152]{2,1,0:T(1,128)}, u32[]{:S(2)}, u32[]{:S(2)}) async-start(f32[144,1,1152]{2,1,0:T(1,128)} %copy.118), calls=%async_computation.3 | async-start | bytes 1327104 | tf_op jit(solution)/shard_map/all_to_all | solution.py:1528
  (82 other events, 588.2 us)
Sparse Core Ops, SparseCore 0:
  131.7 105.8 all-gather.1
  422.7 159.9 reduce-scatter.1

commit v2 on v1

--- a/solution.py
+++ b/solution.py
@@ -30,6 +30,9 @@
 DECAY_SECOND = 0.999
 ADAM_EPS = 1e-08
 LEARN_RATES = (0.1, 0.1, 0.05, 0.2, 0.3, 0.1)
+
+GELU_ROOT = math.sqrt(2.0 / math.pi)
+GELU_CUBE = 0.044715
 
 AXES = ("rows", "band")
 WINDOW = 256
@@ -129,6 +132,7 @@
 DEVICES = 32
 OWN = D // DEVICES
 PADDED = 48
+ROUNDED = 40
 PART = 384
 OWNERS = 24
 OWNER_OF = 7
@@ -164,11 +168,13 @@
         )
         pl.semaphore_wait(barrier, DEVICES - 1)
 
-    def each_source(self, do):
-        do(self.z)
-        for step in range(1, LINE):
-            pl.when(self.z - step >= 0)(functools.partial(do, self.z - step))
-            pl.when(self.z + step < LINE)(functools.partial(do, self.z + step))
+    def each_source(self, do, steps):
+        for step in steps:
+            if step == 0:
+                do(self.z)
+            else:
+                pl.when(self.z - step >= 0)(functools.partial(do, self.z - step))
+                pl.when(self.z + step < LINE)(functools.partial(do, self.z + step))
 
 
 def remote(source, target, send, receive, device):
@@ -237,7 +243,7 @@
                     pl.when(onward)(lambda: copy.start())
                     self.fan(z)
 
-    def around_square(self):
+    def around_square(self, steps=(0, 1, 2, 3)):
         at, cut = self.at, self.cut
 
         def do(z):
@@ -252,9 +258,9 @@
             self.to_x(part, part, 13 + z).start()
             self.to_sibling(ref, ref).start()
 
-        at.each_source(do)
-
-    def close_square(self):
+        at.each_source(do, steps)
+
+    def close_square(self, steps=(0, 1, 2, 3)):
         at, cut = self.at, self.cut
 
         def do(z):
@@ -265,7 +271,7 @@
             ref = self.block(2 * z + at.other_x, at.other_b)
             self.to_sibling(ref, ref).start()
 
-        at.each_source(do)
+        at.each_source(do, steps)
 
     def counted(self, rows):
         if self.width >= 128:
@@ -570,6 +576,9 @@
     )(*operands)
 
 
+ORDER = (3, 0, 2, 1)
+
+
 class Collect:
     def __init__(self, at, part, out, buffers, sems, cut):
         self.at, self.part, self.out, self.cut = at, part, out, cut
@@ -589,31 +598,36 @@
 
     def start(self):
         at = self.at
-        for y in (0, 1):
-            for core in (0, 1):
-
-                def begin(keep, y=y, b=2 * y + core):
-                    for source, first, rows in self.part(b):
-                        self.move(y, pl.ds(first, rows), source, keep).start()
-
-                pl.when(at.c == core)(functools.partial(begin, True))
-                pl.when(at.c != core)(functools.partial(begin, False))
-
-    def move(self, y, rows, source, keep):
+        for z in ORDER:
+            for y in (0, 1):
+                for core in (0, 1):
+
+                    def begin(keep, y=y, z=z, b=2 * y + core):
+                        for source, first, rows in self.part(b, z):
+                            self.move(y, z, pl.ds(first, rows), source, keep).start()
+
+                    pl.when(at.c == core)(functools.partial(begin, True))
+                    pl.when(at.c != core)(functools.partial(begin, False))
+
+    def move(self, y, z, rows, source, keep):
         if keep:
-            return pltpu.make_async_copy(source, self.own.at[y, rows], self.own_sem.at[y])
+            return pltpu.make_async_copy(source, self.own.at[y, rows], self.own_sem.at[y, z])
         return remote(
             source,
             self.got.at[y, rows],
-            self.core_send.at[y],
-            self.core_recv.at[y],
+            self.core_send.at[y, z],
+            self.core_recv.at[y, z],
             self.at.sibling,
         )
 
-    def arrive(self):
+    def whole_move(self, y, z, keep):
+        rows = pl.ds(2 * z * BLOCK, 2 * BLOCK)
+        return self.move(y, z, rows, self.got.at[y, rows], keep)
+
+    def arrive(self, z):
         for y in (0, 1):
-            self.move(y, pl.ds(0, D), self.got.at[y], True).wait()
-            self.move(y, pl.ds(0, D), self.got.at[y], False).wait_recv()
+            self.whole_move(y, z, True).wait()
+            self.whole_move(y, z, False).wait_recv()
 
     @staticmethod
     def rows_of(r, start, size):
@@ -659,8 +673,9 @@
             device = at.across_y
         return remote(source, target, self.far_send.at[route], self.far_recv.at[route, z], device)
 
-    def near_stage(self, begin, end):
+    def near_stage(self, z):
         at, cut, own, got = self.at, self.cut, self.own, self.got
+        self.arrive(z)
 
         def step(i, carry):
             for y, start, size, route in (
@@ -671,24 +686,19 @@
                 self.near_copy(route, i).start()
             return carry
 
-        lax.fori_loop(begin, end, step, 0)
-
-    def far_stage(self, begin, end):
+        lax.fori_loop(2 * z, 2 * z + 2, step, 0)
+
+    def far_stage(self, z):
         at, cut, own, got = self.at, self.cut, self.own, self.got
-
-        def step(z, carry):
-            r, i = 2 * z + at.other_x, 2 * z + self.other_y
-            for y, start, size, route, index, first in (
-                (at.y, r * BLOCK, cut, 0, r, 0),
-                (self.other_y, (2 * z + at.x) * BLOCK + cut, BLOCK - cut, 1, i, cut),
-            ):
-                self.near_copy(route, index).wait_recv()
-                sources = [(own, (y,), start), (got, (y,), start), (self.near, (index,), first)]
-                self.add((own, (y,), start), sources, size)
-                self.far_copy(route, z).start()
-            return carry
-
-        lax.fori_loop(begin, end, step, 0)
+        r, i = 2 * z + at.other_x, 2 * z + self.other_y
+        for y, start, size, route, index, first in (
+            (at.y, r * BLOCK, cut, 0, r, 0),
+            (self.other_y, (2 * z + at.x) * BLOCK + cut, BLOCK - cut, 1, i, cut),
+        ):
+            self.near_copy(route, index).wait_recv()
+            sources = [(own, (y,), start), (got, (y,), start), (self.near, (index,), first)]
+            self.add((own, (y,), start), sources, size)
+            self.far_copy(route, z).start()
 
     def line_copy(self, way, z):
         source = self.own.at[self.at.y, self.rows_of(2 * z + self.at.x, 0, BLOCK)]
@@ -737,10 +747,9 @@
         pl.when(jnp.logical_not(ahead))(lambda: self.total(z, target, ()))
         self.line_copy(way, z).start()
 
-    def line_stage(self, step):
-        z = LINE - 1 - step
+    def line_stage(self, z):
         pl.when(self.at.z < z)(functools.partial(self.pass_on, 0, z))
-        pl.when(self.at.z > step)(functools.partial(self.pass_on, 1, step))
+        pl.when(self.at.z > z)(functools.partial(self.pass_on, 1, z))
 
     def last(self):
         at = self.at
@@ -757,7 +766,8 @@
     def finish(self):
         at, cut = self.at, self.cut
         for y in (0, 1):
-            self.move(y, pl.ds(0, D), self.got.at[y], False).wait_send()
+            for z in range(LINE):
+                self.whole_move(y, z, False).wait_send()
         for route, size in ((0, cut), (1, BLOCK - cut)):
             rows = self.own.at[0, pl.ds(0, 2 * LINE * size)]
             sems = self.near_send.at[route], self.near_recv.at[route, 0]
@@ -765,10 +775,38 @@
             rows = self.own.at[0, pl.ds(0, LINE * size)]
             sems = self.far_send.at[route], self.far_recv.at[route, 0]
             remote(rows, rows, *sems, at.sibling).wait_send()
-        for step in range(LINE - 1):
-            z = LINE - 1 - step
+        for z in range(LINE):
             pl.when(at.z < z)(lambda: self.line_copy(0, z).wait_send())
-            pl.when(at.z > step)(lambda: self.line_copy(1, step).wait_send())
+            pl.when(at.z > z)(lambda: self.line_copy(1, z).wait_send())
+
+
+class Share:
+    def __init__(self, at, sums, shares, scratch):
+        self.at, self.sums, self.shares = at, sums, shares
+        self.stage, self.send, self.recv = scratch
+
+    def copy(self, i):
+        at = self.at
+        b = (at.b + i) % 4
+        target = self.shares.at[at.b]
+        return remote(self.stage.at[b], target, self.send.at[i], self.recv.at[i], (at.r, b))
+
+    def start(self):
+        for j in range(4):
+            self.stage[j, :OWN, :] = self.sums[OWN * j : OWN * (j + 1), :]
+            self.stage[j, OWN:, :] = jnp.zeros((ROUNDED - OWN, D), F32)
+        for i in range(1, 4):
+            self.copy(i).start()
+        self.shares[self.at.b] = self.stage[self.at.b]
+
+    def finish(self):
+        for i in range(1, 4):
+            self.copy(i).wait()
+
+
+def share_scratch():
+    dma = pltpu.SemaphoreType.DMA
+    return [pltpu.VMEM((4, ROUNDED, D), F32), dma((4,)), dma((4,))]
 
 
 def collect_scratch():
@@ -779,9 +817,9 @@
         pltpu.VMEM((2 * LINE, BLOCK, D), BF16),
         pltpu.VMEM((LINE, BLOCK, D), BF16),
         pltpu.VMEM((2, LINE - 1, BLOCK, D), BF16),
-        dma((2,)),
-        dma((2,)),
-        dma((2,)),
+        dma((2, LINE)),
+        dma((2, LINE)),
+        dma((2, LINE)),
         dma((2,)),
         dma((2, 2 * LINE)),
         dma((2,)),
@@ -806,7 +844,6 @@
     totals,
     quarters,
     slots_block,
-    piece,
     pieces,
     tall,
     totals_got,
@@ -817,15 +854,28 @@
     slot_line_send,
     slot_line_recv,
     slot_sem,
+    piece_sems,
+    sums,
     *rest,
 ):
     at = Place()
     at.greet()
-    own = rest[0]
+    own = rest[3]
+    share = Share(at, sums, out, rest[:3])
     of_first = Collect(
-        at, lambda b: [((query, key, value, output)[b], 0, D)], out, rest[:5], rest[5:], SPLIT[0]
+        at,
+        lambda b, z: [
+            (
+                (query, key, value, output)[b].at[pl.ds(2 * z * BLOCK, 2 * BLOCK)],
+                2 * z * BLOCK,
+                2 * BLOCK,
+            )
+        ],
+        sums,
+        rest[3:8],
+        rest[8:],
+        SPLIT[0],
     )
-    of_first.start()
 
     def band_copy(i):
         b = (at.b + i) % 4
@@ -846,9 +896,6 @@
         columns = pl.ds(pl.multiple_of(b * 2 * D + start, 128), size)
         return slots.at[pl.ds(pl.multiple_of(r * 16, 16), 16), columns]
 
-    def in_pieces(r, b, start, size):
-        return pieces.at[4 * r + b, pl.ds(start, size)]
-
     def sems(index):
         return slot_line_send.at[index], slot_line_recv.at[index], slot_sem.at[index]
 
@@ -856,7 +903,10 @@
         return own.at[0, pl.ds(0, rows), pl.ds(0, width)]
 
     of_slots = Spread(at, in_slots, slots_block, 2 * D, 16, D, bytes_of, sems(0))
-    of_piece = Spread(at, in_pieces, piece, PADDED, 128, 16, bytes_of, sems(1))
+
+    def piece_copy(place):
+        mine = pieces.at[at.me]
+        return remote(mine, mine, piece_sems.at[0], piece_sems.at[1], place)
 
     def share_slots():
         mine = pl.ds(pl.multiple_of(at.b * 2 * D, 128), 2 * D)
@@ -873,11 +923,12 @@
         grad = dot(mods_weights[...], slots[...], NT)
         sigmoid = 1.0 / (1.0 + jnp.exp(-condition[...]))
         grad = grad * (sigmoid * (1.0 + condition[...] * (1.0 - sigmoid)))
-        piece[...] = grad.astype(BF16)
-        of_piece.open()
+        pieces[at.me] = grad.astype(BF16)
+        at.others(lambda _, place: piece_copy(place).start())
 
     def condition_arrives():
-        of_piece.arrive()
+        others = pieces.at[pl.ds(0, DEVICES - 1)]
+        remote(others, others, piece_sems.at[0], piece_sems.at[1], at.sibling).wait()
         compact(tall, pieces, 0)
         grad_condition[...] = jnp.transpose(tall[...]).astype(BF16)
 
@@ -887,7 +938,7 @@
     def far_line():
         return (at.r + 4 - 8 * (at.z // 2), at.b)
 
-    partners = (at.sibling, at.across_x, at.across_y, near_line(), far_line())
+    partners = (at.sibling, near_line(), far_line(), at.across_x, at.across_y)
 
     def totals_copy(step):
         return remote(
@@ -908,36 +959,46 @@
     for i in range(1, 4):
         band_copy(i).start()
     totals_copy(0).start()
+    of_first.start()
     share_slots()
-    of_first.arrive()
-    of_first.near_stage(0, 4)
+    of_first.near_stage(3)
     totals_step(0)
-    of_slots.along_line()
-    of_first.near_stage(4, 8)
-    of_slots.around_square()
+    of_slots.along_line((1,))
+    of_first.near_stage(0)
+    of_slots.along_line((2,))
+    of_slots.around_square((0,))
+    of_first.far_stage(3)
+    of_first.near_stage(2)
+    of_slots.along_line((3,))
+    of_slots.around_square((1,))
+    of_first.far_stage(0)
     totals_step(1)
-    of_slots.close_square()
-    of_first.far_stage(0, 2)
+    of_first.near_stage(1)
+    of_slots.around_square((2,))
+    of_slots.close_square((0,))
+    of_slots.around_square((3,))
+    of_first.line_stage(3)
+    of_slots.close_square((1,))
+    totals_step(2)
+    of_first.far_stage(2)
+    of_slots.close_square((2, 3))
+    of_first.line_stage(0)
     condition_back()
-    of_first.far_stage(2, 4)
-    totals_step(2)
-    of_piece.along_line()
-    of_first.line_stage(0)
-    of_piece.around_square()
+    of_first.far_stage(1)
     totals_step(3)
+    of_first.line_stage(2)
     of_first.line_stage(1)
-    of_piece.close_square()
-    of_first.line_stage(2)
+    of_first.last()
+    share.start()
+    condition_arrives()
     totals_step(4)
-    condition_arrives()
-    of_first.last()
     of_first.finish()
+    share.finish()
     for i in range(1, 4):
         band_copy(i).wait_send()
     for step in range(len(partners)):
         totals_copy(step).wait_send()
     of_slots.finish()
-    of_piece.finish()
 
 
 def scatter_sums(matrices, slots_own, mods_weights, condition, totals_own):
@@ -952,7 +1013,7 @@
         in_specs=[anywhere] * 4 + [inside] * 4,
         out_specs=[inside] * 4,
         out_shape=[
-            jax.ShapeDtypeStruct((BLOCK, D), F32),
+            jax.ShapeDtypeStruct((4, ROUNDED, D), F32),
             jax.ShapeDtypeStruct((128, 8 * D), BF16),
             jax.ShapeDtypeStruct((128, D), BF16),
             jax.ShapeDtypeStruct((steps, *totals_own.shape), F32),
@@ -960,7 +1021,6 @@
         scratch_shapes=[
             pltpu.VMEM((4, 16, 2 * D), BF16),
             pltpu.VMEM((16, 2 * D), BF16),
-            pltpu.VMEM((PADDED, 128), BF16),
             pltpu.VMEM((DEVICES, PADDED, 128), BF16),
             pltpu.VMEM((D, 128), F32),
             pltpu.VMEM((steps, *totals_own.shape), F32),
@@ -968,7 +1028,10 @@
             dma((4,)),
             dma((steps,)),
             dma((steps,)),
-            *spread_sems(2),
+            *spread_sems(1),
+            dma((2,)),
+            pltpu.VMEM((BLOCK, D), F32),
+            *share_scratch(),
             *collect_scratch(),
         ],
         compiler_params=pltpu.CompilerParams(
@@ -999,11 +1062,11 @@
             of_up.open()
 
         at_step(head, 0, begin)
-        at_step(head, 3, lambda: of_up.along_line((1,)))
-        at_step(head, 5, lambda: of_up.along_line((2,)))
-        at_step(head, 7, lambda: of_up.along_line((3,)))
-        at_step(head, 10, of_up.around_square)
-        at_step(head, 14, of_up.close_square)
+        for step in (1, 2, 3):
+            at_step(head, 1 + 2 * step, lambda: of_up.along_line((step,)))
+        for step in range(4):
+            at_step(head, 4 + 2 * step, lambda: of_up.around_square((step,)))
+            at_step(head, 8 + 2 * step, lambda: of_up.close_square((step,)))
     else:
         out_ref, log_ref = rest
     attend_head(head, apart, q_ref, k_ref, v_ref, out_ref, log_ref, min(512, q_ref.shape[0]))
@@ -1019,25 +1082,27 @@
 def attend_back_kernel(apart, q_ref, k_ref, v_ref, grad_ref, log_ref, *rest, travels):
     head = pl.program_id(0)
     if travels:
-        up_grad, dq_ref, dk_ref, dv_ref, up_sum, *rest = rest
+        up_grad, dq_ref, dk_ref, dv_ref, shares, sums, *rest = rest
         at = Place()
-
-        def part(b):
-            return [(up_grad.at[:, pl.ds(b * D, D)], 0, D)]
-
-        of_up = Collect(at, part, up_sum, rest[:5], rest[5:], SPLIT[1])
+        share = Share(at, sums, rest[3], rest[:3])
+
+        def part(b, z):
+            rows = pl.ds(2 * z * BLOCK, 2 * BLOCK)
+            return [(up_grad.at[rows, pl.ds(b * D, D)], 2 * z * BLOCK, 2 * BLOCK)]
+
+        of_up = Collect(at, part, sums, rest[4:9], rest[9:], SPLIT[1])
 
         def begin():
             at.greet()
             of_up.start()
 
         at_step(head, 0, begin)
-        at_step(head, 1, of_up.arrive)
-        for step in range(4):
-            at_step(head, 1 + step, lambda: of_up.near_stage(2 * step, 2 * step + 2))
-            at_step(head, 6 + step, lambda: of_up.far_stage(step, step + 1))
-        for step in range(3):
-            at_step(head, 11 + step, lambda: of_up.line_stage(step))
+        for step, z in ((2, 3), (3, 0), (6, 2), (8, 1)):
+            at_step(head, step, lambda: of_up.near_stage(z))
+        for step, z in ((6, 3), (8, 0), (11, 2), (13, 1)):
+            at_step(head, step, lambda: of_up.far_stage(z))
+        for step, z in ((10, 3), (12, 0), (14, 2)):
+            at_step(head, step, lambda: of_up.line_stage(z))
     else:
         dq_ref, dk_ref, dv_ref = rest
     attend_back_head(
@@ -1046,8 +1111,12 @@
     if travels:
 
         def end():
+            of_up.line_stage(1)
             of_up.last()
+            share.start()
             of_up.finish()
+            share.finish()
+            shares[...] = rest[3][...]
 
         at_step(head, HEADS - 1, end)
 
@@ -1098,20 +1167,157 @@
         ]
         + [anywhere] * travels,
         out_specs=[whole_block((q_len, D)), whole_block((k_len, D)), whole_block((k_len, D))]
-        + [whole_block((BLOCK, D))] * travels,
+        + [whole_block((4, ROUNDED, D))] * travels,
         out_shape=[
             jax.ShapeDtypeStruct((q_len, D), BF16),
             jax.ShapeDtypeStruct((k_len, D), BF16),
             jax.ShapeDtypeStruct((k_len, D), BF16),
         ]
-        + [jax.ShapeDtypeStruct((BLOCK, D), F32)] * travels,
-        scratch_shapes=collect_scratch() if travels else [],
+        + [jax.ShapeDtypeStruct((4, ROUNDED, D), F32)] * travels,
+        scratch_shapes=[
+            pltpu.VMEM((BLOCK, D), F32),
+            *share_scratch(),
+            pltpu.VMEM((4, ROUNDED, D), F32),
+            *collect_scratch(),
+        ]
+        if travels
+        else [],
         compiler_params=pltpu.CompilerParams(
             vmem_limit_bytes=61 << 20,
             **(dict(collective_id=3, has_side_effects=True) if travels else {}),
         ),
         name="attend_rows_back",
     )(apart, queries, keys, values, grads, log_total, *((up_grad,) if travels else ()))
+
+
+def mlp_kernel(normed, up, bias, down, active, slope, branch):
+    tile = pl.program_id(0)
+    values = dot(normed[...], up[...], NN) + bias[...]
+    square = values * values
+    curve = jnp.tanh(GELU_ROOT * values * (1.0 + GELU_CUBE * square))
+    half = 0.5 * (1.0 + curve)
+    acting = (values * half).astype(BF16)
+    active[...] = acting
+    steep = values * (GELU_ROOT + 3.0 * GELU_ROOT * GELU_CUBE * square)
+    slope[...] = (half + half * (1.0 - curve) * steep).astype(BF16)
+    part = dot(acting, down[...], NN)
+
+    @pl.when(tile == 0)
+    def _():
+        branch[...] = part
+
+    @pl.when(tile > 0)
+    def _():
+        branch[...] += part
+
+
+def mlp(normed, up, bias, down):
+    rows, tile = normed.shape[0], 768
+    by_tile = pl.BlockSpec((rows, tile), lambda i: (0, i))
+    return pl.pallas_call(
+        mlp_kernel,
+        grid=(FF // tile,),
+        in_specs=[
+            whole_block((rows, D)),
+            pl.BlockSpec((D, tile), lambda i: (0, i)),
+            pl.BlockSpec((1, tile), lambda i: (0, i)),
+            pl.BlockSpec((tile, D), lambda i: (i, 0)),
+        ],
+        out_specs=[by_tile, by_tile, whole_block((rows, D))],
+        out_shape=[
+            jax.ShapeDtypeStruct((rows, FF), BF16),
+            jax.ShapeDtypeStruct((rows, FF), BF16),
+            jax.ShapeDtypeStruct((rows, D), F32),
+        ],
+        compiler_params=pltpu.CompilerParams(vmem_limit_bytes=56 << 20),
+        name="mlp",
+    )(normed, up, bias, down)
+
+
+def mlp_back_kernel(
+    grad,
+    normed,
+    slope,
+    down,
+    up,
+    down_grad,
+    grad_normed,
+    up_grad,
+    bias_grad,
+    down_sum,
+    turned,
+    *rest,
+):
+    tile = pl.program_id(0)
+    at = Place()
+
+    def part(b, z):
+        return [
+            (down_grad.at[pl.ds((4 * r + b) * BLOCK, BLOCK)], r * BLOCK, BLOCK)
+            for r in (2 * z, 2 * z + 1)
+        ]
+
+    of_down = Collect(at, part, down_sum, rest[:5], rest[5:], SPLIT[0])
+
+    def begin():
+        at.greet()
+        of_down.start()
+        turned[...] = jnp.transpose(normed[...])
+        grad_normed[...] = jnp.zeros_like(grad_normed)
+
+    at_step(tile, 0, begin)
+    for step, z in ((1, 3), (1, 0), (3, 2), (4, 1)):
+        at_step(tile, step, lambda: of_down.near_stage(z))
+    for step, z in ((3, 3), (4, 0), (6, 2), (7, 1)):
+        at_step(tile, step, lambda: of_down.far_stage(z))
+    for step, z in ((6, 3), (7, 0), (8, 2)):
+        at_step(tile, step, lambda: of_down.line_stage(z))
+
+    grad_active = dot(grad[...], down[...], NT)
+    grad_up = (grad_active * slope[...].astype(F32)).astype(BF16)
+    bias_grad[...] = jnp.sum(grad_up.astype(F32), axis=0, keepdims=True)
+    up_grad[...] = dot(turned[...], grad_up, NN).astype(BF16)
+    grad_normed[...] += dot(grad_up, up[...], NT)
+
+    def end():
+        of_down.line_stage(1)
+        of_down.last()
+        of_down.finish()
+
+    at_step(tile, pl.num_programs(0) - 1, end)
+
+
+def mlp_back(grad, normed, slope, down, up, down_grad):
+    rows, tile = grad.shape[0], 512
+    return pl.pallas_call(
+        mlp_back_kernel,
+        grid=(FF // tile,),
+        in_specs=[
+            whole_block((rows, D)),
+            whole_block((rows, D)),
+            pl.BlockSpec((rows, tile), lambda i: (0, i)),
+            pl.BlockSpec((tile, D), lambda i: (i, 0)),
+            pl.BlockSpec((D, tile), lambda i: (0, i)),
+            pl.BlockSpec(memory_space=pl.ANY),
+        ],
+        out_specs=[
+            whole_block((rows, D)),
+            pl.BlockSpec((D, tile), lambda i: (0, i)),
+            pl.BlockSpec((1, tile), lambda i: (0, i)),
+            whole_block((BLOCK, D)),
+        ],
+        out_shape=[
+            jax.ShapeDtypeStruct((rows, D), F32),
+            jax.ShapeDtypeStruct((D, FF), BF16),
+            jax.ShapeDtypeStruct((1, FF), F32),
+            jax.ShapeDtypeStruct((BLOCK, D), F32),
+        ],
+        scratch_shapes=[pltpu.VMEM((D, rows), BF16)] + collect_scratch(),
+        compiler_params=pltpu.CompilerParams(
+            vmem_limit_bytes=61 << 20, collective_id=4, has_side_effects=True
+        ),
+        name="mlp_back",
+    )(grad, normed, slope, down, up, down_grad)
 
 
 def matmul(operand, weights):
@@ -1300,9 +1506,10 @@
     device = at_row * n_band + at_band
     if tuned:
         padded = lambda array: jnp.pad(array, ((0, PADDED - OWN), (0, 0)))
-        regroup = functools.partial(
-            lax.all_to_all, axis_name="band", split_axis=1, concat_axis=0, tiled=True
-        )
+        quarters = [first_group.reshape(-1, 4, D), up_group.reshape(-1, 4, D)]
+        quarters = lax.all_to_all(
+            jnp.concatenate(quarters, axis=2), "band", split_axis=1, concat_axis=0, tiled=True
+        )[:, 0]
         own_times = timesteps.reshape(-1)
         codes = (labels + 1024 * image_counts[:, None]).reshape(-1, 1)
         own_codes = jnp.broadcast_to(codes, (rows_here * SLOTS, 128))
@@ -1318,7 +1525,7 @@
             codes,
             given,
         ) = gather_weights(
-            regroup(first_group.reshape(-1, 4, D))[:, 0],
+            quarters[:, :D],
             padded(time_out_low),
             padded(mods_low),
             time_features(own_times).astype(BF16),
@@ -1330,7 +1537,7 @@
             given.transpose(0, 2, 1),
         )
         given = given.T
-        up_own = regroup(up_group.reshape(-1, 4, D))[:, 0]
+        up_own = quarters[:, D:]
         down_own, first_all = lax.optimization_barrier((down_low, first_all))
         down_all = lax.all_gather(down_own, AXES, axis=0, tiled=True)
         weight_q, weight_k, weight_v, weight_o = first_all
@@ -1419,9 +1626,14 @@
     branch_one = matmul(attended, weight_o) + biases[11]
     hidden_one = hidden_zero + gate_one * branch_one
     normed_two = modulate(hidden_one, shift_two, scale_two).astype(BF16)
-    upward = matmul(normed_two, up_all) + biases[12:16].reshape(-1)
-    active = jax.nn.gelu(upward, approximate=True).astype(BF16)
-    branch_two = matmul(active, down_all) + biases[16]
+    up_bias = biases[12:16].reshape(-1)
+    if tuned:
+        active, slope, branch_two = mlp(flat(normed_two), up_all, up_bias[None], down_all)
+        active, branch_two = deep(active), deep(branch_two) + biases[16]
+    else:
+        upward = matmul(normed_two, up_all) + up_bias
+        active = jax.nn.gelu(upward, approximate=True).astype(BF16)
+        branch_two = matmul(active, down_all) + biases[16]
     hidden_two = hidden_one + gate_two * branch_two
     normed_out = modulate(hidden_two, final_shift, final_scale).astype(BF16)
     output = matmul(normed_out, head_matrix) + head_low[D].astype(F32)
@@ -1437,14 +1649,27 @@
     grad_gate_two = seg_sum(grad_two * branch_two)
     grad_branch_two = (gate_two * grad_two).astype(BF16)
     down_grad = outer_sum(active, grad_branch_two)
-    grad_active = matmul_back(grad_branch_two, down_all)
-    grad_upward = jax.vjp(lambda at: jax.nn.gelu(at, approximate=True), upward)[1](grad_active)[
-        0
-    ].astype(BF16)
-    up_grad = outer_sum(normed_two, grad_upward)
+    if tuned:
+        grad_normed_two, up_grad, up_bias_grad, down_sum = mlp_back(
+            flat(grad_branch_two),
+            flat(normed_two),
+            slope,
+            down_all,
+            up_all,
+            down_grad.astype(BF16),
+        )
+        grad_normed_two, up_bias_grad = deep(grad_normed_two), up_bias_grad[0]
+    else:
+        grad_active = matmul_back(grad_branch_two, down_all)
+        grad_upward = jax.vjp(lambda at: jax.nn.gelu(at, approximate=True), upward)[1](
+            grad_active
+        )[0].astype(BF16)
+        up_grad = outer_sum(normed_two, grad_upward)
+        up_bias_grad = column_sum(grad_upward)
+        grad_normed_two = matmul_back(grad_upward, up_all)
     grad_one_part, grad_shift_two, grad_scale_two = jax.vjp(
         modulate, hidden_one, shift_two, scale_two
-    )[1](matmul_back(grad_upward, up_all))
+    )[1](grad_normed_two)
     grad_one = grad_two + grad_one_part
     grad_gate_one = seg_sum(grad_one * branch_one)
     grad_branch_one = (gate_one * grad_one).astype(BF16)
@@ -1452,7 +1677,7 @@
     grad_attended = flat(matmul_back(grad_branch_one, weight_o).astype(BF16))
     if tuned:
         grad_query, grad_key, grad_value, up_sum = attend_back(
-            apart, queries, keys, values, grad_attended, log_total, up_grad.astype(BF16)
+            apart, queries, keys, values, grad_attended, log_total, up_grad
         )
     else:
         grad_query, grad_key, grad_value = attend_back(
@@ -1494,7 +1719,7 @@
             column_sum(grad_query)[None],
             column_sum(grad_value)[None],
             column_sum(grad_branch_one)[None],
-            column_sum(grad_upward).reshape(FF // D, D),
+            up_bias_grad.reshape(FF // D, D),
             column_sum(grad_branch_two)[None],
             patch_grad,
             outer_sum(grad_out, normed_out),
@@ -1506,17 +1731,8 @@
         slots_own = jnp.where(
             (jnp.arange(4 * SLOTS) // SLOTS == at_band)[:, None], jnp.tile(slot_grads, (4, 1)), 0
         ).astype(BF16)
-        regroup_back = functools.partial(
-            lax.all_to_all, axis_name="band", split_axis=0, concat_axis=1, tiled=True
-        )
-        up_squares = jnp.sum(up_sum * up_sum)
-        up_grad = regroup_back(up_sum[:, None]).reshape(-1, FF)
         matrices = (q_grad, k_grad, v_grad, output_grad)
-        down_grad = lax.psum_scatter(
-            down_grad.astype(BF16), AXES, scatter_dimension=0, tiled=True
-        )
-        slots_own, down_grad = lax.optimization_barrier((slots_own, down_grad))
-        down_grad = down_grad.astype(F32)
+        down_grad = down_sum
         sums, slot_grads, grad_condition_all, totals = scatter_sums(
             [array.astype(BF16) for array in matrices],
             slots_own,
@@ -1525,8 +1741,10 @@
             jnp.pad(totals, ((0, -totals.shape[0] % 8), (0, 0))),
         )
         totals = totals[-1]
-        first_grad = regroup_back(sums[:, None]).reshape(-1, 4 * D)
-        local_squares = jnp.sum(sums * sums) + up_squares + jnp.sum(down_grad * down_grad)
+        first_grad, up_grad = (
+            shares[:, :OWN].transpose(1, 0, 2).reshape(OWN, 4 * D) for shares in (sums, up_sum)
+        )
+        local_squares = sum(jnp.sum(array * array) for array in (first_grad, up_grad, down_grad))
         grad_condition = own_columns(grad_condition_all)
     else:
         slot_grads = lax.all_gather(slot_grads, AXES, axis=0, tiled=True)

time: 862 us -> 797 us (0.925)
  matrix products: 224 us -> 102 us
  Pallas kernels: 453 us -> 522 us
    pallas_call x0 -> x2, Pallas kernels: none -> 123 us  [the longest x1 83.9 us: mlp_back(): pl.pallas_call(mlp_back_kernel, grid=(FF // tile,), in_specs=[whole_block...]
    dot_general x8 -> x6, matrix products: 79.6 us -> 29.9 us  [matmul_back(): jnp.einsum('...j,ij->...i', gradient, weights, preferred_element_type=F32)]
    dot_general x8 -> x6, matrix products: 71.5 us -> 27.2 us  [matmul(): jnp.einsum('...i,ij->...j', operand, weights, preferred_element_type=F32)]
    dot_general x12 -> x11, matrix products: 73.3 us -> 45.2 us  [outer_sum(): jnp.einsum('ni,nj->ij', operand.reshape(-1, operand.shape[-1]), gradient....]
    pallas_call x1, Pallas kernels: 128 us -> 101 us  [attend_back(): pl.pallas_call(functools.partial(attend_back_kernel, travels=travels), gr...]
    pallas_call x1, Pallas kernels: 134 us -> 109 us  [scatter_sums(): pl.pallas_call(scatter_kernel, in_specs=[anywhere] * 4 + [inside] * 4, ou...]
    all_to_all x4 -> x1, starting transfers between devices: 17.3 us -> 4.24 us  [body(): lax.all_to_all(jnp.concatenate(quarters, axis=2), 'band', split_axis=1, c...]
  transfers between devices with their start and end apart: 7 -> 3, of which waited for: 3 -> 1; matrix products, arithmetic and copies ran while one was open for 21% -> 7% of each run, Pallas kernels for 25% -> 11%
where the time goes in v2:
time: 797 us; the launch traced here: 792 us
  Pallas kernels  522 us (65%)
  matrix products  102 us (13%)
  other arithmetic  88.5 us (11%)
  local copies, waits for them, and re-layouts  28.3 us (4%)
  between operations  27.3 us (3%)
  starting transfers between devices  16 us (2%)
    pallas_call x1, Pallas kernels, scatter_sums(): pl.pallas_call(scatter_kernel, in_specs=[anywhere] * 4 + [inside] * 4, ou...  109 us
    pallas_call x1, Pallas kernels, gather_weights(): pl.pallas_call(gather_kernel, in_specs=[anywhere] * 3 + [inside] * 7, out...  101 us
    pallas_call x1, Pallas kernels, attend_back(): pl.pallas_call(functools.partial(attend_back_kernel, travels=travels), gr...  101 us
    pallas_call x1, Pallas kernels, attend(): pl.pallas_call(functools.partial(attend_kernel, travels=travels), grid=(H...  87.7 us
    pallas_call x1, Pallas kernels, mlp_back(): pl.pallas_call(mlp_back_kernel, grid=(FF // tile,), in_specs=[whole_block...  83.9 us
    dot_general x11, matrix products, outer_sum(): jnp.einsum('ni,nj->ij', operand.reshape(-1, operand.shape[-1]), gradient....  45.2 us
    pallas_call x1, Pallas kernels, mlp(): pl.pallas_call(mlp_kernel, grid=(FF // tile,), in_specs=[whole_block((row...  39.1 us
    dot_general x6, matrix products, matmul_back(): jnp.einsum('...j,ij->...i', gradient, weights, preferred_element_type=F32)  29.9 us
  transfers between devices with their start and end apart: 3, of which 1 were waited for; matrix products, arithmetic and copies ran while one was open for 7% of the time, Pallas kernels for 11%

profile of v2, /device:TPU:0, one launch (start us, length us, event | category | flops | bytes accessed | tf_op | source)
XLA Modules:
  0.0 792.3 jit_solution(5806830797292155715)
XLA Ops:
  19.5 7.8 all-to-all-done
  29.5 101.4 %gather_weights.1 = (bf16[4,1152,1152]{2,1,0:T(8,128)(2,1)S(1)}, f32[8,9216]{1,0:T(8,128)S(1)}, f32[128,1152]{1,0:T(8,128)S(1)}, f32[128,1152]{1,0:T(8,128)S(1)}...) custom-call(bf16[144,1152]{1,0:T(8,128)(2,1)S(1)} %get-tuple-element, ...), custom_call_target="tpu_custom_call" | custom-call | tf_op jit(solution)/shard_map/gather_weights/pallas_call | solution.py:541
  157.6 4.9 convolution_convert_fusion.6.k_ref
  162.5 4.8 add_convert_fusion.3
  172.0 87.7 %attend_rows.1 = (bf16[1024,1152]{1,0:T(8,128)(2,1)}, f32[16,1024]{1,0:T(8,128)}, bf16[1152,4608]{1,0:T(8,128)(2,1)}) custom-call(f32[4,1024]{1,0:T(4,128)} %compare_select_fusion.apart, bf16[1024,1152]{1,0:T(8,128)(2,1)} %bitcast.248, bf16[1024,1152]{1,0:T(8,128)(2,1)} %convolution_convert_fusion.6.k_ref, bf16[1024,1152]{1,0:T(8,128)(2,1)} %bitcast.246, ...), custom_call_target="tpu_custom_call" | custom-call | tf_op jit(solution)/shard_map/attend_rows/pallas_call | solution.py:1128
  259.7 8.1 %fusion.81 = (f32[4,256]{1,0:T(4,128)S(1)}, f32[4,256,1152]{2,1,0:T(8,128)S(1)}, f32[4,256,1152]{2,1,0:T(8,128)}) fusion(f32[4,256,1152]{2,1,0:T(8,128)S(1)} %get-tuple-element.174, f32[4,1152]{1,0:T(4,128)S(1)} %get-tuple-element.164, f32[1152]{0:T(1024)S(1)} %get-tuple-element.95, bf16[4,256,1152]{2,1,0:T(8,128)(2,1)} %bitcast.276, ...), kind=kOutput, calls=%fused_computation.279 | convolution fusion | flops 2722626560 | bytes 19196416 | tf_op jit(solution)/shard_map/...i,ij->...j/dot_general | solution.py:1324
  273.5 39.1 %mlp.1 = (bf16[1024,4608]{1,0:T(8,128)(2,1)}, bf16[1024,4608]{1,0:T(8,128)(2,1)}, f32[1024,1152]{1,0:T(8,128)}) custom-call(bf16[1024,1152]{1,0:T(8,128)(2,1)} %bitcast.238, bf16[1152,4608]{1,0:T(8,128)(2,1)} %get-tuple-element.62.up, f32[1,4608]{1,0:T(1,128)} %bitcast.263, bf16[4608,1152]{1,0:T(8,128)(2,1)} %all-gather.2.cloned.1.call-done.down), custom_call_target="tpu_custom_call" | custom-call | tf_op jit(solution)/shard_map/mlp/pallas_call | solution.py:1217
  325.4 19.1 %convolution_convert_fusion.down_grad = bf16[4608,1152]{1,0:T(8,128)(2,1)} fusion(bf16[1024,4608]{1,0:T(8,128)(2,1)} %get-tuple-element.67, bf16[1024,1152]{1,0:T(8,128)(2,1)S(1)} %bitcast.244), kind=kOutput, calls=%fused_computation | convolution fusion | flops 10876944384 | bytes 22413312 | tf_op jit(solution)/shard_map/ni,nj->ij/dot_general | solution.py:1332
  344.5 83.9 %mlp_back.1 = (f32[1024,1152]{1,0:T(8,128)}, bf16[1152,4608]{1,0:T(8,128)(2,1)}, f32[1,4608]{1,0:T(1,128)}, f32[144,1152]{1,0:T(8,128)}) custom-call(bf16[1024,1152]{1,0:T(8,128)(2,1)} %bitcast.245, bf16[1024,1152]{1,0:T(8,128)(2,1)} %bitcast.239, bf16[1024,4608]{1,0:T(8,128)(2,1)} %get-tuple-element.66.slope, ...), custom_call_target="tpu_custom_call" | custom-call | tf_op jit(solution)/shard_map/mlp_back/pallas_call | solution.py:1292
  428.5 4.7 multiply_reduce_fusion.4
  442.2 6.5 convolution_convert_fusion.5
  448.7 101.1 %attend_rows_back.1 = (bf16[1024,1152]{1,0:T(8,128)(2,1)}, bf16[1024,1152]{1,0:T(8,128)(2,1)}, bf16[1024,1152]{1,0:T(8,128)(2,1)}, f32[4,40,1152]{2,1,0:T(8,128)}) custom-call(f32[4,1024]{1,0:T(4,128)} %compare_select_fusion.apart, bf16[1024,1152]{1,0:T(8,128)(2,1)} %bitcast.249, bf16[1024,1152]{1,0:T(8,128)(2,1)} %convolution_convert_fusion.6.k_ref, ...), custom_call_target="tpu_custom_call" | custom-call | tf_op jit(solution)/shard_map/attend_rows_back/pallas_call | solution.py:1157
  549.9 8.3 %fusion.12 = f32[1024,1152]{1,0:T(8,128)} fusion(bf16[1024,1152]{1,0:T(8,128)(2,1)} %get-tuple-element.71, bf16[4,1152,1152]{2,1,0:T(8,128)(2,1)} %copy-done.1), kind=kOutput, calls=%fused_computation.63 | convolution fusion | flops 2717908992 | bytes 9732096 | tf_op jit(solution)/shard_map/...j,ij->...i/dot_general | solution.py:1328
  559.8 4.8 convolution_convert_fusion.2.value
  564.6 5.3 fusion.8
  569.9 4.8 convolution_convert_fusion.3.key
  574.7 4.8 convolution_convert_fusion.4.query
  580.8 7.7 bitcast_multiply_fusion
  588.5 4.8 multiply_reduce_fusion
  598.8 7.9 convert_reduce_fusion.5
  608.9 6.5 convolution_convert_fusion.1.output
  616.2 108.8 %scatter_sums.1 = (f32[4,40,1152]{2,1,0:T(8,128)}, bf16[128,9216]{1,0:T(8,128)(2,1)}, bf16[128,1152]{1,0:T(8,128)(2,1)}, f32[5,64,1152]{2,1,0:T(8,128)}) custom-call(bf16[1152,1152]{1,0:T(8,128)(2,1)} %convolution_convert_fusion.4.query, bf16[1152,1152]{1,0:T(8,128)(2,1)} %convolution_convert_fusion.3.key, ...), custom_call_target="tpu_custom_call" | custom-call | tf_op jit(solution)/shard_map/scatter_sums/pallas_call | solution.py:1011
  746.1 11.7 %all-to-all-start.1 = ((f32[32,1,128]{2,1,0:T(1,128)}), f32[32,1,128]{2,1,0:T(1,128)S(1)}, u32[]{:S(2)}, u32[]{:S(2)}) async-start(f32[32,1,128]{2,1,0:T(1,128)} %broadcast_in_dim.201), calls=%async_computation.1 | async-start | bytes 32768 | tf_op jit(solution)/shard_map/all_to_all | solution.py:1795
  776.6 6.3 fusion.77
  (342 shorter events, 114.3 us)
Async XLA Ops:
  11.3 16.0 %all-to-all-start = ((bf16[36,4,2304]{2,0,1:T(8,128)(2,1)}), bf16[36,4,2304]{2,0,1:T(8,128)(2,1)}, u32[]{:S(2)}, u32[]{:S(2)}) async-start(bf16[36,4,2304]{2,0,1:T(8,128)(2,1)} %pad_maximum_fusion.2), calls=%async_computation | async-start | bytes 1474560 | tf_op jit(solution)/shard_map/all_to_all | solution.py:1510
  15.6 257.9 %all-gather.2.cloned.1.call-start = ((), (), s32[]{:S(2)}) async-start(), calls=%async_computation.2 | async-start | bytes 10948608 | tf_op jit(solution)/shard_map/all_gather | solution.py:1542
  16.2 121.2 %copy-start.27 = (f32[1153,32]{0,1:T(8,128)S(1)}, f32[1153,32]{0,1:T(8,128)}, u32[]{:S(2)}) copy-start(f32[1153,32]{0,1:T(8,128)} %param.33) | copy-start | bytes 442756
  16.3 123.3 %copy-start = (bf16[48,9216]{1,0:T(8,128)(2,1)}, bf16[48,9216]{1,0:T(8,128)(2,1)S(1)}, u32[]{:S(2)}) copy-start(bf16[48,9216]{1,0:T(8,128)(2,1)S(1)} %pad.53.mods_own.mods_weights) | copy-start | bytes 2654212
  137.1 12.8 %copy-start.38 = (f32[4,4]{1,0:T(4,128)}, f32[4,4]{1,0:T(4,128)S(1)}, u32[]{:S(2)}) copy-start(f32[4,4]{1,0:T(4,128)S(1)} %fusion.58) | copy-start | bytes 196
  154.1 105.6 %copy-start.2 = (f32[4,256,1152]{2,1,0:T(8,128)}, f32[4,256,1152]{2,1,0:T(8,128)S(1)}, u32[]{:S(2)}) copy-start(f32[4,256,1152]{2,1,0:T(8,128)S(1)} %get-tuple-element.174) | copy-start | bytes 14155780
  156.8 10.4 %copy-start.16 = (bf16[4,256,1152]{2,1,0:T(8,128)(2,1)}, bf16[4,256,1152]{2,1,0:T(8,128)(2,1)S(1)}, u32[]{:S(2)}) copy-start(bf16[4,256,1152]{2,1,0:T(8,128)(2,1)S(1)} %add_convert_fusion.5) | copy-start | bytes 7077892
  273.5 39.1 %copy-start.4 = (f32[4,256,1152]{2,1,0:T(8,128)S(1)}, f32[4,256,1152]{2,1,0:T(8,128)}, u32[]{:S(2)}) copy-start(f32[4,256,1152]{2,1,0:T(8,128)} %copy-done.3) | copy-start | bytes 14155780
  325.4 19.1 %copy-start.9 = (bf16[4,256,1152]{2,1,0:T(8,128)(2,1)}, bf16[4,256,1152]{2,1,0:T(8,128)(2,1)S(1)}, u32[]{:S(2)}) copy-start(bf16[4,256,1152]{2,1,0:T(8,128)(2,1)S(1)} %get-tuple-element.137) | copy-start | bytes 7077892
  428.4 9.4 %slice-start.8 = ((s8[4718592]{0:T(1024)(128)(4,1)}), s8[524288]{0:T(1024)(128)(4,1)S(1)}, s32[]{:S(2)}) async-start(s8[4718592]{0:T(1024)(128)(4,1)} %bitcast.232), calls=%async_computation.11 | async-start | bytes 1048576
  428.4 9.4 %slice-start.10 = ((s8[4718592]{0:T(1024)(128)(4,1)}), s8[4194304]{0:T(1024)(128)(4,1)S(1)}, s32[]{:S(2)}) async-start(s8[4718592]{0:T(1024)(128)(4,1)} %bitcast.236), calls=%async_computation.13 | async-start | bytes 8388608
  549.9 14.7 %slice-start.3 = ((s8[10616832]{0:T(1024)(128)(4,1)}), s8[4194304]{0:T(1024)(128)(4,1)S(1)}, s32[]{:S(2)}) async-start(s8[10616832]{0:T(1024)(128)(4,1)} %bitcast.227), calls=%async_computation.6 | async-start | bytes 8388608
  549.9 14.7 %slice-start.4 = ((s8[10616832]{0:T(1024)(128)(4,1)}), s8[4194304]{0:T(1024)(128)(4,1)S(1)}, s32[]{:S(2)}) async-start(s8[10616832]{0:T(1024)(128)(4,1)} %bitcast.227), calls=%async_computation.7 | async-start | bytes 8388608
  574.7 13.8 %slice-start.6 = ((s8[4718592]{0:T(1024)(128)(4,1)}), s8[4194304]{0:T(1024)(128)(4,1)S(1)}, s32[]{:S(2)}) async-start(s8[4718592]{0:T(1024)(128)(4,1)} %bitcast.230), calls=%async_computation.9 | async-start | bytes 8388608
  598.8 8.5 %copy-start.40 = (f32[1152]{0:T(1024)S(1)}, f32[1152]{0:T(1024)}, u32[]{:S(2)}) copy-start(f32[1152]{0:T(1024)} %get-tuple-element.136) | copy-start | bytes 13828
  598.8 9.7 %copy-start.39 = (f32[4,4]{1,0:T(4,128)S(1)}, f32[4,4]{1,0:T(4,128)}, u32[]{:S(2)}) copy-start(f32[4,4]{1,0:T(4,128)} %copy-done.38) | copy-start | bytes 196
  725.1 8.5 %copy-start.12 = (f32[4,40,1152]{2,1,0:T(8,128)S(1)}, f32[4,40,1152]{2,1,0:T(8,128)}, u32[]{:S(2)}) copy-start(f32[4,40,1152]{2,1,0:T(8,128)} %get-tuple-element.77) | copy-start | bytes 2211844
  746.1 18.9 %all-to-all-start.1 = ((f32[32,1,128]{2,1,0:T(1,128)}), f32[32,1,128]{2,1,0:T(1,128)S(1)}, u32[]{:S(2)}, u32[]{:S(2)}) async-start(f32[32,1,128]{2,1,0:T(1,128)} %broadcast_in_dim.201), calls=%async_computation.1 | async-start | bytes 32768 | tf_op jit(solution)/shard_map/all_to_all | solution.py:1795
  760.1 8.9 %copy-start.35 = (f32[19,36]{1,0:T(8,128)S(1)}, f32[19,36]{1,0:T(8,128)}, u32[]{:S(2)}) copy-start(f32[19,36]{1,0:T(8,128)} %param.32) | copy-start | bytes 8212
  760.1 8.9 %copy-start.44 = (f32[19,36]{1,0:T(8,128)S(1)}, f32[19,36]{1,0:T(8,128)}, u32[]{:S(2)}) copy-start(f32[19,36]{1,0:T(8,128)} %param.38) | copy-start | bytes 8212
  760.1 8.9 %copy-start.45 = (f32[19,36]{1,0:T(8,128)S(1)}, f32[19,36]{1,0:T(8,128)}, u32[]{:S(2)}) copy-start(f32[19,36]{1,0:T(8,128)} %param.44) | copy-start | bytes 8212
  764.2 11.2 %copy-start.20 = (f32[36,2304]{1,0:T(8,128)S(1)}, f32[36,2304]{1,0:T(8,128)}, u32[]{:S(2)}) copy-start(f32[36,2304]{1,0:T(8,128)} %param.29) | copy-start | bytes 995332
  764.2 11.2 %copy-start.24 = (f32[36,1152]{1,0:T(8,128)S(1)}, f32[36,1152]{1,0:T(8,128)}, u32[]{:S(2)}) copy-start(f32[36,1152]{1,0:T(8,128)} %slice.267) | copy-start | bytes 497668
  764.2 11.2 %copy-start.25 = (f32[36,1152]{1,0:T(8,128)S(1)}, f32[36,1152]{1,0:T(8,128)}, u32[]{:S(2)}) copy-start(f32[36,1152]{1,0:T(8,128)} %get-tuple-element.182) | copy-start | bytes 497668
  (46 other events, 257.8 us)
Sparse Core Ops, SparseCore 0:
  135.0 107.8 all-gather.1

commit v3 on v2

--- a/solution.py
+++ b/solution.py
@@ -830,9 +830,7 @@
 
 
 def scatter_kernel(
-    query,
-    key,
-    value,
+    triple,
     output,
     slots_own,
     mods_weights,
@@ -866,7 +864,7 @@
         at,
         lambda b, z: [
             (
-                (query, key, value, output)[b].at[pl.ds(2 * z * BLOCK, 2 * BLOCK)],
+                (output if b == 3 else triple.at[b]).at[pl.ds(2 * z * BLOCK, 2 * BLOCK)],
                 2 * z * BLOCK,
                 2 * BLOCK,
             )
@@ -1010,7 +1008,7 @@
     steps = 5
     return pl.pallas_call(
         scatter_kernel,
-        in_specs=[anywhere] * 4 + [inside] * 4,
+        in_specs=[anywhere] * 2 + [inside] * 4,
         out_specs=[inside] * 4,
         out_shape=[
             jax.ShapeDtypeStruct((4, ROUNDED, D), F32),
@@ -1082,7 +1080,8 @@
 def attend_back_kernel(apart, q_ref, k_ref, v_ref, grad_ref, log_ref, *rest, travels):
     head = pl.program_id(0)
     if travels:
-        up_grad, dq_ref, dk_ref, dv_ref, shares, sums, *rest = rest
+        up_grad, grads, shares, sums, *rest = rest
+        dq_ref, dk_ref, dv_ref = (grads.at[which] for which in range(3))
         at = Place()
         share = Share(at, sums, rest[3], rest[:3])
 
@@ -1121,8 +1120,14 @@
         at_step(head, HEADS - 1, end)
 
 
+def one_of(array, which):
+    if array.ndim == 2:
+        return whole_block(array.shape)
+    return pl.BlockSpec((None, *array.shape[1:]), lambda step: (which, 0, 0))
+
+
 def attend(apart, queries, keys, values, up_own):
-    q_len, k_len = queries.shape[0], keys.shape[0]
+    q_len, k_len = queries.shape[-2], keys.shape[-2]
     travels = up_own is not None
     anywhere = pl.BlockSpec(memory_space=pl.ANY)
     return pl.pallas_call(
@@ -1130,9 +1135,9 @@
         grid=(HEADS,),
         in_specs=[
             whole_block(apart.shape),
-            whole_block((q_len, D)),
-            whole_block((k_len, D)),
-            whole_block((k_len, D)),
+            one_of(queries, 0),
+            one_of(keys, 1),
+            one_of(values, 2),
         ]
         + [anywhere] * travels,
         out_specs=[whole_block((q_len, D)), whole_block((HEADS, q_len))] + [anywhere] * travels,
@@ -1151,7 +1156,7 @@
 
 
 def attend_back(apart, queries, keys, values, grads, log_total, up_grad):
-    q_len, k_len = queries.shape[0], keys.shape[0]
+    q_len, k_len = queries.shape[-2], keys.shape[-2]
     travels = up_grad is not None
     anywhere = pl.BlockSpec(memory_space=pl.ANY)
     return pl.pallas_call(
@@ -1159,21 +1164,26 @@
         grid=(HEADS,),
         in_specs=[
             whole_block(apart.shape),
-            whole_block((q_len, D)),
-            whole_block((k_len, D)),
-            whole_block((k_len, D)),
+            one_of(queries, 0),
+            one_of(keys, 1),
+            one_of(values, 2),
             whole_block((q_len, D)),
             whole_block((HEADS, q_len)),
         ]
         + [anywhere] * travels,
-        out_specs=[whole_block((q_len, D)), whole_block((k_len, D)), whole_block((k_len, D))]
-        + [whole_block((4, ROUNDED, D))] * travels,
+        out_specs=[whole_block((3, q_len, D)), whole_block((4, ROUNDED, D))]
+        if travels
+        else [whole_block((q_len, D)), whole_block((k_len, D)), whole_block((k_len, D))],
         out_shape=[
+            jax.ShapeDtypeStruct((3, q_len, D), BF16),
+            jax.ShapeDtypeStruct((4, ROUNDED, D), F32),
+        ]
+        if travels
+        else [
             jax.ShapeDtypeStruct((q_len, D), BF16),
             jax.ShapeDtypeStruct((k_len, D), BF16),
             jax.ShapeDtypeStruct((k_len, D), BF16),
-        ]
-        + [jax.ShapeDtypeStruct((4, ROUNDED, D), F32)] * travels,
+        ],
         scratch_shapes=[
             pltpu.VMEM((BLOCK, D), F32),
             *share_scratch(),
@@ -1188,6 +1198,80 @@
         ),
         name="attend_rows_back",
     )(apart, queries, keys, values, grads, log_total, *((up_grad,) if travels else ()))
+
+
+def project_kernel(normed, weights, bias, out):
+    out[...] = (dot(normed[...], weights[...], NN) + bias[...]).astype(BF16)
+
+
+def project(normed, weights, bias):
+    rows, count = normed.shape[0], bias.shape[0]
+    return pl.pallas_call(
+        project_kernel,
+        grid=(count,),
+        in_specs=[
+            whole_block((rows, D)),
+            pl.BlockSpec((None, D, D), lambda i: (i, 0, 0)),
+            pl.BlockSpec((None, 1, D), lambda i: (i, 0, 0)),
+        ],
+        out_specs=pl.BlockSpec((None, rows, D), lambda i: (i, 0, 0)),
+        out_shape=jax.ShapeDtypeStruct((count, rows, D), BF16),
+        compiler_params=pltpu.CompilerParams(vmem_limit_bytes=40 << 20),
+        name="project",
+    )(normed, weights, bias[:, None])
+
+
+def project_back_kernel(normed, weights, grad, grad_normed, weight_grad, turned):
+    part = dot(grad[...], weights[...], NT)
+
+    @pl.when(pl.program_id(0) == 0)
+    def _():
+        turned[...] = jnp.transpose(normed[...])
+        grad_normed[...] = part
+
+    @pl.when(pl.program_id(0) > 0)
+    def _():
+        grad_normed[...] += part
+
+    weight_grad[...] = dot(turned[...], grad[...], NN).astype(BF16)
+
+
+def project_back(normed, weights, grads):
+    count, rows = grads.shape[:2]
+    return pl.pallas_call(
+        project_back_kernel,
+        grid=(count,),
+        in_specs=[
+            whole_block((rows, D)),
+            pl.BlockSpec((None, D, D), lambda i: (i, 0, 0)),
+            pl.BlockSpec((None, rows, D), lambda i: (i, 0, 0)),
+        ],
+        out_specs=[whole_block((rows, D)), pl.BlockSpec((None, D, D), lambda i: (i, 0, 0))],
+        out_shape=[
+            jax.ShapeDtypeStruct((rows, D), F32),
+            jax.ShapeDtypeStruct((count, D, D), BF16),
+        ],
+        scratch_shapes=[pltpu.VMEM((D, rows), BF16)],
+        compiler_params=pltpu.CompilerParams(vmem_limit_bytes=56 << 20),
+        name="project_back",
+    )(normed, weights, grads)
+
+
+def outer_kernel(left, right, out):
+    out[...] = dot(left[...], right[...], TN).astype(BF16)
+
+
+def outer(left, right):
+    rows, tile = left.shape[0], 768
+    return pl.pallas_call(
+        outer_kernel,
+        grid=(left.shape[1] // tile,),
+        in_specs=[pl.BlockSpec((rows, tile), lambda i: (0, i)), whole_block((rows, D))],
+        out_specs=pl.BlockSpec((tile, D), lambda i: (i, 0)),
+        out_shape=jax.ShapeDtypeStruct((left.shape[1], D), BF16),
+        compiler_params=pltpu.CompilerParams(vmem_limit_bytes=40 << 20),
+        name="outer",
+    )(left, right)
 
 
 def mlp_kernel(normed, up, bias, down, active, slope, branch):
@@ -1538,9 +1622,9 @@
         )
         given = given.T
         up_own = quarters[:, D:]
-        down_own, first_all = lax.optimization_barrier((down_low, first_all))
+        down_own, codes = lax.optimization_barrier((down_low, codes))
         down_all = lax.all_gather(down_own, AXES, axis=0, tiled=True)
-        weight_q, weight_k, weight_v, weight_o = first_all
+        weight_o = first_all[3]
         biases = small_all[: all_biases.shape[0]]
         patch_in = small_all[all_biases.shape[0] :][:PATCH_IN].astype(BF16)
         mods = lax.dynamic_slice_in_dim(mods, (at_band % 2) * SLOTS, SLOTS, 0)
@@ -1612,10 +1696,14 @@
     normed_one = modulate(hidden_zero, shift_one, scale_one).astype(BF16)
     flat = lambda array: array.reshape(part_len, array.shape[-1])
     deep = lambda array: array.reshape(n_seg, SEGMENT, array.shape[-1])
-    queries = flat(matmul(normed_one, weight_q) + biases[9]).astype(BF16)
-    keys = flat(matmul(normed_one, weight_k)).astype(BF16)
-    values = flat(matmul(normed_one, weight_v) + biases[10]).astype(BF16)
-    keys, values = in_row_gather(keys), in_row_gather(values)
+    if tuned:
+        query_bias = jnp.stack([biases[9], jnp.zeros_like(biases[9]), biases[10]])
+        queries = keys = values = project(flat(normed_one), first_all, query_bias)
+    else:
+        queries = flat(matmul(normed_one, weight_q) + biases[9]).astype(BF16)
+        keys = flat(matmul(normed_one, weight_k)).astype(BF16)
+        values = flat(matmul(normed_one, weight_v) + biases[10]).astype(BF16)
+        keys, values = in_row_gather(keys), in_row_gather(values)
     key_seg = jnp.where(four_way, jnp.arange(SLOTS), 0)
     apart = jnp.where(key_seg[:, None] == jnp.repeat(seg_slot, SEGMENT), 0.0, -1e30).astype(F32)
     if tuned:
@@ -1648,7 +1736,10 @@
     seg_sum = lambda array: jnp.sum(array, axis=1, keepdims=True)
     grad_gate_two = seg_sum(grad_two * branch_two)
     grad_branch_two = (gate_two * grad_two).astype(BF16)
-    down_grad = outer_sum(active, grad_branch_two)
+    if tuned:
+        down_grad = outer(flat(active), flat(grad_branch_two))
+    else:
+        down_grad = outer_sum(active, grad_branch_two)
     if tuned:
         grad_normed_two, up_grad, up_bias_grad, down_sum = mlp_back(
             flat(grad_branch_two),
@@ -1656,7 +1747,7 @@
             slope,
             down_all,
             up_all,
-            down_grad.astype(BF16),
+            down_grad,
         )
         grad_normed_two, up_bias_grad = deep(grad_normed_two), up_bias_grad[0]
     else:
@@ -1676,22 +1767,25 @@
     output_grad = outer_sum(attended, grad_branch_one)
     grad_attended = flat(matmul_back(grad_branch_one, weight_o).astype(BF16))
     if tuned:
-        grad_query, grad_key, grad_value, up_sum = attend_back(
+        triple, up_sum = attend_back(
             apart, queries, keys, values, grad_attended, log_total, up_grad
         )
+        grad_normed, triple_grad = project_back(flat(normed_one), first_all, triple)
+        grad_query, _, grad_value = triple
+        grad_normed = deep(grad_normed)
     else:
         grad_query, grad_key, grad_value = attend_back(
             apart, queries, keys, values, grad_attended, log_total, None
         )
-    grad_key, grad_value = in_row_scatter(grad_key), in_row_scatter(grad_value)
-    q_grad = outer_sum(normed_one, grad_query)
-    k_grad = outer_sum(normed_one, grad_key)
-    v_grad = outer_sum(normed_one, grad_value)
-    grad_normed = deep(
-        matmul_back(grad_query, weight_q)
-        + matmul_back(grad_key, weight_k)
-        + matmul_back(grad_value, weight_v)
-    )
+        grad_key, grad_value = in_row_scatter(grad_key), in_row_scatter(grad_value)
+        q_grad = outer_sum(normed_one, grad_query)
+        k_grad = outer_sum(normed_one, grad_key)
+        v_grad = outer_sum(normed_one, grad_value)
+        grad_normed = deep(
+            matmul_back(grad_query, weight_q)
+            + matmul_back(grad_key, weight_k)
+            + matmul_back(grad_value, weight_v)
+        )
     grad_zero_part, grad_shift_one, grad_scale_one = jax.vjp(
         modulate, hidden_zero, shift_one, scale_one
     )[1](grad_normed)
@@ -1731,10 +1825,9 @@
         slots_own = jnp.where(
             (jnp.arange(4 * SLOTS) // SLOTS == at_band)[:, None], jnp.tile(slot_grads, (4, 1)), 0
         ).astype(BF16)
-        matrices = (q_grad, k_grad, v_grad, output_grad)
         down_grad = down_sum
         sums, slot_grads, grad_condition_all, totals = scatter_sums(
-            [array.astype(BF16) for array in matrices],
+            (triple_grad, output_grad.astype(BF16)),
             slots_own,
             padded(mods_low),
             padded(condition.T),

time: 797 us -> 793 us (level)
  matrix products: 102 us -> 34.1 us
  Pallas kernels: 522 us -> 580 us
    pallas_call x1 -> x4, Pallas kernels: 109 us -> 168 us  [the longest x1 109 us: scatter_sums(): pl.pallas_call(scatter_kernel, in_specs=[anywhere] * 2 + [inside] * 4, ou...]
    dot_general x11 -> x7, matrix products: 45.2 us -> 12.8 us  [outer_sum(): jnp.einsum('ni,nj->ij', operand.reshape(-1, operand.shape[-1]), gradient....]
    dot_general x6 -> x3, matrix products: 29.9 us -> 8.8 us  [matmul_back(): jnp.einsum('...j,ij->...i', gradient, weights, preferred_element_type=F32)]
    dot_general x6 -> x3, matrix products: 27.2 us -> 12.5 us  [matmul(): jnp.einsum('...i,ij->...j', operand, weights, preferred_element_type=F32)]
  transfers between devices with their start and end apart: 3 -> 3, of which waited for: 1 -> 2; matrix products, arithmetic and copies ran while one was open for 7% -> 5% of each run, Pallas kernels for 11% -> 13%
where the time goes in v3:
time: 793 us; the launch traced here: 788 us
  Pallas kernels  580 us (73%)
  other arithmetic  86.8 us (11%)
  matrix products  34.1 us (4%)
  local copies, waits for them, and re-layouts  33.8 us (4%)
  between operations  27.3 us (3%)
  starting transfers between devices  16 us (2%)
  waiting for transfers between devices  9.88 us (1%)
    pallas_call x1, Pallas kernels, scatter_sums(): pl.pallas_call(scatter_kernel, in_specs=[anywhere] * 2 + [inside] * 4, ou...  109 us
    pallas_call x1, Pallas kernels, gather_weights(): pl.pallas_call(gather_kernel, in_specs=[anywhere] * 3 + [inside] * 7, out...  101 us
    pallas_call x1, Pallas kernels, attend_back(): pl.pallas_call(functools.partial(attend_back_kernel, travels=travels), gr...  101 us
    pallas_call x1, Pallas kernels, attend(): pl.pallas_call(functools.partial(attend_kernel, travels=travels), grid=(H...  86.8 us
    pallas_call x1, Pallas kernels, mlp_back(): pl.pallas_call(mlp_back_kernel, grid=(FF // tile,), in_specs=[whole_block...  83.9 us
    pallas_call x1, Pallas kernels, mlp(): pl.pallas_call(mlp_kernel, grid=(FF // tile,), in_specs=[whole_block((row...  39.2 us
    pallas_call x1, Pallas kernels, project_back(): pl.pallas_call(project_back_kernel, grid=(count,), in_specs=[whole_block(...  30.5 us
    reduce_sum x7, other arithmetic, column_sum(): return jnp.sum(gradient.reshape(-1, gradient.shape[-1]), axis=0, dtype=F32)  18.4 us
  transfers between devices with their start and end apart: 3, of which 2 were waited for; matrix products, arithmetic and copies ran while one was open for 5% of the time, Pallas kernels for 13%

profile of v3, /device:TPU:0, one launch (start us, length us, event | category | flops | bytes accessed | tf_op | source)
XLA Modules:
  0.0 788.1 jit_solution(15749033231174027861)
XLA Ops:
  11.3 4.2 all-to-all-start
  18.7 8.7 %all-to-all-done = bf16[36,4,2304]{2,0,1:T(8,128)(2,1)} async-done(((bf16[36,4,2304]{2,0,1:T(8,128)(2,1)}), bf16[36,4,2304]{2,0,1:T(8,128)(2,1)}, u32[]{:S(2)}, u32[]{:S(2)}) %all-to-all-start) | async-done | bytes 663584 | tf_op jit(solution)/shard_map/all_to_all | solution.py:1594
  29.5 101.4 %gather_weights.1 = (bf16[4,1152,1152]{2,1,0:T(8,128)(2,1)S(1)}, f32[8,9216]{1,0:T(8,128)S(1)}, f32[128,1152]{1,0:T(8,128)S(1)}, f32[128,1152]{1,0:T(8,128)S(1)}...) custom-call(bf16[144,1152]{1,0:T(8,128)(2,1)S(1)} %get-tuple-element, ...), custom_call_target="tpu_custom_call" | custom-call | tf_op jit(solution)/shard_map/gather_weights/pallas_call | solution.py:541
  130.9 4.0 copy-done.1
  150.1 3.3 fusion.72
  156.0 13.1 %project.1.q_ref.k_ref.v_ref = bf16[3,1024,1152]{2,1,0:T(8,128)(2,1)S(1)} custom-call(bf16[1024,1152]{1,0:T(8,128)(2,1)S(1)} %bitcast.191, bf16[4,1152,1152]{2,1,0:T(8,128)(2,1)} %copy-done.1, f32[3,1,1152]{2,1,0:T(1,128)S(1)} %broadcast_in_dim.184.bias), custom_call_target="tpu_custom_call" | custom-call | tf_op jit(solution)/shard_map/project/pallas_call | solution.py:1209
  172.0 86.8 %attend_rows.1 = (bf16[1024,1152]{1,0:T(8,128)(2,1)}, f32[16,1024]{1,0:T(8,128)}, bf16[1152,4608]{1,0:T(8,128)(2,1)}) custom-call(f32[4,1024]{1,0:T(4,128)} %compare_select_fusion.apart, bf16[3,1024,1152]{2,1,0:T(8,128)(2,1)} %copy-done, bf16[3,1024,1152]{2,1,0:T(8,128)(2,1)} %copy-done, bf16[3,1024,1152]{2,1,0:T(8,128)(2,1)} %copy-done, ...), custom_call_target="tpu_custom_call" | custom-call | tf_op jit(solution)/shard_map/attend_rows/pallas_call | solution.py:1133
  258.8 8.2 %fusion.67 = (f32[4,256]{1,0:T(4,128)S(1)}, f32[4,256,1152]{2,1,0:T(8,128)S(1)}, f32[4,256,1152]{2,1,0:T(8,128)}) fusion(f32[4,256,1152]{2,1,0:T(8,128)S(1)} %get-tuple-element.176, f32[4,1152]{1,0:T(4,128)S(1)} %get-tuple-element.166, f32[1152]{0:T(1024)S(1)} %get-tuple-element.97, bf16[4,256,1152]{2,1,0:T(8,128)(2,1)} %bitcast.236, ...), kind=kOutput, calls=%fused_computation.256 | convolution fusion | flops 2722626560 | bytes 19196416 | tf_op jit(solution)/shard_map/...i,ij->...j/dot_general | solution.py:1408
  269.2 3.4 add_convert_fusion.2
  272.6 39.2 %mlp.1 = (bf16[1024,4608]{1,0:T(8,128)(2,1)}, bf16[1024,4608]{1,0:T(8,128)(2,1)}, f32[1024,1152]{1,0:T(8,128)}) custom-call(bf16[1024,1152]{1,0:T(8,128)(2,1)} %bitcast.208, bf16[1152,4608]{1,0:T(8,128)(2,1)} %get-tuple-element.61.up, f32[1,4608]{1,0:T(1,128)} %bitcast.223, bf16[4608,1152]{1,0:T(8,128)(2,1)} %all-gather.2.cloned.1.call-done.down), custom_call_target="tpu_custom_call" | custom-call | tf_op jit(solution)/shard_map/mlp/pallas_call | solution.py:1301
  326.3 15.7 %outer.1.down_grad = bf16[4608,1152]{1,0:T(8,128)(2,1)} custom-call(bf16[1024,4608]{1,0:T(8,128)(2,1)S(1)} %bitcast.196, bf16[1024,1152]{1,0:T(8,128)(2,1)S(1)} %bitcast.193), custom_call_target="tpu_custom_call" | custom-call | tf_op jit(solution)/shard_map/outer/pallas_call | solution.py:1266
  342.0 83.9 %mlp_back.1 = (f32[1024,1152]{1,0:T(8,128)}, bf16[1152,4608]{1,0:T(8,128)(2,1)}, f32[1,4608]{1,0:T(1,128)}, f32[144,1152]{1,0:T(8,128)}) custom-call(bf16[1024,1152]{1,0:T(8,128)(2,1)} %bitcast.194, bf16[1024,1152]{1,0:T(8,128)(2,1)} %bitcast.209, bf16[1024,4608]{1,0:T(8,128)(2,1)} %get-tuple-element.66.slope, ...), custom_call_target="tpu_custom_call" | custom-call | tf_op jit(solution)/shard_map/mlp_back/pallas_call | solution.py:1376
  425.9 4.7 multiply_reduce_fusion.4
  431.0 4.4 fusion.2
  435.5 3.8 convert_reduce_fusion.2
  439.2 6.6 convolution_convert_fusion.1
  445.8 100.9 %attend_rows_back.1 = (bf16[3,1024,1152]{2,1,0:T(8,128)(2,1)}, f32[4,40,1152]{2,1,0:T(8,128)}) custom-call(f32[4,1024]{1,0:T(4,128)} %compare_select_fusion.apart, bf16[3,1024,1152]{2,1,0:T(8,128)(2,1)} %copy-done, bf16[3,1024,1152]{2,1,0:T(8,128)(2,1)} %copy-done, bf16[3,1024,1152]{2,1,0:T(8,128)(2,1)} %copy-done, bf16[1024,1152]{1,0:T(8,128)(2,1)} %bitcast.220, ...), custom_call_target="tpu_custom_call" | custom-call | tf_op jit(solution)/shard_map/attend_rows_back/pallas_call | solution.py:1162
  546.7 30.5 %project_back.1 = (f32[1024,1152]{1,0:T(8,128)}, bf16[3,1152,1152]{2,1,0:T(8,128)(2,1)}) custom-call(bf16[1024,1152]{1,0:T(8,128)(2,1)} %bitcast.192, bf16[4,1152,1152]{2,1,0:T(8,128)(2,1)} %copy-done.1, bf16[3,1024,1152]{2,1,0:T(8,128)(2,1)} %get-tuple-element.71.grad), custom_call_target="tpu_custom_call" | custom-call | tf_op jit(solution)/shard_map/project_back/pallas_call | solution.py:1241
  577.2 3.2 convert_reduce_fusion.3
  591.6 7.7 convert_reduce_fusion.5
  601.7 6.5 convolution_convert_fusion.output
  608.9 108.8 %scatter_sums.1 = (f32[4,40,1152]{2,1,0:T(8,128)}, bf16[128,9216]{1,0:T(8,128)(2,1)}, bf16[128,1152]{1,0:T(8,128)(2,1)}, f32[5,64,1152]{2,1,0:T(8,128)}) custom-call(bf16[3,1152,1152]{2,1,0:T(8,128)(2,1)} %get-tuple-element.72.triple, bf16[1152,1152]{1,0:T(8,128)(2,1)} %convolution_convert_fusion.output, bf16[16,9216]{1,0:T(8,128)(2,1)} %broadcast_select_fusion.slots_own, ...), custom_call_target="tpu_custom_call" | custom-call | tf_op jit(solution)/shard_map/scatter_sums/pallas_call | solution.py:1009
  741.0 11.7 %all-to-all-start.1 = ((f32[32,1,128]{2,1,0:T(1,128)}), f32[32,1,128]{2,1,0:T(1,128)S(1)}, u32[]{:S(2)}, u32[]{:S(2)}) async-start(f32[32,1,128]{2,1,0:T(1,128)} %broadcast_in_dim.205), calls=%async_computation.1 | async-start | bytes 32768 | tf_op jit(solution)/shard_map/all_to_all | solution.py:1888
  772.4 6.2 fusion.63
  (308 shorter events, 93.9 us)
Async XLA Ops:
  10.2 8.4 %copy-start.29 = (f32[4,256,16]{1,2,0:T(8,128)S(1)}, f32[4,256,16]{1,2,0:T(8,128)}, u32[]{:S(2)}) copy-start(f32[4,256,16]{1,2,0:T(8,128)} %param.24) | copy-start | bytes 196612
  10.2 8.4 %copy-start.30 = (f32[4,256,16]{1,2,0:T(8,128)S(1)}, f32[4,256,16]{1,2,0:T(8,128)}, u32[]{:S(2)}) copy-start(f32[4,256,16]{1,2,0:T(8,128)} %param.23) | copy-start | bytes 196612
  11.3 16.0 %all-to-all-start = ((bf16[36,4,2304]{2,0,1:T(8,128)(2,1)}), bf16[36,4,2304]{2,0,1:T(8,128)(2,1)}, u32[]{:S(2)}, u32[]{:S(2)}) async-start(bf16[36,4,2304]{2,0,1:T(8,128)(2,1)} %pad_maximum_fusion.2), calls=%async_computation | async-start | bytes 1474560 | tf_op jit(solution)/shard_map/all_to_all | solution.py:1594
  15.6 257.0 %all-gather.2.cloned.1.call-start = ((), (), s32[]{:S(2)}) async-start(), calls=%async_computation.2 | async-start | bytes 10948608 | tf_op jit(solution)/shard_map/all_gather | solution.py:1626
  16.2 121.2 %copy-start.23 = (f32[1153,32]{0,1:T(8,128)S(1)}, f32[1153,32]{0,1:T(8,128)}, u32[]{:S(2)}) copy-start(f32[1153,32]{0,1:T(8,128)} %param.33) | copy-start | bytes 442756
  16.3 122.8 %copy-start.4 = (bf16[48,9216]{1,0:T(8,128)(2,1)}, bf16[48,9216]{1,0:T(8,128)(2,1)S(1)}, u32[]{:S(2)}) copy-start(bf16[48,9216]{1,0:T(8,128)(2,1)S(1)} %pad.53.mods_own.mods_weights) | copy-start | bytes 2654212
  153.4 105.5 %copy-start.6 = (f32[4,256,1152]{2,1,0:T(8,128)}, f32[4,256,1152]{2,1,0:T(8,128)S(1)}, u32[]{:S(2)}) copy-start(f32[4,256,1152]{2,1,0:T(8,128)S(1)} %get-tuple-element.176) | copy-start | bytes 14155780
  156.0 13.1 %copy-start.2 = (bf16[4,256,1152]{2,1,0:T(8,128)(2,1)}, bf16[4,256,1152]{2,1,0:T(8,128)(2,1)S(1)}, u32[]{:S(2)}) copy-start(bf16[4,256,1152]{2,1,0:T(8,128)(2,1)S(1)} %add_convert_fusion.3) | copy-start | bytes 7077892
  272.6 39.2 %copy-start.8 = (f32[4,256,1152]{2,1,0:T(8,128)S(1)}, f32[4,256,1152]{2,1,0:T(8,128)}, u32[]{:S(2)}) copy-start(f32[4,256,1152]{2,1,0:T(8,128)} %copy-done.7) | copy-start | bytes 14155780
  323.8 18.2 %copy-start.3 = (bf16[4,256,1152]{2,1,0:T(8,128)(2,1)}, bf16[4,256,1152]{2,1,0:T(8,128)(2,1)S(1)}, u32[]{:S(2)}) copy-start(bf16[4,256,1152]{2,1,0:T(8,128)(2,1)S(1)} %get-tuple-element.137) | copy-start | bytes 7077892
  425.9 9.5 %slice-start.5 = ((s8[4718592]{0:T(1024)(128)(4,1)}), s8[524288]{0:T(1024)(128)(4,1)S(1)}, s32[]{:S(2)}) async-start(s8[4718592]{0:T(1024)(128)(4,1)} %bitcast.200), calls=%async_computation.8 | async-start | bytes 1048576
  425.9 9.5 %slice-start.9 = ((s8[4718592]{0:T(1024)(128)(4,1)}), s8[4194304]{0:T(1024)(128)(4,1)S(1)}, s32[]{:S(2)}) async-start(s8[4718592]{0:T(1024)(128)(4,1)} %bitcast.206), calls=%async_computation.12 | async-start | bytes 8388608
  591.6 8.1 %copy-start.33 = (f32[1,4608]{1,0:T(1,128)S(1)}, f32[1,4608]{1,0:T(1,128)}, u32[]{:S(2)}) copy-start(f32[1,4608]{1,0:T(1,128)} %get-tuple-element.75) | copy-start | bytes 55300
  741.0 18.9 %all-to-all-start.1 = ((f32[32,1,128]{2,1,0:T(1,128)}), f32[32,1,128]{2,1,0:T(1,128)S(1)}, u32[]{:S(2)}, u32[]{:S(2)}) async-start(f32[32,1,128]{2,1,0:T(1,128)} %broadcast_in_dim.205), calls=%async_computation.1 | async-start | bytes 32768 | tf_op jit(solution)/shard_map/all_to_all | solution.py:1888
  753.9 8.0 %copy-start.24 = (f32[1153,32]{0,1:T(8,128)S(1)}, f32[1153,32]{0,1:T(8,128)}, u32[]{:S(2)}) copy-start(f32[1153,32]{0,1:T(8,128)} %param.33) | copy-start | bytes 442756
  753.9 9.9 %copy-start.32 = (f32[19,36]{1,0:T(8,128)S(1)}, f32[19,36]{1,0:T(8,128)}, u32[]{:S(2)}) copy-start(f32[19,36]{1,0:T(8,128)} %param.32) | copy-start | bytes 8212
  753.9 9.9 %copy-start.34 = (f32[19,36]{1,0:T(8,128)S(1)}, f32[19,36]{1,0:T(8,128)}, u32[]{:S(2)}) copy-start(f32[19,36]{1,0:T(8,128)} %param.38) | copy-start | bytes 8212
  753.9 9.9 %copy-start.35 = (f32[19,36]{1,0:T(8,128)S(1)}, f32[19,36]{1,0:T(8,128)}, u32[]{:S(2)}) copy-start(f32[19,36]{1,0:T(8,128)} %param.44) | copy-start | bytes 8212
  754.1 12.8 %copy-start.17 = (f32[144,1152]{1,0:T(8,128)S(1)}, f32[144,1152]{1,0:T(8,128)}, u32[]{:S(2)}) copy-start(f32[144,1152]{1,0:T(8,128)} %param.30) | copy-start | bytes 1990660
  761.9 8.2 %copy-start.26 = (f32[36,2304]{1,0:T(8,128)S(1)}, f32[36,2304]{1,0:T(8,128)}, u32[]{:S(2)}) copy-start(f32[36,2304]{1,0:T(8,128)} %param.35) | copy-start | bytes 995332
  761.9 8.2 %copy-start.27 = (f32[36,2304]{1,0:T(8,128)S(1)}, f32[36,2304]{1,0:T(8,128)}, u32[]{:S(2)}) copy-start(f32[36,2304]{1,0:T(8,128)} %param.41) | copy-start | bytes 995332
  763.8 8.5 %copy-start.11 = (f32[36,17280]{1,0:T(8,128)S(1)}, f32[36,17280]{1,0:T(8,128)}, u32[]{:S(2)}) copy-start(f32[36,17280]{1,0:T(8,128)} %param.28) | copy-start | bytes 7464964
  763.8 8.5 %copy-start.15 = (f32[36,17280]{1,0:T(8,128)S(1)}, f32[36,17280]{1,0:T(8,128)}, u32[]{:S(2)}) copy-start(f32[36,17280]{1,0:T(8,128)} %param.34) | copy-start | bytes 7464964
  763.8 8.5 %copy-start.16 = (f32[36,17280]{1,0:T(8,128)S(1)}, f32[36,17280]{1,0:T(8,128)}, u32[]{:S(2)}) copy-start(f32[36,17280]{1,0:T(8,128)} %param.40) | copy-start | bytes 7464964
  (31 other events, 146.4 us)
Sparse Core Ops, SparseCore 0:
  135.1 107.5 all-gather.1
